TPU v7x, 32 devices: a whole 2x2x4 slice. The times are simulated.
32 devices in a mesh: section: 2 (over core), dp: 4 (over z), tensor: 4 (over y, x).
Axes of the slice: x: 2, y: 2, z: 4, core: 2. Of those that a mesh axis runs over, the one named last changes fastest.
Arguments:
- tokens: bfloat16 [2, 1024, 2048], P(None, ('dp', 'tensor')), may hold values from -6 to 6
- lengths: int32 [2, 4], P(None, 'dp'), may hold values from 1 to 256, as said below
- cotangent: bfloat16 [2, 1024, 2048], P(None, ('dp', 'tensor')), may hold values from -6 to 6
- attn_gain: float32 [2, 2048], P('section'), may hold values from 0.5 to 1.5
- mlp_gain: float32 [2, 2048], P('section'), may hold values from 0.5 to 1.5
- w_query: bfloat16 [2, 2048, 2048], P('section', None, 'tensor'), may hold values from -0.125 to 0.125
- w_key: bfloat16 [2, 2048, 512], P('section', None, 'tensor'), may hold values from -0.125 to 0.125
- w_value: bfloat16 [2, 2048, 512], P('section', None, 'tensor'), may hold values from -0.125 to 0.125
- w_out: bfloat16 [2, 2048, 2048], P('section', 'tensor'), may hold values from -1 to 1
- w_gate: bfloat16 [2, 2048, 8192], P('section', None, 'tensor'), may hold values from -0.125 to 0.125
- w_up: bfloat16 [2, 2048, 8192], P('section', None, 'tensor'), may hold values from -0.125 to 0.125
- w_down: bfloat16 [2, 8192, 2048], P('section', 'tensor'), may hold values from -0.0625 to 0.0625
Outputs:
- activations: bfloat16 [2, 2, 1024, 2048], P('section', None, ('dp', 'tensor'))
- input_grads: float32 [2, 2, 1024, 2048], P('section', None, ('dp', 'tensor'))
- attn_gain_grad: float32 [2, 2048], P('section', ('dp', 'tensor'))
- mlp_gain_grad: float32 [2, 2048], P('section', ('dp', 'tensor'))
- w_query_grad: float32 [2, 2048, 2048], P('section', 'dp', 'tensor')
- w_key_grad: float32 [2, 2048, 512], P('section', 'dp', 'tensor')
- w_value_grad: float32 [2, 2048, 512], P('section', 'dp', 'tensor')
- w_out_grad: float32 [2, 2048, 2048], P('section', 'tensor', 'dp')
- w_gate_grad: float32 [2, 2048, 8192], P('section', 'dp', 'tensor')
- w_up_grad: float32 [2, 2048, 8192], P('section', 'dp', 'tensor')
- w_down_grad: float32 [2, 8192, 2048], P('section', 'tensor', 'dp')
Inputs may be any that keep to these rules, and one draw needn't show every extreme that they name: `lengths`: in every data group one of its 2 sequences, drawn from the seed, has all 256 positions valid.
All inputs are finite; a program needn't handle non-finite values.
Results may differ from a plain program's by a relative error of at most 0.025.
Values may be sent and summed in bfloat16 or wider, within the bound.
No kernel may reach another device: no remote copies, remote signals or barrier semaphores. Data moves between devices by JAX's collectives and lax.ppermute only.
A program may use at most 256 MiB of HBM per device.

v0:
```python
import jax
import jax.numpy as jnp
from jax import lax
from jax.sharding import PartitionSpec as P

HD = 64


EPSILON = 1e-05
NEGATIVE = -1e30


def passed_along(array, axis, by):
    size = lax.axis_size(axis)
    pairs = [(i, i + by) for i in range(size) if 0 <= i + by < size]
    return lax.ppermute(array, axis, pairs)


def rope_tables(span_rows, head_size):
    half_width = head_size // 2
    counter = jnp.arange(half_width, dtype=jnp.float32)
    base_freq = 1.0 / 500000.0 ** (2.0 * counter / head_size)
    wavelength = 2.0 * jnp.pi / base_freq
    blend_part = (8192.0 / wavelength - 1.0) / 3.0
    middle = (1.0 - blend_part) * base_freq / 32.0 + blend_part * base_freq
    frequency = jnp.where(
        wavelength < 2048.0, base_freq, jnp.where(wavelength > 8192.0, base_freq / 32.0, middle)
    )
    angles = jnp.arange(span_rows, dtype=jnp.float32)[:, None] * frequency[None, :]
    return (jnp.cos(angles), jnp.sin(angles))


def rotate(flat, cosine, sine_table):
    row_count = flat.shape[0]
    half_width = cosine.shape[1]
    shaped = flat.reshape(row_count, -1, 2 * half_width)
    front_half = shaped[..., :half_width]
    back_half = shaped[..., half_width:]
    cos_wide = cosine[:, None, :]
    sin_wide = sine_table[:, None, :]
    turned = jnp.concatenate(
        [
            front_half * cos_wide - back_half * sin_wide,
            back_half * cos_wide + front_half * sin_wide,
        ],
        axis=-1,
    )
    return turned.reshape(row_count, -1)


def unrotate(flat, cosine, sine_table):
    row_count = flat.shape[0]
    half_width = cosine.shape[1]
    shaped = flat.reshape(row_count, -1, 2 * half_width)
    front_half = shaped[..., :half_width]
    back_half = shaped[..., half_width:]
    cos_wide = cosine[:, None, :]
    sin_wide = sine_table[:, None, :]
    turned = jnp.concatenate(
        [
            front_half * cos_wide + back_half * sin_wide,
            back_half * cos_wide - front_half * sin_wide,
        ],
        axis=-1,
    )
    return turned.reshape(row_count, -1)


def rms_scale(stream):
    return lax.rsqrt(jnp.mean(stream * stream, axis=-1, keepdims=True) + EPSILON)


def norm_back(grad_rows, normed, scale_row, gain_row):
    weighted = grad_rows * gain_row
    return scale_row * (weighted - normed * jnp.mean(weighted * normed, axis=-1, keepdims=True))


def matmul(left_side, right_side):
    return jnp.dot(left_side, right_side, preferred_element_type=jnp.float32)


def times_transposed(left_side, right_side):
    return lax.dot_general(
        left_side, right_side, (((1,), (1,)), ((), ())), preferred_element_type=jnp.float32
    )


def transposed_times(left_side, right_side):
    return lax.dot_general(
        left_side, right_side, (((0,), (0,)), ((), ())), preferred_element_type=jnp.float32
    )


def allowed_mask(whole_rows, length):
    places = jnp.arange(whole_rows, dtype=jnp.int32)
    return (places[None, :] <= places[:, None]) & (places[None, :] < length)


def score_block(queries, keys_rot, length):
    whole_rows = queries.shape[0]
    kv_heads = keys_rot.shape[1] // HD
    query_four = queries.reshape(whole_rows, kv_heads, -1, HD)
    keys_three = keys_rot.reshape(whole_rows, kv_heads, HD)
    raw_scores = jnp.einsum(
        "qcgd,scd->cgqs", query_four, keys_three, preferred_element_type=jnp.float32
    )
    scores = jnp.where(allowed_mask(whole_rows, length), raw_scores * HD ** (-0.5), NEGATIVE)
    return (scores, query_four, keys_three)


def attend_forward(queries, keys_rot, values_in, length):
    whole_rows = queries.shape[0]
    scores, query_four, keys_three = score_block(queries, keys_rot, length)
    values_three = values_in.reshape(whole_rows, keys_three.shape[1], HD)
    row_max = jnp.max(scores, axis=-1, keepdims=True)
    lifted = jnp.exp(scores - row_max)
    row_total = jnp.sum(lifted, axis=-1, keepdims=True)
    softmax_w = (lifted / row_total).astype(jnp.bfloat16)
    attended = jnp.einsum(
        "cgqs,scd->qcgd", softmax_w, values_three, preferred_element_type=jnp.float32
    )
    return (attended.reshape(whole_rows, -1).astype(jnp.bfloat16), row_max, row_total)


def attend_backward(queries, keys_rot, values_in, length, row_max, row_total, d_attended):
    whole_rows = queries.shape[0]
    scores, query_four, keys_three = score_block(queries, keys_rot, length)
    values_three = values_in.reshape(whole_rows, keys_three.shape[1], HD)
    softmax_f = jnp.exp(scores - row_max) / row_total
    softmax_w = softmax_f.astype(jnp.bfloat16)
    d_att_four = d_attended.reshape(query_four.shape)
    d_soft = jnp.einsum(
        "qcgd,scd->cgqs", d_att_four, values_three, preferred_element_type=jnp.float32
    )
    d_value = jnp.einsum(
        "cgqs,qcgd->scd", softmax_w, d_att_four, preferred_element_type=jnp.float32
    )
    inner = jnp.sum(d_soft * softmax_f, axis=-1, keepdims=True)
    d_raw = (softmax_f * (d_soft - inner) * HD ** (-0.5)).astype(jnp.bfloat16)
    d_query = jnp.einsum("cgqs,scd->qcgd", d_raw, keys_three, preferred_element_type=jnp.float32)
    d_key = jnp.einsum("cgqs,qcgd->scd", d_raw, query_four, preferred_element_type=jnp.float32)
    return (
        d_query.reshape(whole_rows, -1),
        d_key.reshape(whole_rows, -1),
        d_value.reshape(whole_rows, -1),
    )


def forward_layer(layer_in, length, weights, cosine, sine_table):
    attn_gain_v, mlp_gain_v, w_query_v, w_key_v, w_value_v, w_out_v, w_gate_v, w_up_v, w_down_v = (
        weights
    )
    stream = layer_in.astype(jnp.float32)
    normed_local = (stream * rms_scale(stream) * attn_gain_v).astype(jnp.bfloat16)
    attn_rows = lax.all_gather(normed_local, "tensor", axis=0, tiled=True)
    queries = rotate(matmul(attn_rows, w_query_v), cosine, sine_table).astype(jnp.bfloat16)
    keys_rot = rotate(matmul(attn_rows, w_key_v), cosine, sine_table).astype(jnp.bfloat16)
    values_in = matmul(attn_rows, w_value_v).astype(jnp.bfloat16)
    attended, row_max, row_total = attend_forward(queries, keys_rot, values_in, length)
    mid_stream = stream + lax.psum_scatter(
        matmul(attended, w_out_v), "tensor", scatter_dimension=0, tiled=True
    )
    mlp_local = (mid_stream * rms_scale(mid_stream) * mlp_gain_v).astype(jnp.bfloat16)
    mlp_rows = lax.all_gather(mlp_local, "tensor", axis=0, tiled=True)
    gate_val = matmul(mlp_rows, w_gate_v)
    up_val = matmul(mlp_rows, w_up_v)
    hidden = (gate_val * jax.nn.sigmoid(gate_val) * up_val).astype(jnp.bfloat16)
    layer_out = mid_stream + lax.psum_scatter(
        matmul(hidden, w_down_v).astype(jnp.bfloat16), "tensor", scatter_dimension=0, tiled=True
    ).astype(jnp.float32)
    kept_fwd = (
        layer_in,
        attn_rows,
        queries,
        keys_rot,
        values_in,
        row_max,
        row_total,
        attended,
        mid_stream,
        mlp_rows,
        gate_val,
        up_val,
        hidden,
    )
    return (layer_out, kept_fwd)


def backward_layer(d_out, kept_fwd, length, weights, cosine, sine_table):
    attn_gain_v, mlp_gain_v, w_query_v, w_key_v, w_value_v, w_out_v, w_gate_v, w_up_v, w_down_v = (
        weights
    )
    (
        layer_in,
        attn_rows,
        queries,
        keys_rot,
        values_in,
        row_max,
        row_total,
        attended,
        mid_stream,
        mlp_rows,
        gate_val,
        up_val,
        hidden,
    ) = kept_fwd
    mlp_grad = lax.all_gather(d_out.astype(jnp.bfloat16), "tensor", axis=0, tiled=True)
    d_hidden = times_transposed(mlp_grad, w_down_v)
    sigma = jax.nn.sigmoid(gate_val)
    d_up = (d_hidden * gate_val * sigma).astype(jnp.bfloat16)
    d_gate = (d_hidden * up_val * sigma * (1.0 + gate_val * (1.0 - sigma))).astype(jnp.bfloat16)
    d_mlp_normed = lax.psum_scatter(
        (times_transposed(d_gate, w_gate_v) + times_transposed(d_up, w_up_v)).astype(jnp.bfloat16),
        "tensor",
        scatter_dimension=0,
        tiled=True,
    ).astype(jnp.float32)
    scale_mid = rms_scale(mid_stream)
    normed_mid = mid_stream * scale_mid
    mlp_gain_part = jnp.sum(d_mlp_normed * normed_mid, axis=0)
    d_mid = d_out + norm_back(d_mlp_normed, normed_mid, scale_mid, mlp_gain_v)
    attn_grad = lax.all_gather(d_mid.astype(jnp.bfloat16), "tensor", axis=0, tiled=True)
    d_attended = times_transposed(attn_grad, w_out_v).astype(jnp.bfloat16)
    d_query, d_key, d_value = attend_backward(
        queries, keys_rot, values_in, length, row_max, row_total, d_attended
    )
    d_query = unrotate(d_query, cosine, sine_table).astype(jnp.bfloat16)
    d_key = unrotate(d_key, cosine, sine_table).astype(jnp.bfloat16)
    d_value = d_value.astype(jnp.bfloat16)
    part_query = times_transposed(d_query, w_query_v)
    part_key = times_transposed(d_key, w_key_v)
    part_value = times_transposed(d_value, w_value_v)
    d_attn_normed = lax.psum_scatter(
        (part_query + part_key + part_value).astype(jnp.bfloat16),
        "tensor",
        scatter_dimension=0,
        tiled=True,
    ).astype(jnp.float32)
    stream = layer_in.astype(jnp.float32)
    scale_in = rms_scale(stream)
    normed_in = stream * scale_in
    attn_gain_part = jnp.sum(d_attn_normed * normed_in, axis=0)
    d_stream = d_mid + norm_back(d_attn_normed, normed_in, scale_in, attn_gain_v)
    saved_bwd = (mlp_grad, d_gate, d_up, attn_grad, d_query, d_key, d_value)
    return (d_stream, attn_gain_part, mlp_gain_part, saved_bwd)


def weight_terms(kept_fwd, saved_bwd):
    (
        layer_in,
        attn_rows,
        queries,
        keys_rot,
        values_in,
        row_max,
        row_total,
        attended,
        mid_stream,
        mlp_rows,
        gate_val,
        up_val,
        hidden,
    ) = kept_fwd
    mlp_grad, d_gate, d_up, attn_grad, d_query, d_key, d_value = saved_bwd
    return (
        transposed_times(attn_rows, d_query),
        transposed_times(attn_rows, d_key),
        transposed_times(attn_rows, d_value),
        transposed_times(attended, attn_grad),
        transposed_times(mlp_rows, d_gate),
        transposed_times(mlp_rows, d_up),
        transposed_times(hidden, mlp_grad),
    )


def store_at(buffers, entries, position, is_valid):

    def place_one(buffer, element):
        previous = lax.dynamic_index_in_dim(buffer, position, 0, keepdims=False)
        return lax.dynamic_update_index_in_dim(
            buffer, jnp.where(is_valid, element, previous), position, 0
        )

    return jax.tree.map(place_one, buffers, entries)


def fresh_store(entries, micro_count):
    return jax.tree.map(
        lambda element: jnp.zeros((micro_count,) + element.shape, element.dtype), entries
    )


def local(
    tokens,
    lengths,
    cotangent,
    attn_gain,
    mlp_gain,
    w_query,
    w_key,
    w_value,
    w_out,
    w_gate,
    w_up,
    w_down,
):
    section_index = lax.axis_index("section")
    section_count = lax.axis_size("section")
    tensor_index = lax.axis_index("tensor")
    micro_count = tokens.shape[0]
    local_rows = tokens.shape[1]
    whole_rows = local_rows * lax.axis_size("tensor")
    weights = (
        attn_gain[0],
        mlp_gain[0],
        w_query[0],
        w_key[0],
        w_value[0],
        w_out[0],
        w_gate[0],
        w_up[0],
        w_down[0],
    )
    cosine, sine_table = rope_tables(whole_rows, HD)
    seq_lengths = lengths[:, 0]
    places = tensor_index * local_rows + jnp.arange(local_rows, dtype=jnp.int32)
    last_section = section_count - 1
    step_total = micro_count + section_count - 1
    incoming = jnp.zeros_like(tokens[0])
    kept_store = None
    act_store = jnp.zeros_like(tokens)
    for moment in range(step_total):
        batch_index = moment - section_index
        is_valid = (batch_index >= 0) & (batch_index < micro_count)
        batch_index = jnp.clip(batch_index, 0, micro_count - 1)
        own_input = tokens[min(moment, micro_count - 1)]
        layer_in = jnp.where(section_index == 0, own_input, incoming)
        length = lax.dynamic_index_in_dim(seq_lengths, batch_index, 0, keepdims=False)
        layer_out, kept_fwd = forward_layer(layer_in, length, weights, cosine, sine_table)
        out_low = layer_out.astype(jnp.bfloat16)
        if kept_store is None:
            kept_store = fresh_store(kept_fwd, micro_count)
        kept_store = store_at(kept_store, kept_fwd, batch_index, is_valid)
        act_store = store_at(act_store, out_low, batch_index, is_valid)
        if moment + 1 < step_total:
            incoming = passed_along(out_low, "section", 1)
    returning = jnp.zeros_like(tokens[0])
    saved_store = None
    grad_in_store = jnp.zeros(tokens.shape, jnp.float32)
    attn_gain_sum = jnp.zeros((tokens.shape[2],), jnp.float32)
    mlp_gain_sum = jnp.zeros((tokens.shape[2],), jnp.float32)
    for moment in range(step_total):
        batch_index = moment - (last_section - section_index)
        is_valid = (batch_index >= 0) & (batch_index < micro_count)
        batch_index = jnp.clip(batch_index, 0, micro_count - 1)
        length = lax.dynamic_index_in_dim(seq_lengths, batch_index, 0, keepdims=False)
        row_mask = (places < length).astype(jnp.float32)[:, None]
        cot_now = cotangent[min(moment, micro_count - 1)].astype(jnp.float32) * row_mask
        d_out = jnp.where(section_index == last_section, cot_now, returning.astype(jnp.float32))
        kept_now = jax.tree.map(
            lambda buffer: lax.dynamic_index_in_dim(buffer, batch_index, 0, keepdims=False),
            kept_store,
        )
        d_stream, attn_part, mlp_part, saved_bwd = backward_layer(
            d_out, kept_now, length, weights, cosine, sine_table
        )
        attn_gain_sum = attn_gain_sum + jnp.where(is_valid, attn_part, 0.0)
        mlp_gain_sum = mlp_gain_sum + jnp.where(is_valid, mlp_part, 0.0)
        if saved_store is None:
            saved_store = fresh_store(saved_bwd, micro_count)
        saved_store = store_at(saved_store, saved_bwd, batch_index, is_valid)
        grad_in_store = store_at(grad_in_store, d_stream, batch_index, is_valid)
        if moment + 1 < step_total:
            returning = passed_along(d_stream.astype(jnp.bfloat16), "section", -1)
    grads_sum = None
    for batch_number in range(micro_count):
        kept_now = jax.tree.map(lambda buffer: buffer[batch_number], kept_store)
        saved_now = jax.tree.map(lambda buffer: buffer[batch_number], saved_store)
        terms = weight_terms(kept_now, saved_now)
        grads_sum = terms if grads_sum is None else jax.tree.map(jnp.add, grads_sum, terms)
    grads_sum = (
        lax.psum_scatter(
            grads_sum[0].astype(jnp.bfloat16), "dp", scatter_dimension=0, tiled=True
        ).astype(jnp.float32),
        lax.psum_scatter(
            grads_sum[1].astype(jnp.bfloat16), "dp", scatter_dimension=0, tiled=True
        ).astype(jnp.float32),
        lax.psum_scatter(
            grads_sum[2].astype(jnp.bfloat16), "dp", scatter_dimension=0, tiled=True
        ).astype(jnp.float32),
        lax.psum_scatter(
            grads_sum[3].astype(jnp.bfloat16), "dp", scatter_dimension=1, tiled=True
        ).astype(jnp.float32),
        lax.psum_scatter(
            grads_sum[4].astype(jnp.bfloat16), "dp", scatter_dimension=0, tiled=True
        ).astype(jnp.float32),
        lax.psum_scatter(
            grads_sum[5].astype(jnp.bfloat16), "dp", scatter_dimension=0, tiled=True
        ).astype(jnp.float32),
        lax.psum_scatter(
            grads_sum[6].astype(jnp.bfloat16), "dp", scatter_dimension=1, tiled=True
        ).astype(jnp.float32),
    )
    gain_shares = (
        lax.psum_scatter(attn_gain_sum, ("dp", "tensor"), scatter_dimension=0, tiled=True),
        lax.psum_scatter(mlp_gain_sum, ("dp", "tensor"), scatter_dimension=0, tiled=True),
    )
    return (
        act_store[None],
        grad_in_store[None],
        gain_shares[0][None],
        gain_shares[1][None],
        grads_sum[0][None],
        grads_sum[1][None],
        grads_sum[2][None],
        grads_sum[3][None],
        grads_sum[4][None],
        grads_sum[5][None],
        grads_sum[6][None],
    )


def solution(mesh):
    in_specs = (
        P(None, ("dp", "tensor"), None),
        P(None, "dp"),
        P(None, ("dp", "tensor"), None),
        P("section", None),
        P("section", None),
        P("section", None, "tensor"),
        P("section", None, "tensor"),
        P("section", None, "tensor"),
        P("section", "tensor", None),
        P("section", None, "tensor"),
        P("section", None, "tensor"),
        P("section", "tensor", None),
    )
    out_specs = (
        P("section", None, ("dp", "tensor"), None),
        P("section", None, ("dp", "tensor"), None),
        P("section", ("dp", "tensor")),
        P("section", ("dp", "tensor")),
        P("section", "dp", "tensor"),
        P("section", "dp", "tensor"),
        P("section", "dp", "tensor"),
        P("section", "tensor", "dp"),
        P("section", "dp", "tensor"),
        P("section", "dp", "tensor"),
        P("section", "tensor", "dp"),
    )
    return jax.shard_map(local, mesh=mesh, in_specs=in_specs, out_specs=out_specs, check_vma=False)
```

profile of v0, /device:TPU:0, one launch (start us, length us, event | category | flops | bytes accessed | tf_op | source)
XLA Modules:
  0.0 1534.2 jit_solution(213937779309883987)
XLA Ops:
  17.0 22.8 %all-gather.13.cloned.1.call-done = bf16[256,2048]{1,0:T(8,128)(2,1)} async-done(((bf16[64,2048]{1,0:T(8,128)(2,1)}), bf16[256,2048]{1,0:T(8,128)(2,1)}) %all-gather.13.cloned.1.call-update) | async-done | bytes 1048592 | tf_op jit(solution)/shard_map/all_gather | solution.py:155
  48.9 35.3 %reduce-scatter.20.cloned.1.call-done = f32[64,2048]{1,0:T(8,128)} async-done(((f32[256,2048]{1,0:T(8,128)}), f32[64,2048]{1,0:T(8,128)}) %reduce-scatter.20.cloned.1.call-update) | async-done | bytes 524304 | tf_op jit(solution)/shard_map/reduce_scatter | solution.py:160
  87.4 26.7 %all-gather.15.cloned.1.call-done = bf16[256,2048]{1,0:T(8,128)(2,1)} async-done(((bf16[64,2048]{1,0:T(8,128)(2,1)}), bf16[256,2048]{1,0:T(8,128)(2,1)}) %all-gather.15.cloned.1.call-update) | async-done | bytes 1048592 | tf_op jit(solution)/shard_map/all_gather | solution.py:164
  133.4 27.8 %reduce-scatter.22.cloned.1.call-done = bf16[64,2048]{1,0:T(8,128)(2,1)} async-done(((bf16[256,2048]{1,0:T(8,128)(2,1)}), bf16[64,2048]{1,0:T(8,128)(2,1)}) %reduce-scatter.22.cloned.1.call-update) | async-done | bytes 262160 | tf_op jit(solution)/shard_map/reduce_scatter | solution.py:168
  170.7 24.0 %all-gather.17.cloned.1.call-done = bf16[256,2048]{1,0:T(8,128)(2,1)} async-done(((bf16[64,2048]{1,0:T(8,128)(2,1)}), bf16[256,2048]{1,0:T(8,128)(2,1)}) %all-gather.17.cloned.1.call-update) | async-done | bytes 1048592 | tf_op jit(solution)/shard_map/all_gather | solution.py:155
  203.8 35.3 %reduce-scatter.24.cloned.1.call-done = f32[64,2048]{1,0:T(8,128)} async-done(((f32[256,2048]{1,0:T(8,128)}), f32[64,2048]{1,0:T(8,128)}) %reduce-scatter.24.cloned.1.call-update) | async-done | bytes 524304 | tf_op jit(solution)/shard_map/reduce_scatter | solution.py:160
  247.7 21.2 %all-gather.19.cloned.1.call-done = bf16[256,2048]{1,0:T(8,128)(2,1)} async-done(((bf16[64,2048]{1,0:T(8,128)(2,1)}), bf16[256,2048]{1,0:T(8,128)(2,1)}) %all-gather.19.cloned.1.call-update) | async-done | bytes 1048592 | tf_op jit(solution)/shard_map/all_gather | solution.py:164
  290.1 26.2 %reduce-scatter.26.cloned.1.call-done = bf16[64,2048]{1,0:T(8,128)(2,1)} async-done(((bf16[256,2048]{1,0:T(8,128)(2,1)}), bf16[64,2048]{1,0:T(8,128)(2,1)}) %reduce-scatter.26.cloned.1.call-update) | async-done | bytes 262160 | tf_op jit(solution)/shard_map/reduce_scatter | solution.py:168
  327.2 23.9 %all-gather.21.cloned.1.call-done = bf16[256,2048]{1,0:T(8,128)(2,1)} async-done(((bf16[64,2048]{1,0:T(8,128)(2,1)}), bf16[256,2048]{1,0:T(8,128)(2,1)}) %all-gather.21.cloned.1.call-update) | async-done | bytes 1048592 | tf_op jit(solution)/shard_map/all_gather | solution.py:155
  360.2 35.3 %reduce-scatter.28.cloned.1.call-done = f32[64,2048]{1,0:T(8,128)} async-done(((f32[256,2048]{1,0:T(8,128)}), f32[64,2048]{1,0:T(8,128)}) %reduce-scatter.28.cloned.1.call-update) | async-done | bytes 524304 | tf_op jit(solution)/shard_map/reduce_scatter | solution.py:160
  435.8 18.1 %all-gather.25.cloned.1.call-done = bf16[256,2048]{1,0:T(8,128)(2,1)} async-done(((bf16[64,2048]{1,0:T(8,128)(2,1)}), bf16[256,2048]{1,0:T(8,128)(2,1)}) %all-gather.25.cloned.1.call-update) | async-done | bytes 1048592 | tf_op jit(solution)/shard_map/all_gather | solution.py:208
  491.4 23.8 %reduce-scatter.32.cloned.1.call-done = bf16[64,2048]{1,0:T(8,128)(2,1)} async-done(((bf16[256,2048]{1,0:T(8,128)(2,1)}), bf16[64,2048]{1,0:T(8,128)(2,1)}) %reduce-scatter.32.cloned.1.call-update) | async-done | bytes 262160 | tf_op jit(solution)/shard_map/reduce_scatter | solution.py:213
  533.8 12.2 all-gather.27.cloned.1.call-done
  570.2 26.7 %reduce-scatter.34.cloned.1.call-done = bf16[64,2048]{1,0:T(8,128)(2,1)} async-done(((bf16[256,2048]{1,0:T(8,128)(2,1)}), bf16[64,2048]{1,0:T(8,128)(2,1)}) %reduce-scatter.34.cloned.1.call-update) | async-done | bytes 262160 | tf_op jit(solution)/shard_map/reduce_scatter | solution.py:234
  609.4 22.8 %all-gather.29.cloned.1.call-done = bf16[256,2048]{1,0:T(8,128)(2,1)} async-done(((bf16[64,2048]{1,0:T(8,128)(2,1)}), bf16[256,2048]{1,0:T(8,128)(2,1)}) %all-gather.29.cloned.1.call-update) | async-done | bytes 1048592 | tf_op jit(solution)/shard_map/all_gather | solution.py:208
  632.2 10.0 bitcast_dynamic-update-slice_fusion.16
  656.2 26.7 %reduce-scatter.36.cloned.1.call-done = bf16[64,2048]{1,0:T(8,128)(2,1)} async-done(((bf16[256,2048]{1,0:T(8,128)(2,1)}), bf16[64,2048]{1,0:T(8,128)(2,1)}) %reduce-scatter.36.cloned.1.call-update) | async-done | bytes 262160 | tf_op jit(solution)/shard_map/reduce_scatter | solution.py:213
  690.6 23.0 %all-gather.31.cloned.1.call-done = bf16[256,2048]{1,0:T(8,128)(2,1)} async-done(((bf16[64,2048]{1,0:T(8,128)(2,1)}), bf16[256,2048]{1,0:T(8,128)(2,1)}) %all-gather.31.cloned.1.call-update) | async-done | bytes 1048592 | tf_op jit(solution)/shard_map/all_gather | solution.py:223
  736.8 26.6 %reduce-scatter.38.cloned.1.call-done = bf16[64,2048]{1,0:T(8,128)(2,1)} async-done(((bf16[256,2048]{1,0:T(8,128)(2,1)}), bf16[64,2048]{1,0:T(8,128)(2,1)}) %reduce-scatter.38.cloned.1.call-update) | async-done | bytes 262160 | tf_op jit(solution)/shard_map/reduce_scatter | solution.py:234
  775.9 23.4 %all-gather.33.cloned.1.call-done = bf16[256,2048]{1,0:T(8,128)(2,1)} async-done(((bf16[64,2048]{1,0:T(8,128)(2,1)}), bf16[256,2048]{1,0:T(8,128)(2,1)}) %all-gather.33.cloned.1.call-update) | async-done | bytes 1048592 | tf_op jit(solution)/shard_map/all_gather | solution.py:208
  799.4 10.0 bitcast_dynamic-update-slice_fusion.15
  832.0 18.0 %reduce-scatter.40.cloned.1.call-done = bf16[64,2048]{1,0:T(8,128)(2,1)} async-done(((bf16[256,2048]{1,0:T(8,128)(2,1)}), bf16[64,2048]{1,0:T(8,128)(2,1)}) %reduce-scatter.40.cloned.1.call-update) | async-done | bytes 262160 | tf_op jit(solution)/shard_map/reduce_scatter | solution.py:213
  866.0 14.8 all-gather.35.cloned.1.call-done
  937.9 11.7 add_convert_fusion.2
  949.8 9.9 fusion.150
  959.7 11.5 add_convert_fusion.1
  975.4 9.5 fusion.149
  984.8 12.0 add_convert_fusion
  1010.4 78.7 %all-reduce.2 = (f32[2048]{0:T(1024)S(1)}, f32[2048]{0:T(1024)S(1)}) all-reduce(f32[2048]{0:T(1024)S(1)} %select_add_fusion.1, f32[2048]{0:T(1024)S(1)} %select_add_fusion), channel_id=14, replica_groups=mesh['section'=2,'dp'=4,'tensor'=4] {'dp','tensor'}, use_global_device_ids=true, to_apply=%region_42.43.clone | all-reduce | flops 4096 | bytes 32768
  1096.8 131.2 %reduce-scatter.52.cloned.1.call-done = bf16[512,2048]{1,0:T(8,128)(2,1)} async-done(((bf16[2048,2048]{1,0:T(8,128)(2,1)}), bf16[512,2048]{1,0:T(8,128)(2,1)}) %reduce-scatter.52.cloned.1.call-update) | async-done | bytes 2097168 | tf_op jit(solution)/shard_map/reduce_scatter | solution.py:395
  1232.1 143.3 %reduce-scatter.54.cloned.1.call-done = bf16[512,2048]{1,0:T(8,128)(2,1)} async-done(((bf16[2048,2048]{1,0:T(8,128)(2,1)}), bf16[512,2048]{1,0:T(8,128)(2,1)}) %reduce-scatter.54.cloned.1.call-update) | async-done | bytes 2097168 | tf_op jit(solution)/shard_map/reduce_scatter | solution.py:398
  1379.5 143.5 %reduce-scatter.56.cloned.1.call-done = bf16[2048,512]{1,0:T(8,128)(2,1)} async-done(((bf16[2048,2048]{1,0:T(8,128)(2,1)}), bf16[2048,512]{1,0:T(8,128)(2,1)}) %reduce-scatter.56.cloned.1.call-update) | async-done | bytes 2097168 | tf_op jit(solution)/shard_map/reduce_scatter | solution.py:401
  (690 shorter events, 430.7 us)
Async XLA Ops:
  7.2 32.6 %all-gather.13.cloned.1.call-start = ((), (), s32[]{:S(2)}) async-start(), calls=%async_computation.19 | async-start | bytes 1310720 | tf_op jit(solution)/shard_map/all_gather | solution.py:155
  10.3 73.9 %reduce-scatter.20.cloned.1.call-start = ((), (), s32[]{:S(2)}) async-start(), calls=%async_computation.20 | async-start | bytes 2621440 | tf_op jit(solution)/shard_map/reduce_scatter | solution.py:160
  48.9 65.3 %all-gather.15.cloned.1.call-start = ((), (), s32[]{:S(2)}) async-start(), calls=%async_computation.21 | async-start | bytes 1310720 | tf_op jit(solution)/shard_map/all_gather | solution.py:164
  87.4 73.9 %reduce-scatter.22.cloned.1.call-start = ((), (), s32[]{:S(2)}) async-start(), calls=%async_computation.22 | async-start | bytes 1310720 | tf_op jit(solution)/shard_map/reduce_scatter | solution.py:168
  133.4 61.3 %all-gather.17.cloned.1.call-start = ((), (), s32[]{:S(2)}) async-start(), calls=%async_computation.23 | async-start | bytes 1310720 | tf_op jit(solution)/shard_map/all_gather | solution.py:155
  167.8 71.3 %reduce-scatter.24.cloned.1.call-start = ((), (), s32[]{:S(2)}) async-start(), calls=%async_computation.24 | async-start | bytes 2621440 | tf_op jit(solution)/shard_map/reduce_scatter | solution.py:160
  203.7 65.3 %all-gather.19.cloned.1.call-start = ((), (), s32[]{:S(2)}) async-start(), calls=%async_computation.25 | async-start | bytes 1310720 | tf_op jit(solution)/shard_map/all_gather | solution.py:164
  242.2 74.0 %reduce-scatter.26.cloned.1.call-start = ((), (), s32[]{:S(2)}) async-start(), calls=%async_computation.26 | async-start | bytes 1310720 | tf_op jit(solution)/shard_map/reduce_scatter | solution.py:168
  288.4 62.8 %all-gather.21.cloned.1.call-start = ((), (), s32[]{:S(2)}) async-start(), calls=%async_computation.27 | async-start | bytes 1310720 | tf_op jit(solution)/shard_map/all_gather | solution.py:155
  324.3 71.3 %reduce-scatter.28.cloned.1.call-start = ((), (), s32[]{:S(2)}) async-start(), calls=%async_computation.28 | async-start | bytes 2621440 | tf_op jit(solution)/shard_map/reduce_scatter | solution.py:160
  360.2 67.0 %all-gather.23.cloned.1.call-start = ((), (), s32[]{:S(2)}) async-start(), calls=%async_computation.29 | async-start | bytes 1310720 | tf_op jit(solution)/shard_map/all_gather | solution.py:164
  398.6 55.3 %all-gather.25.cloned.1.call-start = ((), (), s32[]{:S(2)}) async-start(), calls=%async_computation.31 | async-start | bytes 1310720 | tf_op jit(solution)/shard_map/all_gather | solution.py:208
  400.8 114.4 %reduce-scatter.32.cloned.1.call-start = ((), (), s32[]{:S(2)}) async-start(), calls=%async_computation.32 | async-start | bytes 1310720 | tf_op jit(solution)/shard_map/reduce_scatter | solution.py:213
  487.3 58.8 %all-gather.27.cloned.1.call-start = ((), (), s32[]{:S(2)}) async-start(), calls=%async_computation.33 | async-start | bytes 1310720 | tf_op jit(solution)/shard_map/all_gather | solution.py:223
  519.2 77.7 %reduce-scatter.34.cloned.1.call-start = ((), (), s32[]{:S(2)}) async-start(), calls=%async_computation.34 | async-start | bytes 1310720 | tf_op jit(solution)/shard_map/reduce_scatter | solution.py:234
  569.1 63.2 %all-gather.29.cloned.1.call-start = ((), (), s32[]{:S(2)}) async-start(), calls=%async_computation.35 | async-start | bytes 1310720 | tf_op jit(solution)/shard_map/all_gather | solution.py:208
  605.4 77.4 %reduce-scatter.36.cloned.1.call-start = ((), (), s32[]{:S(2)}) async-start(), calls=%async_computation.36 | async-start | bytes 1310720 | tf_op jit(solution)/shard_map/reduce_scatter | solution.py:213
  655.0 58.6 %all-gather.31.cloned.1.call-start = ((), (), s32[]{:S(2)}) async-start(), calls=%async_computation.37 | async-start | bytes 1310720 | tf_op jit(solution)/shard_map/all_gather | solution.py:223
  686.8 76.6 %reduce-scatter.38.cloned.1.call-start = ((), (), s32[]{:S(2)}) async-start(), calls=%async_computation.38 | async-start | bytes 1310720 | tf_op jit(solution)/shard_map/reduce_scatter | solution.py:234
  735.5 63.8 %all-gather.33.cloned.1.call-start = ((), (), s32[]{:S(2)}) async-start(), calls=%async_computation.39 | async-start | bytes 1310720 | tf_op jit(solution)/shard_map/all_gather | solution.py:208
  766.6 3.4 collective-permute-start.3
  772.6 77.4 %reduce-scatter.40.cloned.1.call-start = ((), (), s32[]{:S(2)}) async-start(), calls=%async_computation.40 | async-start | bytes 1310720 | tf_op jit(solution)/shard_map/reduce_scatter | solution.py:213
  822.1 58.7 %all-gather.35.cloned.1.call-start = ((), (), s32[]{:S(2)}) async-start(), calls=%async_computation.41 | async-start | bytes 1310720 | tf_op jit(solution)/shard_map/all_gather | solution.py:223
  854.0 146.5 %reduce-scatter.30.cloned.1.call-start = ((), (), s32[]{:S(2)}) async-start(), calls=%async_computation.30 | async-start | bytes 1310720 | tf_op jit(solution)/shard_map/reduce_scatter | solution.py:168
  865.8 140.0 %reduce-scatter.46.cloned.1.call-start = ((), (), s32[]{:S(2)}) async-start(), calls=%async_computation.44 | async-start | bytes 655360 | tf_op jit(solution)/shard_map/reduce_scatter | solution.py:386
  895.5 112.0 %reduce-scatter.48.cloned.1.call-start = ((), (), s32[]{:S(2)}) async-start(), calls=%async_computation.45 | async-start | bytes 655360 | tf_op jit(solution)/shard_map/reduce_scatter | solution.py:389
  904.9 104.2 %reduce-scatter.42.cloned.1.call-start = ((), (), s32[]{:S(2)}) async-start(), calls=%async_computation.42 | async-start | bytes 1310720 | tf_op jit(solution)/shard_map/reduce_scatter | solution.py:234
  909.5 182.9 %reduce-scatter.44.cloned.1.call-start = ((), (), s32[]{:S(2)}) async-start(), calls=%async_computation.43 | async-start | bytes 2621440 | tf_op jit(solution)/shard_map/reduce_scatter | solution.py:383
  916.0 178.7 %reduce-scatter.50.cloned.1.call-start = ((), (), s32[]{:S(2)}) async-start(), calls=%async_computation.46 | async-start | bytes 2621440 | tf_op jit(solution)/shard_map/reduce_scatter | solution.py:392
  923.8 304.1 %reduce-scatter.52.cloned.1.call-start = ((), (), s32[]{:S(2)}) async-start(), calls=%async_computation.47 | async-start | bytes 10485760 | tf_op jit(solution)/shard_map/reduce_scatter | solution.py:395
  949.6 425.8 %reduce-scatter.54.cloned.1.call-start = ((), (), s32[]{:S(2)}) async-start(), calls=%async_computation.48 | async-start | bytes 10485760 | tf_op jit(solution)/shard_map/reduce_scatter | solution.py:398
  971.2 551.8 %reduce-scatter.56.cloned.1.call-start = ((), (), s32[]{:S(2)}) async-start(), calls=%async_computation.49 | async-start | bytes 10485760 | tf_op jit(solution)/shard_map/reduce_scatter | solution.py:401
  (166 other events, 1044.4 us)
Sparse Core Ops, SparseCore 0:
  10.5 29.3 all-gather.12
  49.0 35.1 reduce-scatter.19
  87.5 26.6 all-gather.14
  133.5 27.7 reduce-scatter.21
  167.9 26.7 all-gather.16
  203.9 35.1 reduce-scatter.23
  242.3 26.6 all-gather.18
  288.5 27.7 reduce-scatter.25
  324.4 26.7 all-gather.20
  360.3 35.1 reduce-scatter.27
  398.8 26.6 all-gather.22
  427.3 26.6 all-gather.24
  487.4 27.7 reduce-scatter.31
  519.4 26.6 all-gather.26
  569.2 27.7 reduce-scatter.33
  605.6 26.6 all-gather.28
  655.1 27.7 reduce-scatter.35
  686.9 26.6 all-gather.30
  735.7 27.7 reduce-scatter.37
  772.7 26.6 all-gather.32
  822.2 27.7 reduce-scatter.39
  854.2 26.6 all-gather.34
  884.3 27.7 reduce-scatter.29
  914.3 21.6 reduce-scatter.45
  938.3 19.9 reduce-scatter.47
  961.9 26.0 reduce-scatter.41
  990.6 44.2 reduce-scatter.43
  1037.9 43.5 reduce-scatter.49
  1083.9 144.0 reduce-scatter.51
  1230.2 145.1 reduce-scatter.53
  1377.8 145.1 reduce-scatter.55
where the time goes:
time: 1550 us; the launch traced here: 1530 us
  waiting for transfers between devices  937 us (60%)
  matrix products  284 us (18%)
  other arithmetic  111 us (7%)
  local copies, waits for them, and re-layouts  87.5 us (6%)
  blocking collectives  78.7 us (5%)
  starting transfers between devices  19.1 us (1%)
  between operations  17.7 us (1%)
    reduce_scatter x1, waiting for transfers between devices, local(): lax.psum_scatter(grads_sum[6].astype(jnp.bfloat16), 'dp', scatter_dimensi...  143 us
    reduce_scatter x1, waiting for transfers between devices, local(): lax.psum_scatter(grads_sum[5].astype(jnp.bfloat16), 'dp', scatter_dimensi...  143 us
    reduce_scatter x1, waiting for transfers between devices, local(): lax.psum_scatter(grads_sum[4].astype(jnp.bfloat16), 'dp', scatter_dimensi...  131 us
    reduce_scatter x3, waiting for transfers between devices, forward_layer(): lax.psum_scatter(matmul(attended, w_out_v), 'tensor', scatter_dimension=0...  106 us
    dot_general x21, matrix products, times_transposed(): lax.dot_general(left_side, right_side, (((1,), (1,)), ((), ())), preferre...  80.3 us
    dot_general x14, matrix products, transposed_times(): lax.dot_general(left_side, right_side, (((0,), (0,)), ((), ())), preferre...  79.5 us
    unnamed x1, blocking collectives  78.7 us
    dot_general x21, matrix products, matmul(): return jnp.dot(left_side, right_side, preferred_element_type=jnp.float32)  74.8 us
  transfers between devices with their start and end apart: 35, of which 28 were waited for; matrix products, arithmetic and copies ran while one was open for 15% of the time, Pallas kernels for 0%

commit v1 on v0

v1 whole, which is shorter than its diff:
```python
import functools

import jax
import jax.numpy as jnp
from jax import lax
from jax.experimental import pallas as pl
from jax.experimental.pallas import tpu as pltpu
from jax.sharding import PartitionSpec as P

HD = 64
EPSILON = 1e-05
NEGATIVE = -1e30
BF = jnp.bfloat16
F32 = jnp.float32
VMEM = pl.BlockSpec(memory_space=pltpu.VMEM)
ANY = pl.BlockSpec(memory_space=pl.ANY)
LIMIT = 56 * 1024 * 1024


def nn(a, b):
    return jnp.dot(a, b, preferred_element_type=F32)


def nt(a, b):
    return lax.dot_general(a, b, (((1,), (1,)), ((), ())), preferred_element_type=F32)


def tn(a, b):
    return lax.dot_general(a, b, (((0,), (0,)), ((), ())), preferred_element_type=F32)


def shaped(shape, dtype):
    return jax.ShapeDtypeStruct(shape, dtype)


def cost(flops, nbytes):
    return pl.CostEstimate(flops=int(flops), bytes_accessed=int(nbytes), transcendentals=0)


def partners(size):
    return [[(a, a ^ k) for a in range(size)] for k in range(1, size)]


def gather_rows(x, size):
    return [x] + [lax.ppermute(x, "tensor", pairs) for pairs in partners(size)]


def scatter_rows(parts, size):
    return [parts[0]] + [
        lax.ppermute(part, "tensor", pairs) for part, pairs in zip(parts[1:], partners(size))
    ]


def swapped(x):
    return lax.ppermute(x, "section", [(0, 1), (1, 0)])


def norm_kernel(x_ref, gain_ref, out_ref):
    x = x_ref[...].astype(F32)
    scale = lax.rsqrt(jnp.mean(x * x, axis=-1, keepdims=True) + EPSILON)
    out_ref[...] = (x * scale * gain_ref[...]).astype(BF)


def norm_rows(x, gain):
    return pl.pallas_call(
        norm_kernel, out_shape=shaped(x.shape, BF), in_specs=[VMEM] * 2, out_specs=VMEM
    )(x, gain)


def add_norm_kernel(round_out, base_ref, a_ref, b_ref, c_ref, d_ref, gain_ref, out_ref, normed_ref):
    x = base_ref[...].astype(F32) + (
        (a_ref[...].astype(F32) + b_ref[...].astype(F32))
        + (c_ref[...].astype(F32) + d_ref[...].astype(F32))
    )
    if round_out:
        x = x.astype(BF)
        out_ref[...] = x
        x = x.astype(F32)
    else:
        out_ref[...] = x
    scale = lax.rsqrt(jnp.mean(x * x, axis=-1, keepdims=True) + EPSILON)
    normed_ref[...] = (x * scale * gain_ref[...]).astype(BF)


def add_norm(base, terms, gain, round_out):
    return pl.pallas_call(
        functools.partial(add_norm_kernel, round_out),
        out_shape=(shaped(base.shape, BF if round_out else F32), shaped(base.shape, BF)),
        in_specs=[VMEM] * 6,
        out_specs=(VMEM, VMEM),
    )(base, *terms, gain)


def norm_back_kernel(base_ref, a_ref, b_ref, c_ref, d_ref, gain_ref, res_ref, out_ref, low_ref, gp_ref):
    g = (a_ref[...].astype(F32) + b_ref[...].astype(F32)) + (
        c_ref[...].astype(F32) + d_ref[...].astype(F32)
    )
    x = base_ref[...].astype(F32)
    scale = lax.rsqrt(jnp.mean(x * x, axis=-1, keepdims=True) + EPSILON)
    y = x * scale
    gp_ref[...] = jnp.sum(g * y, axis=0, keepdims=True)
    e = g * gain_ref[...]
    out = res_ref[...].astype(F32) + scale * (e - y * jnp.mean(e * y, axis=-1, keepdims=True))
    out_ref[...] = out
    low_ref[...] = out.astype(BF)


def norm_back(base, terms, gain, residual):
    return pl.pallas_call(
        norm_back_kernel,
        out_shape=(shaped(base.shape, F32), shaped(base.shape, BF), shaped((1, base.shape[1]), F32)),
        in_specs=[VMEM] * 7,
        out_specs=(VMEM,) * 3,
    )(base, *terms, gain, residual)


def turn(x, cos, sin, low):
    return x * cos + jnp.where(low, pltpu.roll(x, 96, 1), pltpu.roll(x, 32, 1)) * sin


def fetch_start(mine, ours, theirs, buffer, sem):
    @pl.when(mine)
    def _():
        pltpu.make_async_copy(ours, buffer, sem).start()

    @pl.when(jnp.logical_not(mine))
    def _():
        pltpu.make_async_copy(theirs, buffer, sem).start()


def fetch_wait(ours, buffer, sem):
    pltpu.make_async_copy(ours, buffer, sem).wait()


def spread(x, first_lanes):
    x = x.astype(F32)
    moved = pltpu.roll(x, 64, 1)
    zero = jnp.zeros_like(x)
    return [
        (jnp.where(first_lanes, x, zero).astype(BF), jnp.where(first_lanes, zero, moved).astype(BF)),
        (jnp.where(first_lanes, moved, zero).astype(BF), jnp.where(first_lanes, zero, x).astype(BF)),
    ]


def soft(q, k, mask):
    scores = jnp.where(mask, nt(q, k) * HD**-0.5, NEGATIVE)
    lifted = jnp.exp(scores - jnp.max(scores, axis=-1, keepdims=True))
    return lifted * (1.0 / jnp.sum(lifted, axis=-1, keepdims=True))


def attend_fwd_kernel(
    layer, x0, x1, x2, x3, wq_a, wq_b, wk_a, wk_b, wv_a, wv_b, wo_a, wo_b, cos_ref, sin_ref, pq_ref, pk_ref,
    p0, p1, p2, p3, x_out, q_out, k_out, v_out, att_out, wq, wk, wv, wo, sems,
):
    mine = lax.axis_index("section") == layer
    pairs = [(wq_a, wq_b, wq), (wk_a, wk_b, wk), (wv_a, wv_b, wv), (wo_a, wo_b, wo)]
    for n, (a, b, buffer) in enumerate(pairs):
        fetch_start(mine, a, b, buffer, sems.at[n])
    rows = x0.shape[0]
    for n, x in enumerate((x0, x1, x2, x3)):
        x_out[n * rows : (n + 1) * rows, :] = x[...]
    whole = 4 * rows
    lane = lax.broadcasted_iota(jnp.int32, (whole, 128), 1)
    low = (lane & (HD - 1)) < HD // 2
    first_lanes = lane < HD
    cos, sin = cos_ref[...], sin_ref[...]
    mask = pk_ref[...] <= pq_ref[...]
    for n in range(3):
        fetch_wait(pairs[n][0], pairs[n][2], sems.at[n])
    x = x_out[...]
    k = turn(nn(x, wk[...]), cos, sin, low).astype(BF)
    v = nn(x, wv[...]).astype(BF)
    k_out[...] = k
    v_out[...] = v
    keys, values = spread(k, first_lanes), spread(v, first_lanes)
    for p in range(q_out.shape[1] // 128):
        cut = slice(p * 128, (p + 1) * 128)
        q = turn(nn(x, wq[:, cut]), cos, sin, low).astype(BF)
        q_out[:, cut] = q
        head = p // 2
        att_out[:, cut] = (
            nn(soft(q, keys[head][0], mask).astype(BF), values[head][0])
            + nn(soft(q, keys[head][1], mask).astype(BF), values[head][1])
        ).astype(BF)
    fetch_wait(wo_a, wo, sems.at[3])
    att = att_out[...]
    for n, part in enumerate((p0, p1, p2, p3)):
        part[...] = jnp.zeros_like(part)
    columns = 512
    for c in range(p0.shape[1] // columns):
        cut = slice(c * columns, (c + 1) * columns)
        out = nn(att, wo[:, cut]).astype(BF)
        for n, part in enumerate((p0, p1, p2, p3)):
            part[:, cut] = out[n * rows : (n + 1) * rows, :]


def attend_fwd(layer, blocks, weights, tables):
    rows, depth = blocks[0].shape
    wq, wk, wv, wo = weights
    whole, width, narrow = 4 * rows, wq[0].shape[1], wk[0].shape[1]
    block = shaped((rows, depth), BF)
    return pl.pallas_call(
        functools.partial(attend_fwd_kernel, layer),
        out_shape=(block,) * 4
        + (
            shaped((whole, depth), BF),
            shaped((whole, width), BF),
            shaped((whole, narrow), BF),
            shaped((whole, narrow), BF),
            shaped((whole, width), BF),
        ),
        in_specs=[VMEM] * 4 + [ANY] * 8 + [VMEM] * 4,
        out_specs=(VMEM,) * 9,
        scratch_shapes=[
            pltpu.VMEM(wq[0].shape, BF),
            pltpu.VMEM(wk[0].shape, BF),
            pltpu.VMEM(wv[0].shape, BF),
            pltpu.VMEM(wo[0].shape, BF),
            pltpu.SemaphoreType.DMA((4,)),
        ],
        compiler_params=pltpu.CompilerParams(vmem_limit_bytes=LIMIT),
        cost_estimate=cost(4e9, 12e6),
    )(*blocks, *wq, *wk, *wv, *wo, *tables)


def attend_bwd_kernel(
    layer, d0, d1, d2, d3, q_ref, k_ref, v_ref, wq_a, wq_b, wk_a, wk_b, wv_a, wv_b, wo_a, wo_b,
    cos_ref, sin_ref, pq_ref, pk_ref,
    p0, p1, p2, p3, dm_out, dq_out, dk_out, dv_out, wq, wk, wv, wo, sems,
):
    mine = lax.axis_index("section") == layer
    pairs = [(wo_a, wo_b, wo), (wq_a, wq_b, wq), (wk_a, wk_b, wk), (wv_a, wv_b, wv)]
    for n, (a, b, buffer) in enumerate(pairs):
        fetch_start(mine, a, b, buffer, sems.at[n])
    rows = d0.shape[0]
    for n, d in enumerate((d0, d1, d2, d3)):
        dm_out[n * rows : (n + 1) * rows, :] = d[...]
    whole = 4 * rows
    lane = lax.broadcasted_iota(jnp.int32, (whole, 128), 1)
    low = (lane & (HD - 1)) < HD // 2
    first_lanes = lane < HD
    cos, sin = cos_ref[...], -sin_ref[...]
    mask = pk_ref[...] <= pq_ref[...]
    keys, values = spread(k_ref[...], first_lanes), spread(v_ref[...], first_lanes)
    fetch_wait(wo_a, wo, sems.at[0])
    dm = dm_out[...]
    dk_sums, dv_sums = [[None, None], [None, None]], [[None, None], [None, None]]

    def add(sums, head, side, term):
        sums[head][side] = term if sums[head][side] is None else sums[head][side] + term

    for p in range(q_ref.shape[1] // 128):
        cut = slice(p * 128, (p + 1) * 128)
        head = p // 2
        q = q_ref[:, cut]
        d_att = nt(dm, wo[cut, :]).astype(BF)
        d_q = None
        for side in range(2):
            probs = soft(q, keys[head][side], mask)
            d_probs = nt(d_att, values[head][side])
            inner = jnp.sum(d_probs * probs, axis=-1, keepdims=True)
            d_raw = (probs * (d_probs - inner) * HD**-0.5).astype(BF)
            term = nn(d_raw, keys[head][side])
            d_q = term if d_q is None else d_q + term
            add(dk_sums, head, side, tn(d_raw, q))
            add(dv_sums, head, side, tn(probs.astype(BF), d_att))
        dq_out[:, cut] = turn(d_q, cos, sin, low).astype(BF)

    def folded(sums):
        return jnp.where(
            first_lanes,
            sums[0][0] + pltpu.roll(sums[0][1], 64, 1),
            pltpu.roll(sums[1][0], 64, 1) + sums[1][1],
        )

    dk_out[...] = turn(folded(dk_sums), cos, sin, low).astype(BF)
    dv_out[...] = folded(dv_sums).astype(BF)
    for n in range(1, 4):
        fetch_wait(pairs[n][0], pairs[n][2], sems.at[n])
    dq, dk, dv = dq_out[...], dk_out[...], dv_out[...]
    columns = 512
    for c in range(p0.shape[1] // columns):
        cut = slice(c * columns, (c + 1) * columns)
        out = (nt(dq, wq[cut, :]) + nt(dk, wk[cut, :]) + nt(dv, wv[cut, :])).astype(BF)
        for n, part in enumerate((p0, p1, p2, p3)):
            part[:, cut] = out[n * rows : (n + 1) * rows, :]


def attend_bwd(layer, blocks, qkv, weights, tables):
    rows, depth = blocks[0].shape
    wq, wk, wv, wo = weights
    whole, width, narrow = 4 * rows, wq[0].shape[1], wk[0].shape[1]
    block = shaped((rows, depth), BF)
    return pl.pallas_call(
        functools.partial(attend_bwd_kernel, layer),
        out_shape=(block,) * 4
        + (
            shaped((whole, depth), BF),
            shaped((whole, width), BF),
            shaped((whole, narrow), BF),
            shaped((whole, narrow), BF),
        ),
        in_specs=[VMEM] * 7 + [ANY] * 8 + [VMEM] * 4,
        out_specs=(VMEM,) * 8,
        scratch_shapes=[
            pltpu.VMEM(wq[0].shape, BF),
            pltpu.VMEM(wk[0].shape, BF),
            pltpu.VMEM(wv[0].shape, BF),
            pltpu.VMEM(wo[0].shape, BF),
            pltpu.SemaphoreType.DMA((4,)),
        ],
        compiler_params=pltpu.CompilerParams(vmem_limit_bytes=LIMIT),
        cost_estimate=cost(5e9, 14e6),
    )(*blocks, *qkv, *wq, *wk, *wv, *wo, *tables)


TILE = 256


def chosen(layer, a, b, sec):
    pass


def mlp_fwd_kernel(
    layer, s_ref, x0, x1, x2, x3, wg_a, wg_b, wu_a, wu_b, wd_a, wd_b,
    p0, p1, p2, p3, x_out, gate_out, up_out, total,
):
    f = pl.program_id(0)
    rows = x0.shape[0]

    @pl.when(f == 0)
    def _():
        for n, x in enumerate((x0, x1, x2, x3)):
            x_out[n * rows : (n + 1) * rows, :] = x[...]
        total[...] = jnp.zeros_like(total)

    def work(wg, wu, wd):
        x = x_out[...]
        gate, up = nn(x, wg[...]), nn(x, wu[...])
        gate_out[...] = gate.astype(BF)
        up_out[...] = up.astype(BF)
        hidden = (gate * jax.nn.sigmoid(gate) * up).astype(BF)
        total[...] += nn(hidden, wd[...])

    mine = s_ref[0] == layer
    pl.when(mine)(lambda: work(wg_a, wu_a, wd_a))
    pl.when(jnp.logical_not(mine))(lambda: work(wg_b, wu_b, wd_b))

    @pl.when(f == pl.num_programs(0) - 1)
    def _():
        for n, part in enumerate((p0, p1, p2, p3)):
            part[...] = total[n * rows : (n + 1) * rows, :].astype(BF)


def pair_specs(layer, shape, dim, tile):
    block = tuple(tile if d == dim else size for d, size in enumerate(shape))

    def spec(flip):
        def index(f, s):
            used = (s[0] == layer) != flip
            return tuple(jnp.where(used, f, 0) if d == dim else 0 for d in range(2))

        return pl.BlockSpec(block, index)

    return [spec(False), spec(True)]


def whole_spec(shape):
    return pl.BlockSpec(shape, lambda f, s: (0,) * len(shape))


def mlp_fwd(layer, sec, blocks, weights):
    rows, depth = blocks[0].shape
    wg, wu, wd = weights
    units, whole = wg[0].shape[1], 4 * rows
    columns = pl.BlockSpec((whole, TILE), lambda f, s: (0, f))
    return pl.pallas_call(
        functools.partial(mlp_fwd_kernel, layer),
        grid_spec=pltpu.PrefetchScalarGridSpec(
            num_scalar_prefetch=1,
            grid=(units // TILE,),
            in_specs=[whole_spec((rows, depth))] * 4
            + pair_specs(layer, wg[0].shape, 1, TILE)
            + pair_specs(layer, wu[0].shape, 1, TILE)
            + pair_specs(layer, wd[0].shape, 0, TILE),
            out_specs=[whole_spec((rows, depth))] * 4 + [whole_spec((whole, depth)), columns, columns],
            scratch_shapes=[pltpu.VMEM((whole, depth), F32)],
        ),
        out_shape=[shaped((rows, depth), BF)] * 4
        + [shaped((whole, depth), BF), shaped((whole, units), BF), shaped((whole, units), BF)],
        compiler_params=pltpu.CompilerParams(vmem_limit_bytes=LIMIT),
        cost_estimate=cost(6 * whole * units * depth, 30e6),
    )(sec, *blocks, *wg, *wu, *wd)


def mlp_bwd_kernel(
    layer, s_ref, g0, g1, g2, g3, gate_ref, up_ref, wg_a, wg_b, wu_a, wu_b, wd_a, wd_b,
    p0, p1, p2, p3, g_out, total,
):
    f = pl.program_id(0)
    rows = g0.shape[0]

    @pl.when(f == 0)
    def _():
        for n, g in enumerate((g0, g1, g2, g3)):
            g_out[n * rows : (n + 1) * rows, :] = g[...]
        total[...] = jnp.zeros_like(total)

    def work(wg, wu, wd):
        d_hidden = nt(g_out[...], wd[...])
        gate, up = gate_ref[...].astype(F32), up_ref[...].astype(F32)
        s = jax.nn.sigmoid(gate)
        d_up = (d_hidden * gate * s).astype(BF)
        d_gate = (d_hidden * up * s * (1.0 + gate * (1.0 - s))).astype(BF)
        total[...] += nt(d_gate, wg[...]) + nt(d_up, wu[...])

    mine = s_ref[0] == layer
    pl.when(mine)(lambda: work(wg_a, wu_a, wd_a))
    pl.when(jnp.logical_not(mine))(lambda: work(wg_b, wu_b, wd_b))

    @pl.when(f == pl.num_programs(0) - 1)
    def _():
        for n, part in enumerate((p0, p1, p2, p3)):
            part[...] = total[n * rows : (n + 1) * rows, :].astype(BF)


def mlp_bwd(layer, sec, blocks, gate, up, weights):
    rows, depth = blocks[0].shape
    wg, wu, wd = weights
    units, whole = wg[0].shape[1], 4 * rows
    columns = pl.BlockSpec((whole, TILE), lambda f, s: (0, f))
    return pl.pallas_call(
        functools.partial(mlp_bwd_kernel, layer),
        grid_spec=pltpu.PrefetchScalarGridSpec(
            num_scalar_prefetch=1,
            grid=(units // TILE,),
            in_specs=[whole_spec((rows, depth))] * 4
            + [columns, columns]
            + pair_specs(layer, wg[0].shape, 1, TILE)
            + pair_specs(layer, wu[0].shape, 1, TILE)
            + pair_specs(layer, wd[0].shape, 0, TILE),
            out_specs=[whole_spec((rows, depth))] * 4 + [whole_spec((whole, depth))],
            scratch_shapes=[pltpu.VMEM((whole, depth), F32)],
        ),
        out_shape=[shaped((rows, depth), BF)] * 4 + [shaped((whole, depth), BF)],
        compiler_params=pltpu.CompilerParams(vmem_limit_bytes=LIMIT),
        cost_estimate=cost(6 * whole * units * depth, 30e6),
    )(sec, *blocks, gate, up, *wg, *wu, *wd)


WIDE = 512
CHUNK = 512


def mlp_grads_kernel(x_ref, g_ref, wg, wu, wd, dwg, dwu, dwd):
    c = pl.program_id(1)
    share = dwg.shape[0]
    start = pl.multiple_of(lax.axis_index("dp") * share, share)
    x, g = x_ref[...], g_ref[...]
    gate, up = nn(x, wg[...]), nn(x, wu[...])
    d_hidden = nt(g, wd[...])
    s = jax.nn.sigmoid(gate)
    gated = gate * s
    hidden = (gated * up).astype(BF)
    d_up = (d_hidden * gated).astype(BF)
    d_gate = (d_hidden * up * s * (1.0 + gate * (1.0 - s))).astype(BF)
    x_cut, g_cut = x_ref[:, pl.ds(start, share)], g_ref[:, pl.ds(start, share)]

    @pl.when(c == 0)
    def _():
        dwg[...] = jnp.zeros_like(dwg)
        dwu[...] = jnp.zeros_like(dwu)
        dwd[...] = jnp.zeros_like(dwd)

    dwg[...] += tn(x_cut, d_gate)
    dwu[...] += tn(x_cut, d_up)
    dwd[...] += tn(hidden, g_cut)


def mlp_grads(x, g, wg, wu, wd, groups):
    rows, depth = x.shape
    units, share = wg.shape[1], depth // groups
    return pl.pallas_call(
        mlp_grads_kernel,
        grid=(units // WIDE, rows // CHUNK),
        in_specs=[
            pl.BlockSpec((CHUNK, depth), lambda f, c: (c, 0)),
            pl.BlockSpec((CHUNK, depth), lambda f, c: (c, 0)),
            pl.BlockSpec((depth, WIDE), lambda f, c: (0, f)),
            pl.BlockSpec((depth, WIDE), lambda f, c: (0, f)),
            pl.BlockSpec((WIDE, depth), lambda f, c: (f, 0)),
        ],
        out_specs=[
            pl.BlockSpec((share, WIDE), lambda f, c: (0, f)),
            pl.BlockSpec((share, WIDE), lambda f, c: (0, f)),
            pl.BlockSpec((WIDE, share), lambda f, c: (f, 0)),
        ],
        out_shape=[shaped((share, units), F32), shaped((share, units), F32), shaped((units, share), F32)],
        compiler_params=pltpu.CompilerParams(vmem_limit_bytes=LIMIT),
        cost_estimate=cost(6 * rows * units * (depth + share), 100e6),
    )(x, g, wg, wu, wd)


def rope_tables(places, head_size):
    half_width = head_size // 2
    counter = jnp.arange(half_width, dtype=F32)
    base_freq = 1.0 / 500000.0 ** (2.0 * counter / head_size)
    wavelength = 2.0 * jnp.pi / base_freq
    blend_part = (8192.0 / wavelength - 1.0) / 3.0
    middle = (1.0 - blend_part) * base_freq / 32.0 + blend_part * base_freq
    frequency = jnp.where(
        wavelength < 2048.0, base_freq, jnp.where(wavelength > 8192.0, base_freq / 32.0, middle)
    )
    angles = places.astype(F32)[:, None] * frequency[None, :]
    cosine, sine = jnp.cos(angles), jnp.sin(angles)
    return (
        jnp.concatenate([cosine] * 4, axis=1),
        jnp.concatenate([-sine, sine, -sine, sine], axis=1),
    )


def summed_shares(parts, tensor_size, groups):
    kinds, depth = parts.shape
    t, i = lax.axis_index("tensor"), lax.axis_index("dp")
    share = depth // (tensor_size * groups)
    cut = parts.reshape(kinds, groups, tensor_size, share)
    total = lax.dynamic_index_in_dim(cut, t, 2, False)
    for k, pairs in enumerate(partners(tensor_size), 1):
        total = total + lax.ppermute(lax.dynamic_index_in_dim(cut, t ^ k, 2, False), "tensor", pairs)
    mine = lax.dynamic_index_in_dim(total, i, 1, False)
    for k in range(1, groups):
        pairs = [(a, (a + k) % groups) for a in range(groups)]
        send = lax.dynamic_index_in_dim(total, lax.rem(i + k, groups), 1, False)
        mine = mine + lax.ppermute(send, "dp", pairs)
    return mine


def attend_grads(sec, groups, x, att, dm, dq, dk, dv):
    depth = x.shape[1]
    d_qkv = jnp.concatenate([dq, dk, dv], axis=1)
    cut = x.reshape(x.shape[0], groups, 2, depth // (2 * groups))
    halves = [cut[:, :, c].reshape(x.shape[0], depth // 2) for c in range(2)]
    half_att = [att[:, : att.shape[1] // 2], att[:, att.shape[1] // 2 :]]
    first = sec == 0
    keep_x, send_x = jnp.where(first, halves[0], halves[1]), jnp.where(first, halves[1], halves[0])
    keep_a = jnp.where(first, half_att[0], half_att[1])
    send_a = jnp.where(first, half_att[1], half_att[0])
    in_grad = tn(keep_x, d_qkv) + tn(swapped(send_x), swapped(d_qkv))
    out_grad = tn(keep_a, dm) + tn(swapped(send_a), swapped(dm))
    return (
        lax.psum_scatter(in_grad.astype(BF), "dp", scatter_dimension=0, tiled=True),
        lax.psum_scatter(out_grad.astype(BF), "dp", scatter_dimension=1, tiled=True),
    )


def local(groups, size, tokens, lengths, cotangent, attn_gain, mlp_gain, *weights):
    sec, t = lax.axis_index("section"), lax.axis_index("tensor")
    first = sec == 0
    rows, depth = tokens.shape[1:]
    mine = [w[0] for w in weights]
    gains = jnp.concatenate([attn_gain, mlp_gain], axis=0)
    other_gains = swapped(gains)
    pairs = [(w, swapped(w)) for w in mine]
    attn_w, mlp_w = pairs[:4], pairs[4:]
    layer_gains = [jnp.where(sec == l, gains, other_gains) for l in range(2)]
    attn_gains = [g[0:1] for g in layer_gains]
    mlp_gains = [g[1:2] for g in layer_gains]
    length = lax.dynamic_index_in_dim(lengths[:, 0], sec, 0, keepdims=False)
    tok = lax.dynamic_index_in_dim(tokens, sec, 0, keepdims=False)
    cot = lax.dynamic_index_in_dim(cotangent, sec, 0, keepdims=False)
    within = jnp.arange(rows, dtype=jnp.int32)
    own_places = t * rows + within
    places = jnp.concatenate([(t ^ k) * rows + within for k in range(size)])
    readable = jnp.where(places < length, places, jnp.int32(1 << 20))
    tables = rope_tables(places, HD) + (places[:, None], readable[None, :])
    sec_ref = sec.reshape(1).astype(jnp.int32)

    def over_groups(x):
        return lax.all_gather(x, "dp", axis=0, tiled=True)

    g_low = jnp.where((own_places < length)[:, None], cot, jnp.zeros_like(cot))
    g_blocks = gather_rows(g_low, size)

    stream, acts, kept = tok, [], []
    normed = norm_rows(tok, attn_gains[0])
    for l in range(2):
        *parts, x_attn, q, k, v, att = attend_fwd(l, gather_rows(normed, size), attn_w, tables)
        mid, normed = add_norm(stream, scatter_rows(parts, size), mlp_gains[l], False)
        *parts, x_mlp, gate, up = mlp_fwd(l, sec_ref, gather_rows(normed, size), mlp_w)
        act, normed = add_norm(mid, scatter_rows(parts, size), attn_gains[1], True)
        kept.append((stream, x_attn, q, k, v, att, mid, x_mlp, gate, up))
        acts.append(act)
        stream = act

    d_res = g_low
    input_grads, gain_parts, attn_shares, xs, gs = [None] * 2, [None] * 2, [None] * 2, [None] * 2, [None] * 2
    for l in (1, 0):
        stream, x_attn, q, k, v, att, mid, x_mlp, gate, up = kept[l]
        if l == 0:
            g_blocks = gather_rows(d_res, size)
        *parts, g_all = mlp_bwd(l, sec_ref, g_blocks, gate, up, mlp_w)
        d_mid, d_mid_low, mlp_part = norm_back(mid, scatter_rows(parts, size), mlp_gains[l], d_res)
        *parts, dm, dq, dk, dv = attend_bwd(l, gather_rows(d_mid_low, size), (q, k, v), attn_w, tables)
        d_stream, d_low, attn_part = norm_back(stream, scatter_rows(parts, size), attn_gains[l], d_mid)
        attn_shares[l] = attend_grads(sec, groups, x_attn, att, dm, dq, dk, dv)
        xs[l], gs[l] = over_groups(x_mlp), over_groups(g_all)
        input_grads[l], gain_parts[l], d_res = d_stream, (attn_part, mlp_part), d_low

    def for_layer(pair):
        keep, send = jnp.where(first, pair[0], pair[1]), jnp.where(first, pair[1], pair[0])
        return keep, swapped(send)

    def both(pair):
        keep, came = for_layer(pair)
        return jnp.stack([jnp.where(first, keep, came), jnp.where(first, came, keep)])

    x = jnp.concatenate(for_layer(xs), axis=0)
    g = jnp.concatenate(for_layer(gs), axis=0)
    gate_grad, up_grad, down_grad = mlp_grads(x, g, *mine[4:], groups)
    in_rows = jnp.concatenate(list(both([s[0] for s in attn_shares])), axis=0).astype(F32)
    out_grad = jnp.concatenate(list(both([s[1] for s in attn_shares])), axis=0).astype(F32)
    width, narrow = mine[0].shape[1], mine[1].shape[1]
    keep, came = for_layer([jnp.concatenate(parts, axis=0) for parts in gain_parts])
    shares = summed_shares(keep + came, size, groups)
    return (
        both(acts)[None],
        both(input_grads)[None],
        shares[0:1],
        shares[1:2],
        in_rows[None, :, :width],
        in_rows[None, :, width : width + narrow],
        in_rows[None, :, width + narrow :],
        out_grad[None],
        gate_grad[None],
        up_grad[None],
        down_grad[None],
    )


def solution(mesh):
    rows = P(None, ("dp", "tensor"), None)
    in_specs = (
        rows,
        P(None, "dp"),
        rows,
        P("section", None),
        P("section", None),
        P("section", None, "tensor"),
        P("section", None, "tensor"),
        P("section", None, "tensor"),
        P("section", "tensor", None),
        P("section", None, "tensor"),
        P("section", None, "tensor"),
        P("section", "tensor", None),
    )
    out_rows = P("section", None, ("dp", "tensor"), None)
    shares = P("section", ("dp", "tensor"))
    by_dp, by_tensor = P("section", "dp", "tensor"), P("section", "tensor", "dp")
    out_specs = (
        out_rows, out_rows, shares, shares, by_dp, by_dp, by_dp, by_tensor, by_dp, by_dp, by_tensor,
    )
    step = functools.partial(local, mesh.shape["dp"], mesh.shape["tensor"])
    return jax.shard_map(step, mesh=mesh, in_specs=in_specs, out_specs=out_specs, check_vma=False)
```

time: 1550 us -> 690 us (0.45)
  waiting for transfers between devices: 937 us -> 274 us
  matrix products: 284 us -> 10.9 us
  Pallas kernels: 0 us -> 222 us
  blocking collectives: 78.7 us -> 0 us
  other arithmetic: 111 us -> 45 us
  starting transfers between devices: 19.1 us -> 79.3 us
  local copies, waits for them, and re-layouts: 87.5 us -> 35.9 us
    reduce_scatter x19 -> x4, waiting for transfers between devices: 700 us -> 107 us  [the longest x2 70.7 us: attend_grads(): lax.psum_scatter(in_grad.astype(BF), 'dp', scatter_dimension=0, tiled=True)]
    dot_general x77 -> x8, matrix products: 284 us -> 10.9 us  [tn(): lax.dot_general(a, b, (((0,), (0,)), ((), ())), preferred_element_type=F32)]
    all_gather x12 -> x4, waiting for transfers between devices: 233 us -> 0.08 us  [over_groups(): return lax.all_gather(x, 'dp', axis=0, tiled=True)]
    pallas_call x0 -> x18, Pallas kernels: none -> 222 us  [the longest x1 82.6 us: mlp_grads(): pl.pallas_call(mlp_grads_kernel, grid=(units // WIDE, rows // CHUNK), in_...]
    ppermute x4 -> x77, waiting for transfers between devices: 3.85 us -> 166 us  [the longest x24 79.1 us: scatter_rows(): lax.ppermute(part, 'tensor', pairs)]
    unnamed x1 -> x0, blocking collectives: 78.7 us -> none
    ppermute x4 -> x77, starting transfers between devices: 7.7 us -> 78 us  [the longest x24 33 us: gather_rows(): return [x] + [lax.ppermute(x, 'tensor', pairs) for pairs in partners(size)]]
    dynamic_slice x29 -> x3, local copies, waits for them, and re-layouts: 35.1 us -> 1.83 us  [the longest x1 1.24 us: local(): length = lax.dynamic_index_in_dim(lengths[:, 0], sec, 0, keepdims=False)]
  transfers between devices with their start and end apart: 35 -> 85, of which waited for: 28 -> 52; matrix products, arithmetic and copies ran while one was open for 15% -> 11% of each run, Pallas kernels for 0% -> 18%
where the time goes in v1:
time: 690 us; the launch traced here: 682 us
  waiting for transfers between devices  274 us (40%)
  Pallas kernels  222 us (32%)
  starting transfers between devices  79.3 us (11%)
  other arithmetic  45 us (7%)
  local copies, waits for them, and re-layouts  35.9 us (5%)
  between operations  15 us (2%)
  matrix products  10.9 us (2%)
    pallas_call x1, Pallas kernels, mlp_grads(): pl.pallas_call(mlp_grads_kernel, grid=(units // WIDE, rows // CHUNK), in_...  82.6 us
    ppermute x24, waiting for transfers between devices, scatter_rows(): lax.ppermute(part, 'tensor', pairs)  79.1 us
    reduce_scatter x2, waiting for transfers between devices, attend_grads(): lax.psum_scatter(in_grad.astype(BF), 'dp', scatter_dimension=0, tiled=True)  70.7 us
    ppermute x24, waiting for transfers between devices, gather_rows(): return [x] + [lax.ppermute(x, 'tensor', pairs) for pairs in partners(size)]  62.5 us
    pallas_call x2, Pallas kernels, mlp_bwd(): pl.pallas_call(functools.partial(mlp_bwd_kernel, layer), grid_spec=pltpu....  40.1 us
    reduce_scatter x2, waiting for transfers between devices, attend_grads(): lax.psum_scatter(out_grad.astype(BF), 'dp', scatter_dimension=1, tiled=True)  36.4 us
    pallas_call x2, Pallas kernels, mlp_fwd(): pl.pallas_call(functools.partial(mlp_fwd_kernel, layer), grid_spec=pltpu....  34.3 us
    ppermute x24, starting transfers between devices, gather_rows(): return [x] + [lax.ppermute(x, 'tensor', pairs) for pairs in partners(size)]  33 us
  transfers between devices with their start and end apart: 85, of which 52 were waited for; matrix products, arithmetic and copies ran while one was open for 11% of the time, Pallas kernels for 18%

profile of v1, /device:TPU:0, one launch (start us, length us, event | category | flops | bytes accessed | tf_op | source)
XLA Modules:
  0.0 681.9 jit_solution(5579373630955553433)
XLA Ops:
  9.9 10.7 %collective-permute-done = f32[2,2048]{1,0:T(2,128)S(1)} collective-permute-done((f32[2,2048]{1,0:T(2,128)S(1)}, f32[2,2048]{1,0:T(2,128)S(1)}, u32[]{:S(2)}, u32[]{:S(2)}) %collective-permute-start) | collective-permute-done | bytes 16416 | tf_op jit(solution)/shard_map/ppermute | solution.py:55
  28.1 5.3 collective-permute-done.1.x1
  36.1 6.2 collective-permute-done.3.x3
  54.0 9.1 %shard_map.204 = (bf16[64,2048]{1,0:T(8,128)(2,1)}, bf16[64,2048]{1,0:T(8,128)(2,1)}, bf16[64,2048]{1,0:T(8,128)(2,1)}, bf16[64,2048]{1,0:T(8,128)(2,1)}, bf16[2...) custom-call(bf16[64,2048]{1,0:T(8,128)(2,1)} %shard_map.203.x0, ...), custom_call_target="tpu_custom_call" | custom-call | flops 4000000000 | bytes 12000000 | tf_op jit(solution)/shard_map/pallas_call | solution.py:202
  67.6 5.3 collective-permute-done.8.b_ref
  75.6 6.2 collective-permute-done.10.d_ref
  94.1 5.5 collective-permute-done.13.x3
  100.2 16.8 %shard_map.206 = (bf16[64,2048]{1,0:T(8,128)(2,1)}, bf16[64,2048]{1,0:T(8,128)(2,1)}, bf16[64,2048]{1,0:T(8,128)(2,1)}, bf16[64,2048]{1,0:T(8,128)(2,1)}, bf16[2...) custom-call(s32[1]{0:T(128)} %bitcast.11.s_ref, bf16[64,2048]{1,0:T(8,128)(2,1)} %get-tuple-element.95.x0, ...), custom_call_target="tpu_custom_call" | custom-call | flops 6442450944 | bytes 30000000 | tf_op jit(solution)/shard_map/pallas_call | solution.py:377
  121.5 4.4 collective-permute-done.17.b_ref
  143.8 9.2 %shard_map.208 = (bf16[64,2048]{1,0:T(8,128)(2,1)}, bf16[64,2048]{1,0:T(8,128)(2,1)}, bf16[64,2048]{1,0:T(8,128)(2,1)}, bf16[64,2048]{1,0:T(8,128)(2,1)}, bf16[2...) custom-call(bf16[64,2048]{1,0:T(8,128)(2,1)} %get-tuple-element.101., ...), custom_call_target="tpu_custom_call" | custom-call | flops 4000000000 | bytes 12000000 | tf_op jit(solution)/shard_map/pallas_call | solution.py:202
  159.6 4.3 collective-permute-done.24.c_ref
  178.4 17.5 %shard_map.210 = (bf16[64,2048]{1,0:T(8,128)(2,1)}, bf16[64,2048]{1,0:T(8,128)(2,1)}, bf16[64,2048]{1,0:T(8,128)(2,1)}, bf16[64,2048]{1,0:T(8,128)(2,1)}, bf16[2...) custom-call(s32[1]{0:T(128)} %bitcast.11.s_ref, ...), custom_call_target="tpu_custom_call" | custom-call | flops 6442450944 | bytes 30000000 | tf_op jit(solution)/shard_map/pallas_call | solution.py:377
  203.2 4.4 collective-permute-done.34.g2
  208.4 20.4 %shard_map.212 = (bf16[64,2048]{1,0:T(8,128)(2,1)}, bf16[64,2048]{1,0:T(8,128)(2,1)}, bf16[64,2048]{1,0:T(8,128)(2,1)}, bf16[64,2048]{1,0:T(8,128)(2,1)}, bf16[256,2048]{1,0:T(8,128)(2,1)}) custom-call(s32[1]{0:T(128)} %bitcast.11.s_ref, bf16[64,2048]{1,0:T(8,128)(2,1)} %copy-done.3, bf16[64,2048]{1,0:T(8,128)(2,1)} %copy-done.16, ...), custom_call_target="tpu_custom_call" | custom-call | flops 6442450944 | bytes 30000000 | tf_op jit(solution)/shard_map/pallas_call | solution.py:432
  237.5 5.9 collective-permute-done.38.d_ref
  257.2 11.9 %shard_map.214 = (bf16[64,2048]{1,0:T(8,128)(2,1)}, bf16[64,2048]{1,0:T(8,128)(2,1)}, bf16[64,2048]{1,0:T(8,128)(2,1)}, bf16[64,2048]{1,0:T(8,128)(2,1)}, bf16[2...) custom-call(bf16[64,2048]{1,0:T(8,128)(2,1)} %get-tuple-element.119.d0, ...), custom_call_target="tpu_custom_call" | custom-call | flops 5000000000 | bytes 14000000 | tf_op jit(solution)/shard_map/pallas_call | solution.py:294
  272.7 5.1 collective-permute-done.42.b_ref
  277.8 8.2 %collective-permute-done.43.c_ref = bf16[64,2048]{1,0:T(8,128)(2,1)S(1)} collective-permute-done((bf16[64,2048]{1,0:T(8,128)(2,1)}, bf16[64,2048]{1,0:T(8,128)(2,1)S(1)}, u32[]{:S(2)}, u32[]{:S(2)}) %collective-permute-start.43) | collective-permute-done | bytes 262176 | tf_op jit(solution)/shard_map/ppermute | solution.py:50
  300.1 19.7 %shard_map.216 = (bf16[64,2048]{1,0:T(8,128)(2,1)}, bf16[64,2048]{1,0:T(8,128)(2,1)}, bf16[64,2048]{1,0:T(8,128)(2,1)}, bf16[64,2048]{1,0:T(8,128)(2,1)}, bf16[256,2048]{1,0:T(8,128)(2,1)}) custom-call(s32[1]{0:T(128)} %bitcast.11.s_ref, bf16[64,2048]{1,0:T(8,128)(2,1)} %get-tuple-element.128.g0.res_ref, bf16[64,2048]{1,0:T(8,128)(2,1)} %copy-done.14, ...), custom_call_target="tpu_custom_call" | custom-call | flops 6442450944 | bytes 30000000 | tf_op jit(solution)/shard_map/pallas_call | solution.py:432
  324.1 5.7 collective-permute-done.48.b_ref
  329.8 6.8 %collective-permute-done.49.c_ref = bf16[64,2048]{1,0:T(8,128)(2,1)S(1)} collective-permute-done((bf16[64,2048]{1,0:T(8,128)(2,1)}, bf16[64,2048]{1,0:T(8,128)(2,1)S(1)}, u32[]{:S(2)}, u32[]{:S(2)}) %collective-permute-start.49) | collective-permute-done | bytes 262176 | tf_op jit(solution)/shard_map/ppermute | solution.py:50
  354.5 12.0 %shard_map.218 = (bf16[64,2048]{1,0:T(8,128)(2,1)}, bf16[64,2048]{1,0:T(8,128)(2,1)}, bf16[64,2048]{1,0:T(8,128)(2,1)}, bf16[64,2048]{1,0:T(8,128)(2,1)}, bf16[2...) custom-call(bf16[64,2048]{1,0:T(8,128)(2,1)} %get-tuple-element.135.d0, ...), custom_call_target="tpu_custom_call" | custom-call | flops 5000000000 | bytes 14000000 | tf_op jit(solution)/shard_map/pallas_call | solution.py:294
  399.9 6.2 collective-permute-done.30.c_ref
  441.7 5.8 broadcast_select_fusion.3
  447.6 6.0 broadcast_select_fusion.1
  460.9 8.4 %reduce-scatter.11.cloned.1.call-done = bf16[256,512]{1,0:T(8,128)(2,1)} async-done(((bf16[256,2048]{1,0:T(8,128)(2,1)}), bf16[256,512]{1,0:T(8,128)(2,1)}) %reduce-scatter.11.cloned.1.call-update) | async-done | bytes 262160 | tf_op jit(solution)/shard_map/reduce_scatter | solution.py:552
  469.3 28.1 %reduce-scatter.9.cloned.1.call-done = bf16[256,512]{1,0:T(8,128)(2,1)} async-done(((bf16[256,2048]{1,0:T(8,128)(2,1)}), bf16[256,512]{1,0:T(8,128)(2,1)}) %reduce-scatter.9.cloned.1.call-update) | async-done | bytes 262160 | tf_op jit(solution)/shard_map/reduce_scatter | solution.py:552
  499.5 34.1 %reduce-scatter.7.cloned.1.call-done = bf16[256,768]{1,0:T(8,128)(2,1)} async-done(((bf16[1024,768]{1,0:T(8,128)(2,1)}), bf16[256,768]{1,0:T(8,128)(2,1)}) %reduce-scatter.7.cloned.1.call-update) | async-done | bytes 393232 | tf_op jit(solution)/shard_map/reduce_scatter | solution.py:551
  533.6 36.6 %reduce-scatter.5.cloned.1.call-done = bf16[256,768]{1,0:T(8,128)(2,1)} async-done(((bf16[1024,768]{1,0:T(8,128)(2,1)}), bf16[256,768]{1,0:T(8,128)(2,1)}) %reduce-scatter.5.cloned.1.call-update) | async-done | bytes 393232 | tf_op jit(solution)/shard_map/reduce_scatter | solution.py:551
  575.3 8.5 %pad_maximum_fusion.x_ref = bf16[2048,2048]{1,0:T(8,128)(2,1)} fusion(bf16[1024,2048]{1,0:T(8,128)(2,1)} %collective-permute-done.75, bf16[1024,2048]{1,0:T(8,128)(2,1)} %get-tuple-element.173), kind=kLoop, calls=%fused_computation | loop fusion | flops 16777216 | bytes 16777216 | tf_op jit(solution)/shard_map/concatenate | solution.py:617
  583.8 8.4 %pad_maximum_fusion.1.g_ref = bf16[2048,2048]{1,0:T(8,128)(2,1)} fusion(bf16[1024,2048]{1,0:T(8,128)(2,1)} %collective-permute-done.76, bf16[1024,2048]{1,0:T(8,128)(2,1)} %get-tuple-element.171), kind=kLoop, calls=%fused_computation.1 | loop fusion | flops 16777216 | bytes 16777216 | tf_op jit(solution)/shard_map/concatenate | solution.py:618
  592.2 82.6 %shard_map.220 = (f32[512,2048]{1,0:T(8,128)}, f32[512,2048]{1,0:T(8,128)}, f32[2048,512]{1,0:T(8,128)}) custom-call(bf16[2048,2048]{1,0:T(8,128)(2,1)} %pad_maximum_fusion.x_ref, bf16[2048,2048]{1,0:T(8,128)(2,1)} %pad_maximum_fusion.1.g_ref, bf16[2048,2048]{1,0:T(8,128)(2,1)} %bitcast.91, bf16[2048,2048]{1,0:T(8,128)(2,1)} %bitcast.97, ...), custom_call_target="tpu_custom_call" | custom-call | flops 64424509440 | bytes 100000000 | tf_op jit(solution)/shard_map/pallas_call | solution.py:483
  (367 shorter events, 241.3 us)
Async XLA Ops:
  7.2 434.4 %all-gather.5.cloned.1.call-start = ((), (), s32[]{:S(2)}) async-start(), calls=%async_computation.8 | async-start | bytes 5242880 | tf_op jit(solution)/shard_map/all_gather | solution.py:579
  7.2 92.3 %collective-permute-start.14 = (bf16[2048,2048]{1,0:T(8,128)(2,1)}, bf16[2048,2048]{1,0:T(8,128)(2,1)}, u32[]{:S(2)}, u32[]{:S(2)}) collective-permute-start(bf16[2048,2048]{1,0:T(8,128)(2,1)} %bitcast.86), channel_id=1, source_target_pairs={{0,16},{16,0},{1,17},{17,1},{2,18},{18,2},{3,19},{19,3},{4,20},{20... | collective-permute-start | bytes 25165832 | tf_op jit(solution)/shard_map/ppermute | solution.py:55
  7.8 91.8 %collective-permute-start.15 = (bf16[2048,2048]{1,0:T(8,128)(2,1)}, bf16[2048,2048]{1,0:T(8,128)(2,1)}, u32[]{:S(2)}, u32[]{:S(2)}) collective-permute-start(bf16[2048,2048]{1,0:T(8,128)(2,1)} %bitcast.92), channel_id=1, source_target_pairs={{0,16},{16,0},{1,17},{17,1},{2,18},{18,2},{3,19},{19,3},{4,20},{20... | collective-permute-start | bytes 25165832 | tf_op jit(solution)/shard_map/ppermute | solution.py:55
  7.8 91.7 %collective-permute-start.16 = (bf16[2048,2048]{1,0:T(8,128)(2,1)}, bf16[2048,2048]{1,0:T(8,128)(2,1)}, u32[]{:S(2)}, u32[]{:S(2)}) collective-permute-start(bf16[2048,2048]{1,0:T(8,128)(2,1)} %bitcast.98), channel_id=1, source_target_pairs={{0,16},{16,0},{1,17},{17,1},{2,18},{18,2},{3,19},{19,3},{4,20},{20... | collective-permute-start | bytes 25165832 | tf_op jit(solution)/shard_map/ppermute | solution.py:55
  9.0 11.6 %collective-permute-start = (f32[2,2048]{1,0:T(2,128)S(1)}, f32[2,2048]{1,0:T(2,128)S(1)}, u32[]{:S(2)}, u32[]{:S(2)}) collective-permute-start(f32[2,2048]{1,0:T(2,128)S(1)} %pad_maximum_fusion.4), channel_id=1, source_target_pairs={{0,16},{16,0},{1,17},{17,1},{2,18},{18,2},{3,19},{19,3},{4,20},{20... | collective-permute-start | bytes 49160 | tf_op jit(solution)/shard_map/ppermute | solution.py:55
  117.1 324.6 %all-gather.7.cloned.1.call-start = ((), (), s32[]{:S(2)}) async-start(), calls=%async_computation.9 | async-start | bytes 5242880 | tf_op jit(solution)/shard_map/all_gather | solution.py:579
  195.9 251.7 %all-gather.11.cloned.1.call-start = ((), (), s32[]{:S(2)}) async-start(), calls=%async_computation.11 | async-start | bytes 5242880 | tf_op jit(solution)/shard_map/all_gather | solution.py:579
  228.8 218.9 %all-gather.9.cloned.1.call-start = ((), (), s32[]{:S(2)}) async-start(), calls=%async_computation.10 | async-start | bytes 5242880 | tf_op jit(solution)/shard_map/all_gather | solution.py:579
  231.3 12.1 %collective-permute-start.38 = (bf16[64,2048]{1,0:T(8,128)(2,1)}, bf16[64,2048]{1,0:T(8,128)(2,1)S(1)}, u32[]{:S(2)}, u32[]{:S(2)}) collective-permute-start(bf16[64,2048]{1,0:T(8,128)(2,1)} %get-tuple-element.118), channel_id=1, source_target_pairs={{0,3},{1,2},{2,1},{3,0},{4,7},{5,6},{6,5},{7,4},{8,11},{9,10},{10,... | collective-permute-start | bytes 786440 | tf_op jit(solution)/shard_map/ppermute | solution.py:50
  271.2 14.8 %collective-permute-start.43 = (bf16[64,2048]{1,0:T(8,128)(2,1)}, bf16[64,2048]{1,0:T(8,128)(2,1)S(1)}, u32[]{:S(2)}, u32[]{:S(2)}) collective-permute-start(bf16[64,2048]{1,0:T(8,128)(2,1)} %get-tuple-element.125), channel_id=1, source_target_pairs={{0,2},{1,3},{2,0},{3,1},{4,6},{5,7},{6,4},{7,5},{8,10},{9,11},{10,... | collective-permute-start | bytes 786440 | tf_op jit(solution)/shard_map/ppermute | solution.py:50
  271.2 14.8 %collective-permute-start.44 = (bf16[64,2048]{1,0:T(8,128)(2,1)}, bf16[64,2048]{1,0:T(8,128)(2,1)S(1)}, u32[]{:S(2)}, u32[]{:S(2)}) collective-permute-start(bf16[64,2048]{1,0:T(8,128)(2,1)} %get-tuple-element.126), channel_id=1, source_target_pairs={{0,3},{1,2},{2,1},{3,0},{4,7},{5,6},{6,5},{7,4},{8,11},{9,10},{10,... | collective-permute-start | bytes 786440 | tf_op jit(solution)/shard_map/ppermute | solution.py:50
  319.8 149.5 %reduce-scatter.11.cloned.1.call-start = ((), (), s32[]{:S(2)}) async-start(), calls=%async_computation.7 | async-start | bytes 1310720 | tf_op jit(solution)/shard_map/reduce_scatter | solution.py:552
  320.3 23.4 %collective-permute-start.73 = (bf16[256,2048]{1,0:T(8,128)(2,1)S(1)}, bf16[256,2048]{1,0:T(8,128)(2,1)S(1)}, u32[]{:S(2)}, u32[]{:S(2)}) collective-permute-start(bf16[256,2048]{1,0:T(8,128)(2,1)S(1)} %copy-done.8), channel_id=1, source_target_pairs={{0,16},{16,0},{1,17},{17,1},{2,18},{18,2},{3,19},{19,3},{4,20},{20... | collective-permute-start | bytes 3145736 | tf_op jit(solution)/shard_map/ppermute | solution.py:55
  322.4 14.2 %collective-permute-start.49 = (bf16[64,2048]{1,0:T(8,128)(2,1)}, bf16[64,2048]{1,0:T(8,128)(2,1)S(1)}, u32[]{:S(2)}, u32[]{:S(2)}) collective-permute-start(bf16[64,2048]{1,0:T(8,128)(2,1)} %get-tuple-element.133), channel_id=1, source_target_pairs={{0,2},{1,3},{2,0},{3,1},{4,6},{5,7},{6,4},{7,5},{8,10},{9,11},{10,... | collective-permute-start | bytes 786440 | tf_op jit(solution)/shard_map/ppermute | solution.py:50
  322.5 14.2 %collective-permute-start.50 = (bf16[64,2048]{1,0:T(8,128)(2,1)}, bf16[64,2048]{1,0:T(8,128)(2,1)S(1)}, u32[]{:S(2)}, u32[]{:S(2)}) collective-permute-start(bf16[64,2048]{1,0:T(8,128)(2,1)} %get-tuple-element.134), channel_id=1, source_target_pairs={{0,3},{1,2},{2,1},{3,0},{4,7},{5,6},{6,5},{7,4},{8,11},{9,10},{10,... | collective-permute-start | bytes 786440 | tf_op jit(solution)/shard_map/ppermute | solution.py:50
  324.0 19.7 %collective-permute-start.72 = (bf16[256,256]{1,0:T(8,128)(2,1)S(1)}, bf16[256,256]{1,0:T(8,128)(2,1)S(1)}, u32[]{:S(2)}, u32[]{:S(2)}) collective-permute-start(bf16[256,256]{1,0:T(8,128)(2,1)S(1)} %broadcast_select_fusion.18), channel_id=1, source_target_pairs={{0,16},{16,0},{1,17},{17,1},{2,18},{18,2},{3,19},{19,3},{4,20},{20... | collective-permute-start | bytes 393224 | tf_op jit(solution)/shard_map/ppermute | solution.py:55
  340.5 13.2 %collective-permute-start.52 = (bf16[64,2048]{1,0:T(8,128)(2,1)}, bf16[64,2048]{1,0:T(8,128)(2,1)S(1)}, u32[]{:S(2)}, u32[]{:S(2)}) collective-permute-start(bf16[64,2048]{1,0:T(8,128)(2,1)} %get-tuple-element.135.d0), channel_id=1, source_target_pairs={{0,2},{1,3},{2,0},{3,1},{4,6},{5,7},{6,4},{7,5},{8,10},{9,11},{10,... | collective-permute-start | bytes 786440 | tf_op jit(solution)/shard_map/ppermute | solution.py:45
  341.9 11.9 %collective-permute-start.53 = (bf16[64,2048]{1,0:T(8,128)(2,1)}, bf16[64,2048]{1,0:T(8,128)(2,1)S(1)}, u32[]{:S(2)}, u32[]{:S(2)}) collective-permute-start(bf16[64,2048]{1,0:T(8,128)(2,1)} %get-tuple-element.135.d0), channel_id=1, source_target_pairs={{0,3},{1,2},{2,1},{3,0},{4,7},{5,6},{6,5},{7,4},{8,11},{9,10},{10,... | collective-permute-start | bytes 786440 | tf_op jit(solution)/shard_map/ppermute | solution.py:45
  345.6 151.7 %reduce-scatter.9.cloned.1.call-start = ((), (), s32[]{:S(2)}) async-start(), calls=%async_computation.6 | async-start | bytes 1310720 | tf_op jit(solution)/shard_map/reduce_scatter | solution.py:552
  373.1 160.6 %reduce-scatter.7.cloned.1.call-start = ((), (), s32[]{:S(2)}) async-start(), calls=%async_computation.5 | async-start | bytes 1966080 | tf_op jit(solution)/shard_map/reduce_scatter | solution.py:551
  379.7 14.2 %collective-permute-start.67 = (bf16[256,1024]{0,1:T(8,128)(2,1)}, bf16[256,1024]{0,1:T(8,128)(2,1)S(1)}, u32[]{:S(2)}, u32[]{:S(2)}) collective-permute-start(bf16[256,1024]{0,1:T(8,128)(2,1)} %bitcast.33), channel_id=1, source_target_pairs={{0,16},{16,0},{1,17},{17,1},{2,18},{18,2},{3,19},{19,3},{4,20},{20... | collective-permute-start | bytes 1572872 | tf_op jit(solution)/shard_map/ppermute | solution.py:55
  392.1 14.0 %collective-permute-start.30 = (bf16[64,2048]{1,0:T(8,128)(2,1)}, bf16[64,2048]{1,0:T(8,128)(2,1)}, u32[]{:S(2)}, u32[]{:S(2)}) collective-permute-start(bf16[64,2048]{1,0:T(8,128)(2,1)} %get-tuple-element.110), channel_id=1, source_target_pairs={{0,2},{1,3},{2,0},{3,1},{4,6},{5,7},{6,4},{7,5},{8,10},{9,11},{10,... | collective-permute-start | bytes 786440 | tf_op jit(solution)/shard_map/ppermute | solution.py:50
  392.5 13.6 %collective-permute-start.31 = (bf16[64,2048]{1,0:T(8,128)(2,1)}, bf16[64,2048]{1,0:T(8,128)(2,1)}, u32[]{:S(2)}, u32[]{:S(2)}) collective-permute-start(bf16[64,2048]{1,0:T(8,128)(2,1)} %get-tuple-element.111), channel_id=1, source_target_pairs={{0,3},{1,2},{2,1},{3,0},{4,7},{5,6},{6,5},{7,4},{8,11},{9,10},{10,... | collective-permute-start | bytes 786440 | tf_op jit(solution)/shard_map/ppermute | solution.py:50
  397.3 173.0 %reduce-scatter.5.cloned.1.call-start = ((), (), s32[]{:S(2)}) async-start(), calls=%async_computation.4 | async-start | bytes 1966080 | tf_op jit(solution)/shard_map/reduce_scatter | solution.py:551
  397.4 41.8 %collective-permute-start.65 = (bf16[256,1024]{0,1:T(8,128)(2,1)S(1)}, bf16[256,1024]{0,1:T(8,128)(2,1)S(1)}, u32[]{:S(2)}, u32[]{:S(2)}) collective-permute-start(bf16[256,1024]{0,1:T(8,128)(2,1)S(1)} %bitcast.106), channel_id=1, source_target_pairs={{0,16},{16,0},{1,17},{17,1},{2,18},{18,2},{3,19},{19,3},{4,20},{20... | collective-permute-start | bytes 1572872 | tf_op jit(solution)/shard_map/ppermute | solution.py:55
  408.8 12.9 %collective-permute-start.55 = (bf16[64,2048]{1,0:T(8,128)(2,1)}, bf16[64,2048]{1,0:T(8,128)(2,1)S(1)}, u32[]{:S(2)}, u32[]{:S(2)}) collective-permute-start(bf16[64,2048]{1,0:T(8,128)(2,1)} %get-tuple-element.141), channel_id=1, source_target_pairs={{0,2},{1,3},{2,0},{3,1},{4,6},{5,7},{6,4},{7,5},{8,10},{9,11},{10,... | collective-permute-start | bytes 786440 | tf_op jit(solution)/shard_map/ppermute | solution.py:50
  413.6 17.6 %collective-permute-start.32 = (bf16[64,2048]{1,0:T(8,128)(2,1)}, bf16[64,2048]{1,0:T(8,128)(2,1)S(1)}, u32[]{:S(2)}, u32[]{:S(2)}) collective-permute-start(bf16[64,2048]{1,0:T(8,128)(2,1)} %broadcast_select_fusion.16), channel_id=1, source_target_pairs={{0,16},{16,0},{1,17},{17,1},{2,18},{18,2},{3,19},{19,3},{4,20},{20... | collective-permute-start | bytes 786440 | tf_op jit(solution)/shard_map/ppermute | solution.py:55
  426.2 13.1 %collective-permute-start.66 = (bf16[256,768]{1,0:T(8,128)(2,1)S(1)}, bf16[256,768]{1,0:T(8,128)(2,1)S(1)}, u32[]{:S(2)}, u32[]{:S(2)}) collective-permute-start(bf16[256,768]{1,0:T(8,128)(2,1)S(1)} %constant_dynamic-update-slice_fusion), channel_id=1, source_target_pairs={{0,16},{16,0},{1,17},{17,1},{2,18},{18,2},{3,19},{19,3},{4,20},{20... | collective-permute-start | bytes 1179656 | tf_op jit(solution)/shard_map/ppermute | solution.py:55
  435.4 18.9 %collective-permute-start.64 = (f32[2,128]{1,0:T(2,128)}, f32[2,128]{1,0:T(2,128)S(1)}, u32[]{:S(2)}, u32[]{:S(2)}) collective-permute-start(f32[2,128]{1,0:T(2,128)} %bitcast.29), channel_id=1, source_target_pairs={{0,12},{4,0},{8,4},{12,8},{1,13},{5,1},{9,5},{13,9},{2,14},{6,2},{... | collective-permute-start | bytes 3080 | tf_op jit(solution)/shard_map/ppermute | solution.py:534
  447.5 127.8 %collective-permute-start.75 = (bf16[1024,2048]{1,0:T(8,128)(2,1)}, bf16[1024,2048]{1,0:T(8,128)(2,1)}, u32[]{:S(2)}, u32[]{:S(2)}) collective-permute-start(bf16[1024,2048]{1,0:T(8,128)(2,1)} %get-tuple-element.174), channel_id=1, source_target_pairs={{0,16},{16,0},{1,17},{17,1},{2,18},{18,2},{3,19},{19,3},{4,20},{20... | collective-permute-start | bytes 12582920 | tf_op jit(solution)/shard_map/ppermute | solution.py:55
  453.6 130.2 %collective-permute-start.76 = (bf16[1024,2048]{1,0:T(8,128)(2,1)}, bf16[1024,2048]{1,0:T(8,128)(2,1)}, u32[]{:S(2)}, u32[]{:S(2)}) collective-permute-start(bf16[1024,2048]{1,0:T(8,128)(2,1)} %get-tuple-element.172), channel_id=1, source_target_pairs={{0,16},{16,0},{1,17},{17,1},{2,18},{18,2},{3,19},{19,3},{4,20},{20... | collective-permute-start | bytes 12582920 | tf_op jit(solution)/shard_map/ppermute | solution.py:55
  498.4 73.0 %collective-permute-start.74 = (bf16[256,512]{1,0:T(8,128)(2,1)S(1)}, bf16[256,512]{1,0:T(8,128)(2,1)S(1)}, u32[]{:S(2)}, u32[]{:S(2)}) collective-permute-start(bf16[256,512]{1,0:T(8,128)(2,1)S(1)} %broadcast_select_fusion.12), channel_id=1, source_target_pairs={{0,16},{16,0},{1,17},{17,1},{2,18},{18,2},{3,19},{19,3},{4,20},{20... | collective-permute-start | bytes 786440 | tf_op jit(solution)/shard_map/ppermute | solution.py:55
  (119 other events, 1090.5 us)
Sparse Core Ops, SparseCore 0:
  117.2 81.5 all-gather.4
  200.4 79.2 all-gather.6
  281.3 79.2 all-gather.10
  362.1 79.2 all-gather.8
  443.5 25.7 reduce-scatter.10
  471.5 25.7 reduce-scatter.8
  499.7 33.9 reduce-scatter.6
  535.9 34.2 reduce-scatter.4

commit v2 on v1

v2 whole, which is shorter than its diff:
```python
import functools

import jax
import jax.numpy as jnp
from jax import lax
from jax.experimental import pallas as pl
from jax.experimental.pallas import tpu as pltpu
from jax.sharding import PartitionSpec as P

HD = 64
EPSILON = 1e-05
NEGATIVE = -1e30
BF = jnp.bfloat16
F32 = jnp.float32
VMEM = pl.BlockSpec(memory_space=pltpu.VMEM)
HBM = pl.BlockSpec(memory_space=pltpu.HBM)
ANY = pl.BlockSpec(memory_space=pl.ANY)
MIB = 1024 * 1024
SHRINK = 50


def nn(a, b):
    return jnp.dot(a, b, preferred_element_type=F32)


def nt(a, b):
    return lax.dot_general(a, b, (((1,), (1,)), ((), ())), preferred_element_type=F32)


def tn(a, b):
    return lax.dot_general(a, b, (((0,), (0,)), ((), ())), preferred_element_type=F32)


def shaped(shape, dtype):
    return jax.ShapeDtypeStruct(shape, dtype)


def far(shape, dtype=BF):
    return pltpu.HBM(shape, dtype)


def in_hbm(*arrays):
    return [pltpu.with_memory_space_constraint(a, pltpu.HBM) for a in arrays]


def tied(first, *others):
    return lax.optimization_barrier((first, *others))[0]


def cost(flops, nbytes):
    return pl.CostEstimate(flops=int(flops / SHRINK), bytes_accessed=int(nbytes / SHRINK), transcendentals=0)


def partners(size):
    return [[(a, a ^ k) for a in range(size)] for k in range(1, size)]


def gather_rows(x, size):
    return [x] + [lax.ppermute(x, "tensor", pairs) for pairs in partners(size)]


def scatter_rows(parts, size):
    return [parts[0]] + [
        lax.ppermute(part, "tensor", pairs) for part, pairs in zip(parts[1:], partners(size))
    ]


def swapped(x):
    return lax.ppermute(x, "section", [(0, 1), (1, 0)])


def norm_kernel(x_ref, gain_ref, out_ref):
    x = x_ref[...].astype(F32)
    scale = lax.rsqrt(jnp.mean(x * x, axis=-1, keepdims=True) + EPSILON)
    out_ref[...] = (x * scale * gain_ref[...]).astype(BF)


def norm_rows(x, gain):
    return pl.pallas_call(
        norm_kernel, name="norm", cost_estimate=cost(0, 1e6), out_shape=shaped(x.shape, BF), in_specs=[VMEM] * 2, out_specs=VMEM
    )(x, gain)


def add_norm_kernel(round_out, base_ref, a_ref, b_ref, c_ref, d_ref, gain_ref, out_ref, normed_ref):
    x = base_ref[...].astype(F32) + (
        (a_ref[...].astype(F32) + b_ref[...].astype(F32))
        + (c_ref[...].astype(F32) + d_ref[...].astype(F32))
    )
    if round_out:
        x = x.astype(BF)
        out_ref[...] = x
        x = x.astype(F32)
    else:
        out_ref[...] = x
    scale = lax.rsqrt(jnp.mean(x * x, axis=-1, keepdims=True) + EPSILON)
    normed_ref[...] = (x * scale * gain_ref[...]).astype(BF)


def add_norm(base, terms, gain, round_out):
    return pl.pallas_call(
        functools.partial(add_norm_kernel, round_out),
        name="add_norm",
        cost_estimate=cost(0, 2e6),
        out_shape=(shaped(base.shape, BF if round_out else F32), shaped(base.shape, BF)),
        in_specs=[VMEM] * 6,
        out_specs=(VMEM, VMEM),
    )(base, *terms, gain)


def norm_back_kernel(base_ref, a_ref, b_ref, c_ref, d_ref, gain_ref, res_ref, out_ref, low_ref, gp_ref):
    g = (a_ref[...].astype(F32) + b_ref[...].astype(F32)) + (
        c_ref[...].astype(F32) + d_ref[...].astype(F32)
    )
    x = base_ref[...].astype(F32)
    scale = lax.rsqrt(jnp.mean(x * x, axis=-1, keepdims=True) + EPSILON)
    y = x * scale
    gp_ref[...] = jnp.sum(g * y, axis=0, keepdims=True)
    e = g * gain_ref[...]
    out = res_ref[...].astype(F32) + scale * (e - y * jnp.mean(e * y, axis=-1, keepdims=True))
    out_ref[...] = out
    low_ref[...] = out.astype(BF)


def norm_back(base, terms, gain, residual):
    return pl.pallas_call(
        norm_back_kernel,
        name="norm_back",
        cost_estimate=cost(0, 3e6),
        out_shape=(shaped(base.shape, F32), shaped(base.shape, BF), shaped((1, base.shape[1]), F32)),
        in_specs=[VMEM] * 7,
        out_specs=(VMEM,) * 3,
    )(base, *terms, gain, residual)


def prefetch_kernel(layer, cuts, after_ref, *refs):
    sources, refs = refs[: 2 * len(cuts)], refs[2 * len(cuts) :]
    total = sum(len(cut) - 1 for cut in cuts)
    buffers, token, sems = refs[:total], refs[total], refs[-1]
    token[...] = jnp.zeros_like(token)
    mine = lax.axis_index("section") == layer

    def copies(side):
        moves = []
        for source, cut in zip(sources[side::2], cuts):
            for at, to in zip(cut, cut[1:]):
                n = len(moves)
                part = source.at[pl.ds(at, to - at), :]
                moves.append(pltpu.make_async_copy(part, buffers[n], sems.at[n]))
        return moves

    @pl.when(mine)
    def _():
        for copy in copies(0):
            copy.start()

    @pl.when(jnp.logical_not(mine))
    def _():
        for copy in copies(1):
            copy.start()

    for copy in copies(0):
        copy.wait()


def prefetch(layer, pairs, cuts, after):
    shapes = [
        (to - at, own.shape[1]) for (own, _), cut in zip(pairs, cuts) for at, to in zip(cut, cut[1:])
    ]
    return pl.pallas_call(
        functools.partial(prefetch_kernel, layer, cuts),
        out_shape=[pltpu.VMEM(shape, BF) for shape in shapes] + [shaped((8, 128), F32)],
        in_specs=[ANY] + [HBM] * (2 * len(pairs)),
        out_specs=[VMEM] * (len(shapes) + 1),
        scratch_shapes=[pltpu.SemaphoreType.DMA((len(shapes),))],
        compiler_params=pltpu.CompilerParams(vmem_limit_bytes=MIB),
        cost_estimate=cost(0, sum(4 * a * b for a, b in shapes)),
        name="prefetch",
    )(after, *in_hbm(*[w for pair in pairs for w in pair]))


def turn(x, cos, sin, low):
    return x * cos + jnp.where(low, pltpu.roll(x, 96, 1), pltpu.roll(x, 32, 1)) * sin


def spread(x, first_lanes):
    x = x.astype(F32)
    moved = pltpu.roll(x, 64, 1)
    zero = jnp.zeros_like(x)
    return [
        (jnp.where(first_lanes, x, zero).astype(BF), jnp.where(first_lanes, zero, moved).astype(BF)),
        (jnp.where(first_lanes, moved, zero).astype(BF), jnp.where(first_lanes, zero, x).astype(BF)),
    ]


def soft(q, k, mask):
    scores = jnp.where(mask, nt(q, k) * HD**-0.5, NEGATIVE)
    lifted = jnp.exp(scores - jnp.max(scores, axis=-1, keepdims=True))
    return lifted * (1.0 / jnp.sum(lifted, axis=-1, keepdims=True))


class Rows:
    def __init__(self, blocks, buffer, sems, *kept):
        rows = blocks[0].shape[0]
        self.come = [
            pltpu.make_async_copy(b, buffer.at[pl.ds(n * rows, rows), :], sems.at[n])
            for n, b in enumerate(blocks)
        ]
        self.go = []
        for ref, order in kept:
            for at, n in enumerate(order):
                source, target = buffer.at[pl.ds(n * rows, rows), :], ref.at[pl.ds(at * rows, rows), :]
                sem = sems.at[len(blocks) + len(self.go)]
                self.go.append(pltpu.make_async_copy(source, target, sem))
        for copy in self.come:
            copy.start()

    def ready(self):
        for copy in self.come:
            copy.wait()
        for copy in self.go:
            copy.start()

    def end(self):
        for copy in self.go:
            copy.wait()


ALL = (0, 1, 2, 3)


COLUMNS = 512


def attend_fwd_kernel(
    x0, x1, x2, x3, w_in, wo, cos_ref, sin_ref, pq_ref, pk_ref,
    p0, p1, p2, p3, x_kept, q_out, k_out, v_out, att_out, x_all, sems,
):
    rows = x0.shape[0]
    held = Rows((x0, x1, x2, x3), x_all, sems, (x_kept, ALL))
    whole = 4 * rows
    lane = lax.broadcasted_iota(jnp.int32, (whole, 128), 1)
    low = (lane & (HD - 1)) < HD // 2
    first_lanes = lane < HD
    cos, sin = cos_ref[...], sin_ref[...]
    mask = pk_ref[...] <= pq_ref[...]
    held.ready()
    x = x_all[...]
    width, narrow = q_out.shape[1], k_out.shape[1]
    k = turn(nn(x, w_in[:, width : width + narrow]), cos, sin, low).astype(BF)
    v = nn(x, w_in[:, width + narrow :]).astype(BF)
    k_out[...] = k
    v_out[...] = v
    keys, values = spread(k, first_lanes), spread(v, first_lanes)
    for p in range(q_out.shape[1] // 128):
        cut = slice(p * 128, (p + 1) * 128)
        q = turn(nn(x, w_in[:, cut]), cos, sin, low).astype(BF)
        q_out[:, cut] = q
        head = p // 2
        att_out[:, cut] = (
            nn(soft(q, keys[head][0], mask).astype(BF), values[head][0])
            + nn(soft(q, keys[head][1], mask).astype(BF), values[head][1])
        ).astype(BF)
    att = att_out[...]
    for c in range(p0.shape[1] // COLUMNS):
        cut = slice(c * COLUMNS, (c + 1) * COLUMNS)
        out = nn(att, wo[:, cut]).astype(BF)
        for n, part in enumerate((p0, p1, p2, p3)):
            part[:, cut] = out[n * rows : (n + 1) * rows, :]
    held.end()


def attend_fwd(blocks, weights, tables):
    rows, depth = blocks[0].shape
    whole, width = 4 * rows, weights[1].shape[0]
    narrow = (weights[0].shape[1] - width) // 2
    block = shaped((rows, depth), BF)
    return pl.pallas_call(
        attend_fwd_kernel,
        out_shape=(block,) * 4
        + (
            far((whole, depth)),
            shaped((whole, width), BF),
            shaped((whole, narrow), BF),
            shaped((whole, narrow), BF),
            shaped((whole, width), BF),
        ),
        in_specs=[HBM] * 4 + [VMEM] * 6,
        out_specs=(VMEM,) * 4 + (HBM,) + (VMEM,) * 4,
        scratch_shapes=[pltpu.VMEM((whole, depth), BF), pltpu.SemaphoreType.DMA((8,))],
        compiler_params=pltpu.CompilerParams(vmem_limit_bytes=12 * MIB),
        cost_estimate=cost(5e9, 12e6),
        name="attend_fwd",
    )(*in_hbm(*blocks), *weights, *tables)


def attend_bwd_kernel(
    d0, d1, d2, d3, q_ref, k_ref, v_ref, w_in, wo, cos_ref, sin_ref, pq_ref, pk_ref,
    p0, p1, p2, p3, dm_kept, d_out, dm_all, sems,
):
    rows = d0.shape[0]
    held = Rows((d0, d1, d2, d3), dm_all, sems, (dm_kept, ALL))
    width, narrow = q_ref.shape[1], k_ref.shape[1]
    whole = 4 * rows
    lane = lax.broadcasted_iota(jnp.int32, (whole, 128), 1)
    low = (lane & (HD - 1)) < HD // 2
    first_lanes = lane < HD
    cos, sin = cos_ref[...], -sin_ref[...]
    mask = pk_ref[...] <= pq_ref[...]
    keys, values = spread(k_ref[...], first_lanes), spread(v_ref[...], first_lanes)
    held.ready()
    dm = dm_all[...]
    dk_sums, dv_sums = [[None, None], [None, None]], [[None, None], [None, None]]

    def add(sums, head, side, term):
        sums[head][side] = term if sums[head][side] is None else sums[head][side] + term

    for p in range(q_ref.shape[1] // 128):
        cut = slice(p * 128, (p + 1) * 128)
        head = p // 2
        q = q_ref[:, cut]
        d_att = nt(dm, wo[cut, :]).astype(BF)
        d_q = None
        for side in range(2):
            probs = soft(q, keys[head][side], mask)
            d_probs = nt(d_att, values[head][side])
            inner = jnp.sum(d_probs * probs, axis=-1, keepdims=True)
            d_raw = (probs * (d_probs - inner) * HD**-0.5).astype(BF)
            term = nn(d_raw, keys[head][side])
            d_q = term if d_q is None else d_q + term
            add(dk_sums, head, side, tn(d_raw, q))
            add(dv_sums, head, side, tn(probs.astype(BF), d_att))
        d_out[:, cut] = turn(d_q, cos, sin, low).astype(BF)

    def folded(sums):
        return jnp.where(
            first_lanes,
            sums[0][0] + pltpu.roll(sums[0][1], 64, 1),
            pltpu.roll(sums[1][0], 64, 1) + sums[1][1],
        )

    dk = turn(folded(dk_sums), cos, sin, low).astype(BF)
    dv = folded(dv_sums).astype(BF)
    d_out[:, width : width + narrow] = dk
    d_out[:, width + narrow :] = dv
    for c in range(p0.shape[1] // COLUMNS):
        cut = slice(c * COLUMNS, (c + 1) * COLUMNS)
        out = nt(d_out[...], w_in[cut, :]).astype(BF)
        for n, part in enumerate((p0, p1, p2, p3)):
            part[:, cut] = out[n * rows : (n + 1) * rows, :]
    held.end()


def attend_bwd(blocks, qkv, weights, tables):
    rows, depth = blocks[0].shape
    whole, width = 4 * rows, weights[1].shape[0]
    narrow = (weights[0].shape[1] - width) // 2
    block = shaped((rows, depth), BF)
    return pl.pallas_call(
        attend_bwd_kernel,
        out_shape=(block,) * 4
        + (far((whole, depth)), shaped((whole, width + 2 * narrow), BF)),
        in_specs=[HBM] * 4 + [VMEM] * 9,
        out_specs=(VMEM,) * 4 + (HBM, VMEM),
        scratch_shapes=[pltpu.VMEM((whole, depth), BF), pltpu.SemaphoreType.DMA((8,))],
        compiler_params=pltpu.CompilerParams(vmem_limit_bytes=14 * MIB),
        cost_estimate=cost(7e9, 14e6),
        name="attend_bwd",
    )(*in_hbm(*blocks), *qkv, *weights, *tables)


TILE = 512


def mlp_fwd_kernel(
    x0, x1, x2, x3, wg, wu, wd, p0, p1, p2, p3, gate_out, up_out, x_kept, x_all, total, sems
):
    rows = x0.shape[0]
    held = Rows((x0, x1, x2, x3), x_all, sems, (x_kept, (0, 2)))
    held.ready()

    def step(f, first):
        cut = slice(0, TILE) if first else pl.ds(pl.multiple_of(f * TILE, TILE), TILE)
        x = x_all[...]
        gate, up = nn(x, wg[:, cut]), nn(x, wu[:, cut])
        gate_out[:, cut] = gate.astype(BF)
        up_out[:, cut] = up.astype(BF)
        term = nn((gate * jax.nn.sigmoid(gate) * up).astype(BF), wd[cut, :])
        total[...] = term if first else total[...] + term

    step(0, True)
    pl.loop(1, wg.shape[1] // TILE)(lambda f: step(f, False))
    for n, part in enumerate((p0, p1, p2, p3)):
        part[...] = total[n * rows : (n + 1) * rows, :].astype(BF)
    held.end()


def mlp_fwd(blocks, weights):
    rows, depth = blocks[0].shape
    units, whole = weights[0].shape[1], 4 * rows
    return pl.pallas_call(
        mlp_fwd_kernel,
        in_specs=[HBM] * 4 + [VMEM] * 3,
        out_specs=[VMEM] * 6 + [HBM],
        scratch_shapes=[
            pltpu.VMEM((whole, depth), BF),
            pltpu.VMEM((whole, depth), F32),
            pltpu.SemaphoreType.DMA((8,)),
        ],
        out_shape=[shaped((rows, depth), BF)] * 4
        + [shaped((whole, units), BF)] * 2
        + [far((whole // 2, depth))],
        compiler_params=pltpu.CompilerParams(vmem_limit_bytes=12 * MIB),
        cost_estimate=cost(6 * whole * units * depth, 30e6),
        name="mlp_fwd",
    )(*in_hbm(*blocks), *weights)


def mlp_bwd_kernel(
    g0, g1, g2, g3, gate_ref, up_ref, wg, wu, wd, p0, p1, p2, p3, g_kept, g_all, total, sems
):
    rows = g0.shape[0]
    held = Rows((g0, g1, g2, g3), g_all, sems, (g_kept, ALL))
    held.ready()

    def step(f, first):
        cut = slice(0, TILE) if first else pl.ds(pl.multiple_of(f * TILE, TILE), TILE)
        d_hidden = nt(g_all[...], wd[cut, :])
        gate, up = gate_ref[:, cut].astype(F32), up_ref[:, cut].astype(F32)
        s = jax.nn.sigmoid(gate)
        d_up = (d_hidden * gate * s).astype(BF)
        d_gate = (d_hidden * up * s * (1.0 + gate * (1.0 - s))).astype(BF)
        term = nt(d_gate, wg[:, cut]) + nt(d_up, wu[:, cut])
        total[...] = term if first else total[...] + term

    step(0, True)
    pl.loop(1, wg.shape[1] // TILE)(lambda f: step(f, False))
    for n, part in enumerate((p0, p1, p2, p3)):
        part[...] = total[n * rows : (n + 1) * rows, :].astype(BF)
    held.end()


def mlp_bwd(blocks, gate, up, weights):
    rows, depth = blocks[0].shape
    units, whole = weights[0].shape[1], 4 * rows
    return pl.pallas_call(
        mlp_bwd_kernel,
        in_specs=[HBM] * 4 + [VMEM] * 5,
        out_specs=[VMEM] * 4 + [HBM],
        scratch_shapes=[
            pltpu.VMEM((whole, depth), BF),
            pltpu.VMEM((whole, depth), F32),
            pltpu.SemaphoreType.DMA((8,)),
        ],
        out_shape=[shaped((rows, depth), BF)] * 4 + [far((whole, depth))],
        compiler_params=pltpu.CompilerParams(vmem_limit_bytes=12 * MIB),
        cost_estimate=cost(6 * whole * units * depth, 30e6),
        name="mlp_bwd",
    )(*in_hbm(*blocks), gate, up, *weights)


def mlp_both_kernel(
    x0, x1, x2, x3, g0, g1, g2, g3, wg, wu, wd,
    p0, p1, p2, p3, r0, r1, r2, r3, x_kept, x_all, g_all, gate_all, up_all, total, x_sems, g_sems,
):
    rows = x0.shape[0]
    held = Rows((x0, x1, x2, x3), x_all, x_sems, (x_kept, ALL))
    held_g = Rows((g0, g1, g2, g3), g_all, g_sems)
    held.ready()

    def tile(f, first):
        return slice(0, TILE) if first else pl.ds(pl.multiple_of(f * TILE, TILE), TILE)

    def forward(f, first):
        cut = tile(f, first)
        x = x_all[...]
        gate, up = nn(x, wg[:, cut]), nn(x, wu[:, cut])
        gate_all[:, cut] = gate.astype(BF)
        up_all[:, cut] = up.astype(BF)
        term = nn((gate * jax.nn.sigmoid(gate) * up).astype(BF), wd[cut, :])
        total[...] = term if first else total[...] + term

    def backward(f, first):
        cut = tile(f, first)
        d_hidden = nt(g_all[...], wd[cut, :])
        gate, up = gate_all[:, cut].astype(F32), up_all[:, cut].astype(F32)
        s = jax.nn.sigmoid(gate)
        d_up = (d_hidden * gate * s).astype(BF)
        d_gate = (d_hidden * up * s * (1.0 + gate * (1.0 - s))).astype(BF)
        term = nt(d_gate, wg[:, cut]) + nt(d_up, wu[:, cut])
        total[...] = term if first else total[...] + term

    for step, parts in ((forward, (p0, p1, p2, p3)), (backward, (r0, r1, r2, r3))):
        step(0, True)
        pl.loop(1, wg.shape[1] // TILE)(lambda f: step(f, False))
        for n, part in enumerate(parts):
            part[...] = total[n * rows : (n + 1) * rows, :].astype(BF)
        if step is forward:
            held_g.ready()
    held.end()


def mlp_both(blocks, g_blocks, weights):
    rows, depth = blocks[0].shape
    units, whole = weights[0].shape[1], 4 * rows
    return pl.pallas_call(
        mlp_both_kernel,
        in_specs=[HBM] * 8 + [VMEM] * 3,
        out_specs=[VMEM] * 8 + [HBM],
        scratch_shapes=[
            pltpu.VMEM((whole, depth), BF),
            pltpu.VMEM((whole, depth), BF),
            pltpu.VMEM((whole, units), BF),
            pltpu.VMEM((whole, units), BF),
            pltpu.VMEM((whole, depth), F32),
            pltpu.SemaphoreType.DMA((8,)),
            pltpu.SemaphoreType.DMA((4,)),
        ],
        out_shape=[shaped((rows, depth), BF)] * 8 + [far((whole, depth))],
        compiler_params=pltpu.CompilerParams(vmem_limit_bytes=14 * MIB),
        cost_estimate=cost(12 * whole * units * depth, 30e6),
        name="mlp_both",
    )(*in_hbm(*blocks, *g_blocks), *weights)


PIECE = 512


def mlp_grads_kernel(layer, f, first, last, x_orders, g_orders, *refs):
    n_x, n_g = len(x_orders), len(g_orders)
    x_refs, g_refs, refs = refs[:n_x], refs[n_x : n_x + n_g], refs[n_x + n_g :]
    *weights, out = refs[:7]
    wg, wu, wd, x_all, g_all, total, w_sems, sems = refs[7:]
    share = out.shape[0]
    units = weights[0].shape[1]
    mine = lax.axis_index("section") == layer
    column = lax.axis_index("section") * (units // 2) + f * PIECE
    cut = pl.ds(pl.multiple_of(column, PIECE), PIECE)
    start = pl.ds(pl.multiple_of(lax.axis_index("dp") * share, share), share)

    def chunk(p, slot):
        moves = []
        for to, arrays, orders in ((x_all, x_refs, x_orders), (g_all, g_refs, g_orders)):
            for a, (half, order) in zip(arrays, orders):
                rows = a.shape[1] // len(order)
                at = p if a.shape[0] > last - first else p - first
                for n, place in enumerate(order):
                    target = to.at[slot, pl.ds((half * 4 + place) * rows, rows), :]
                    source = a.at[at, pl.ds(n * rows, rows), :]
                    moves.append(pltpu.make_async_copy(source, target, sems.at[slot, len(moves)]))
        return moves

    def copies(g, u, d):
        return [
            pltpu.make_async_copy(g.at[:, cut], wg, w_sems.at[0]),
            pltpu.make_async_copy(u.at[:, cut], wu, w_sems.at[1]),
            pltpu.make_async_copy(d.at[cut, :], wd, w_sems.at[2]),
        ]

    @pl.when(mine)
    def _():
        for copy in copies(*weights[0::2]):
            copy.start()

    @pl.when(jnp.logical_not(mine))
    def _():
        for copy in copies(*weights[1::2]):
            copy.start()

    for copy in chunk(first, 0):
        copy.start()
    total[...] = jnp.zeros_like(total)
    for copy in copies(*weights[0::2]):
        copy.wait()

    @pl.loop(first, last)
    def _(p):
        slot = lax.rem(p - first, 2)

        @pl.when(p + 1 < last)
        def _():
            for copy in chunk(p + 1, 1 - slot):
                copy.start()

        for copy in chunk(p, slot):
            copy.wait()
        x = x_all[slot]
        gate, up = nn(x, wg[...]), nn(x, wu[...])
        d_hidden = nt(g_all[slot], wd[...])
        s = jax.nn.sigmoid(gate)
        gated = gate * s
        hidden = (gated * up).astype(BF)
        d_up = (d_hidden * gated).astype(BF)
        d_gate = (d_hidden * up * s * (1.0 + gate * (1.0 - s))).astype(BF)
        x_cut, g_cut = x_all[slot, :, start], g_all[slot, :, start]
        total[:, :PIECE] += tn(x_cut, d_gate)
        total[:, PIECE : 2 * PIECE] += tn(x_cut, d_up)
        total[:, 2 * PIECE :] += tn(g_cut, hidden)

    out[...] = total[...].astype(BF)


def mlp_grads(layer, f, part, xs, gs, pairs):
    groups, _, depth = xs[0][0].shape
    first, last = part * (groups // 2), (part + 1) * (groups // 2)
    rows = sum(a.shape[1] for a, _ in xs)
    share = depth // groups
    return pl.pallas_call(
        functools.partial(
            mlp_grads_kernel, layer, f, first, last, [o for _, o in xs], [o for _, o in gs]
        ),
        in_specs=[HBM] * (len(xs) + len(gs) + 6),
        out_specs=VMEM,
        out_shape=shaped((share, 3 * PIECE), BF),
        scratch_shapes=[
            pltpu.VMEM((depth, PIECE), BF),
            pltpu.VMEM((depth, PIECE), BF),
            pltpu.VMEM((PIECE, depth), BF),
            pltpu.VMEM((2, rows, depth), BF),
            pltpu.VMEM((2, rows, depth), BF),
            pltpu.VMEM((share, 3 * PIECE), F32),
            pltpu.SemaphoreType.DMA((3,)),
            pltpu.SemaphoreType.DMA((2, 16)),
        ],
        compiler_params=pltpu.CompilerParams(vmem_limit_bytes=50 * MIB),
        cost_estimate=cost(3 * rows * groups * PIECE * (depth + share), 20e6),
        name="mlp_grads",
    )(*in_hbm(*[a for a, _ in xs], *[a for a, _ in gs], *[w for pair in pairs for w in pair]))


def assemble_kernel(n, *refs):
    sources, outs, scratch = refs[: 4 * (n + 1)], refs[4 * (n + 1) : 4 * (n + 1) + 7], refs[4 * (n + 1) + 7 :]
    q_out, k_out, v_out, o_out, gate_out, up_out, down_out = outs
    held, attn, in_rows, wide, tall, flat, sems, out_sems = scratch
    sec = lax.axis_index("section")

    def fetches(layer):
        mine = sources[layer * 2 * (n + 1) : (layer + 1) * 2 * (n + 1)]
        moves = []
        for side in range(2):
            for f in range(n + 1):
                source = mine[side * (n + 1) + f]
                target = held.at[side, f] if f < n else attn.at[side]
                moves.append(pltpu.make_async_copy(source, target, sems.at[len(moves)]))
        return moves

    for layer in range(2):

        @pl.when(sec == layer)
        def _(layer=layer):
            for move in fetches(layer):
                move.start()

    for move in fetches(0):
        move.wait()
    share, width = attn.shape[1:]
    columns = in_rows.shape[1] // 2
    half_units = wide.shape[2] // 2
    going = []

    def leave(source, target):
        going.append(pltpu.make_async_copy(source, target, out_sems.at[len(going)]))
        going[-1].start()

    q, k = q_out.shape[1], k_out.shape[1]
    halves = [sec, 1 - sec]
    rest = width - columns
    for side, half in enumerate(halves):
        in_rows[:, pl.ds(pl.multiple_of(half * columns, columns), columns)] = attn[side, :, :columns].astype(F32)
        flat[pl.ds(pl.multiple_of(half * rest, rest), rest), :] = attn[side, :, columns:].astype(F32).T
    leave(flat, o_out)
    leave(in_rows.at[:, pl.ds(0, q)], q_out)
    leave(in_rows.at[:, pl.ds(q, k)], k_out)
    leave(in_rows.at[:, pl.ds(q + k, k)], v_out)
    for kind, (target, out) in enumerate(((wide.at[0], gate_out), (wide.at[1], up_out), (tall, down_out))):
        for side, half in enumerate(halves):
            for f in range(n // 2):
                at = pl.ds(pl.multiple_of(half * half_units + f * PIECE, PIECE), PIECE)
                cut = slice(kind * PIECE, (kind + 1) * PIECE)
                tile = held[side, 2 * f, :, cut].astype(F32) + held[side, 2 * f + 1, :, cut].astype(F32)
                if kind < 2:
                    target[:, at] = tile
                else:
                    target[at, :] = tile.T
        leave(target, out)
    for move in going:
        move.wait()


def assemble(layers, width, narrow, units):
    n = len(layers[0][0])
    share, attn_width = layers[0][1].shape
    depth_out = 2 * attn_width - width - 2 * narrow
    sources = []
    for tiles, part, other_tiles, other_part in layers:
        sources += [*tiles, part, *other_tiles, other_part]
    shapes = [(share, width), (share, narrow), (share, narrow), (depth_out, share)]
    shapes += [(share, units), (share, units), (units, share)]
    return pl.pallas_call(
        functools.partial(assemble_kernel, n),
        in_specs=[HBM] * len(sources),
        out_specs=[HBM] * 7,
        out_shape=[far(shape, F32) for shape in shapes],
        scratch_shapes=[
            pltpu.VMEM((2, n, share, 3 * PIECE), BF),
            pltpu.VMEM((2, share, attn_width), BF),
            pltpu.VMEM((share, width + 2 * narrow), F32),
            pltpu.VMEM((2, share, units), F32),
            pltpu.VMEM((units, share), F32),
            pltpu.VMEM((depth_out, share), F32),
            pltpu.SemaphoreType.DMA((2 * (n + 1),)),
            pltpu.SemaphoreType.DMA((7,)),
        ],
        compiler_params=pltpu.CompilerParams(vmem_limit_bytes=48 * MIB),
        cost_estimate=cost(0, 30e6),
        name="assemble",
    )(*in_hbm(*sources))


def attend_grads_kernel(x_own, x_other, d_own, d_other, m_own, m_other, a_own, a_other, out):
    sec = lax.axis_index("section")
    at = 0
    for left_own, left_other, own, other in (
        (x_own, x_other, d_own, d_other),
        (m_own, m_other, a_own, a_other),
    ):
        width = own.shape[1] // 2
        half = pl.ds(pl.multiple_of(sec * width, width), width)
        out[:, at : at + width] = (tn(left_own[...], own[:, half]) + tn(left_other[...], other[:, half])).astype(BF)
        at += width


def attend_grads(x, d_qkv, d_mid, att):
    depth, width = x.shape[1], (d_qkv.shape[1] + att.shape[1]) // 2
    terms = [x, swapped(x), d_qkv, swapped(d_qkv), d_mid, swapped(d_mid), att, swapped(att)]
    both = pl.pallas_call(
        attend_grads_kernel,
        in_specs=[VMEM] * 8,
        out_specs=VMEM,
        out_shape=shaped((depth, width), BF),
        compiler_params=pltpu.CompilerParams(vmem_limit_bytes=14 * MIB),
        cost_estimate=cost(4 * x.size * width, 6e6),
        name="attend_grads",
    )(*terms)
    return both


def summed_over_groups(x):
    return lax.psum_scatter(x, "dp", scatter_dimension=0, tiled=True)


def rope_tables(places, head_size):
    half_width = head_size // 2
    counter = jnp.arange(half_width, dtype=F32)
    base_freq = 1.0 / 500000.0 ** (2.0 * counter / head_size)
    wavelength = 2.0 * jnp.pi / base_freq
    blend_part = (8192.0 / wavelength - 1.0) / 3.0
    middle = (1.0 - blend_part) * base_freq / 32.0 + blend_part * base_freq
    frequency = jnp.where(
        wavelength < 2048.0, base_freq, jnp.where(wavelength > 8192.0, base_freq / 32.0, middle)
    )
    angles = places.astype(F32)[:, None] * frequency[None, :]
    cosine, sine = jnp.cos(angles), jnp.sin(angles)
    return (
        jnp.concatenate([cosine] * 4, axis=1),
        jnp.concatenate([-sine, sine, -sine, sine], axis=1),
    )


def halved(total, axis, size, bit, dim):
    low, high = lax.slice_in_dim(total, 0, bit, axis=dim), lax.slice_in_dim(total, bit, 2 * bit, axis=dim)
    upper = (lax.axis_index(axis) & bit) != 0
    keep, send = jnp.where(upper, high, low), jnp.where(upper, low, high)
    return keep + lax.ppermute(send, axis, [(a, a ^ bit) for a in range(size)])


def over_groups(x):
    return lax.all_gather(x, "dp", axis=0, tiled=False)


def from_both_cores(*arrays):
    return [(a, (0, places)) for a, places in arrays] + [(swapped(a), (1, places)) for a, places in arrays]


def local(groups, size, tokens, lengths, cotangent, attn_gain, mlp_gain, *weights):
    sec, t = lax.axis_index("section"), lax.axis_index("tensor")
    first = sec == 0
    rows, depth = tokens.shape[1:]
    mine = [w[0] for w in weights]
    gains = jnp.concatenate([attn_gain, mlp_gain], axis=0)
    other_gains = swapped(gains)
    layer_gains = [jnp.where(sec == l, gains, other_gains) for l in range(2)]
    attn_gains = [g[0:1] for g in layer_gains]
    mlp_gains = [g[1:2] for g in layer_gains]
    length = lax.dynamic_index_in_dim(lengths[:, 0], sec, 0, keepdims=False)
    tok = lax.dynamic_index_in_dim(tokens, sec, 0, keepdims=False)
    cot = lax.dynamic_index_in_dim(cotangent, sec, 0, keepdims=False)
    within = jnp.arange(rows, dtype=jnp.int32)
    own_places = t * rows + within
    places = jnp.concatenate([(t ^ k) * rows + within for k in range(size)])
    readable = jnp.where(places < length, places, jnp.int32(1 << 20))
    tables = rope_tables(places, HD) + (places[:, None], readable[None, :])

    g_low = jnp.where((own_places < length)[:, None], cot, jnp.zeros_like(cot))

    def for_layer(pair):
        keep, send = jnp.where(first, pair[0], pair[1]), jnp.where(first, pair[1], pair[0])
        return keep, swapped(send)

    def both(pair):
        keep, came = for_layer(pair)
        return [jnp.where(first, keep, came), jnp.where(first, came, keep)]

    attn_mine = [jnp.concatenate(mine[:3], axis=1), mine[3]]
    attn_w = [(w, swapped(tied(w, other_gains))) for w in attn_mine]
    attn_cuts = [(0, w.shape[0]) for w in attn_mine]
    g_blocks1 = gather_rows(g_low, size)
    normed = tied(norm_rows(tok, attn_gains[0]), *g_blocks1)
    *weights_in, token = prefetch(0, attn_w, attn_cuts, normed)
    blocks = gather_rows(normed, size)
    all_g1 = jnp.concatenate(g_blocks1, axis=0)
    blocks[0] = tied(blocks[0], all_g1)
    all_g1 = over_groups(all_g1)
    *parts, x_attn0, q0, k0, v0, att0 = attend_fwd(blocks, weights_in, tables)
    gate_other, up_other = [swapped(tied(w, normed, *[o for _, o in attn_w])) for w in mine[4:6]]
    down_other = swapped(tied(mine[6], gate_other, parts[0]))
    mlp_w = list(zip(mine[4:], (gate_other, up_other, down_other)))
    mlp_cuts = [(0, w.shape[0]) for w in mine[4:]]
    mid0, normed = add_norm(tok, scatter_rows(parts, size), mlp_gains[0], False)
    *weights_in, token = prefetch(0, mlp_w, mlp_cuts, normed)
    *parts, gate0, up0, x_half = mlp_fwd(gather_rows(normed, size), weights_in)
    act0, normed = add_norm(mid0, scatter_rows(parts, size), attn_gains[1], True)

    *weights_in, token = prefetch(1, attn_w, attn_cuts, normed)
    *parts, x_attn1, q1, k1, v1, att1 = attend_fwd(gather_rows(normed, size), weights_in, tables)
    parts[0] = tied(parts[0], all_g1)
    half_x0 = over_groups(tied(x_half, all_g1, parts[0]))
    mid1, normed = add_norm(act0, scatter_rows(parts, size), mlp_gains[1], False)
    *weights_in, token = prefetch(1, mlp_w, mlp_cuts, normed)
    *both_parts, x_all = mlp_both(gather_rows(normed, size), g_blocks1, weights_in)
    parts1, parts = both_parts[:size], both_parts[size:]
    parts[0] = tied(parts[0], half_x0)
    all_x1 = over_groups(tied(x_all, half_x0, parts[0]))
    d_mid, d_mid_low, mlp_part1 = norm_back(mid1, scatter_rows(parts, size), mlp_gains[1], g_low)
    *weights_in, token = prefetch(1, attn_w, attn_cuts, d_mid_low)
    *parts, dm, dqkv = attend_bwd(gather_rows(d_mid_low, size), (q1, k1, v1), weights_in, tables)
    attn_terms1 = attend_grads(x_attn1, dqkv, dm, att1)
    came = scatter_rows(parts, size)
    came[0] = tied(came[0], attn_terms1)
    d_stream1, d_low, attn_part1 = norm_back(act0, came, attn_gains[1], d_mid)

    *weights_in, token = prefetch(0, mlp_w, mlp_cuts, d_low)
    *parts, g_all = mlp_bwd(gather_rows(d_low, size), gate0, up0, weights_in)
    parts[0] = tied(parts[0], all_x1)
    all_g0 = over_groups(tied(g_all, all_x1, parts[0]))
    x1, g1 = from_both_cores((all_x1, ALL)), from_both_cores((all_g1, ALL))
    pieces = [(f, part) for f in range(mine[4].shape[1] // (2 * PIECE)) for part in range(2)]
    tiles1 = []

    def piece1(*after):
        f, part = pieces[len(tiles1)]
        tiles1.append(mlp_grads(1, f, part, [(tied(a, *after), o) for a, o in x1], g1, mlp_w))
        return tiles1[-1]

    d_mid, d_mid_low, mlp_part0 = norm_back(mid0, scatter_rows(parts, size), mlp_gains[0], d_low)
    *weights_in, token = prefetch(0, attn_w, attn_cuts, d_mid_low)
    blocks = gather_rows(d_mid_low, size)
    blocks[0] = tied(blocks[0], piece1(d_mid_low, token))
    *parts, dm, dqkv = attend_bwd(blocks, (q0, k0, v0), weights_in, tables)
    attn_terms0 = attend_grads(x_attn0, dqkv, dm, att0)
    x_pair, at = partners(size)[0], groups // 2
    rest_x0 = [lax.ppermute(tied(x, parts[0]), "tensor", x_pair) for x in (half_x0[:at], half_x0[at:])]
    came = scatter_rows(parts, size)
    came[0] = tied(came[0], piece1(parts[0], attn_terms0))
    d_stream0, _, attn_part0 = norm_back(tok, came, attn_gains[0], d_mid)

    attn_share1 = summed_over_groups(tied(attn_terms1, all_g0, d_stream0))
    keep, came = for_layer(
        [jnp.concatenate(p, axis=0) for p in ((attn_part0, mlp_part0), (attn_part1, mlp_part1))]
    )
    shares = (keep + came).reshape(2, groups, size, depth // (groups * size))
    while len(tiles1) < len(pieces):
        piece1(tiles1[-1], d_stream0)
    x0 = from_both_cores((half_x0, (0, 2)))
    x0_rest = [from_both_cores((rest, (1, 3))) for rest in rest_x0]
    g0 = from_both_cores((all_g0, ALL))
    tiles0, others1 = [], [swapped(tile) for tile in tiles1]
    order0 = [(f, part) for part in range(2) for f in range(len(pieces) // 2)]

    def piece0(*after):
        f, part = order0[len(tiles0)]
        tiles0.append(mlp_grads(0, f, part, [(tied(a, *after), o) for a, o in x0 + x0_rest[part]], g0, mlp_w))
        return tiles0[-1]

    while len(tiles0) < len(pieces):
        piece0(tiles1[-1], *tiles0[-1:])
    attn_share0 = summed_over_groups(tied(attn_terms0, attn_share1, tiles0[0]))
    done = iter([tiles1[2], tiles1[3], *tiles0])
    for axis, count, dim in (("tensor", size, 2), ("dp", groups, 1)):
        bit = count // 2
        while bit:
            shares = halved(tied(shares, next(done, tiles0[-1])), axis, count, bit, dim)
            bit //= 2
    shares = shares.reshape(2, -1)
    act1, _ = add_norm(
        mid1, scatter_rows([tied(p, tiles0[1]) for p in parts1], size), attn_gains[1], True
    )
    tiles0 = [tiles0[order0.index(piece)] for piece in pieces]
    others0 = [swapped(tile) for tile in tiles0]
    layers = [
        (tiles0, attn_share0, others0, swapped(attn_share0)),
        (tiles1, attn_share1, others1, swapped(attn_share1)),
    ]
    weight_grads = assemble(layers, mine[0].shape[1], mine[1].shape[1], mine[4].shape[1])
    acts, input_grads = (act0, act1), (d_stream0, d_stream1)

    return (
        jnp.stack(both(acts))[None],
        jnp.stack(both(input_grads))[None],
        shares[0:1],
        shares[1:2],
        *[grad[None] for grad in weight_grads],
    )


def solution(mesh):
    rows = P(None, ("dp", "tensor"), None)
    in_specs = (
        rows,
        P(None, "dp"),
        rows,
        P("section", None),
        P("section", None),
        P("section", None, "tensor"),
        P("section", None, "tensor"),
        P("section", None, "tensor"),
        P("section", "tensor", None),
        P("section", None, "tensor"),
        P("section", None, "tensor"),
        P("section", "tensor", None),
    )
    out_rows = P("section", None, ("dp", "tensor"), None)
    shares = P("section", ("dp", "tensor"))
    by_dp, by_tensor = P("section", "dp", "tensor"), P("section", "tensor", "dp")
    out_specs = (
        out_rows, out_rows, shares, shares, by_dp, by_dp, by_dp, by_tensor, by_dp, by_dp, by_tensor,
    )
    step = functools.partial(local, mesh.shape["dp"], mesh.shape["tensor"])
    return jax.shard_map(step, mesh=mesh, in_specs=in_specs, out_specs=out_specs, check_vma=False)
```

time: 690 us -> 554 us (0.80)
  waiting for transfers between devices: 274 us -> 131 us
  Pallas kernels: 222 us -> 263 us
  other arithmetic: 45 us -> 17.1 us
  matrix products: 10.9 us -> 0 us
  local copies, waits for them, and re-layouts: 35.9 us -> 46.8 us
    reduce_scatter x4 -> x2, waiting for transfers between devices: 107 us -> 0.01 us  [summed_over_groups(): return lax.psum_scatter(x, 'dp', scatter_dimension=0, tiled=True)]
    pallas_call x18 -> x34, Pallas kernels: 222 us -> 263 us  [the longest x8 115 us: mlp_grads(): pl.pallas_call(functools.partial(mlp_grads_kernel, layer, f, first, last,...]
    ppermute x24, waiting for transfers between devices: 62.5 us -> 24.5 us  [gather_rows(): return [x] + [lax.ppermute(x, 'tensor', pairs) for pairs in partners(size)]]
    ppermute x6, waiting for transfers between devices: 7.03 us -> 31 us  [the longest x2 24.2 us: local(): lax.ppermute(tied(x, parts[0]), 'tensor', x_pair)]
    unnamed x140 -> x200, local copies, waits for them, and re-layouts: 20.5 us -> 40.8 us
    select_n x7 -> x4, other arithmetic: 12.9 us -> 0.03 us  [halved(): keep, send = (jnp.where(upper, high, low), jnp.where(upper, low, high))]
    ppermute x23 -> x33, waiting for transfers between devices: 17.8 us -> 6.6 us  [swapped(): return lax.ppermute(x, 'section', [(0, 1), (1, 0)])]
    concatenate x3 -> x2, other arithmetic: 17 us -> 6.07 us  [the longest x1 3.97 us: local(): attn_mine = [jnp.concatenate(mine[:3], axis=1), mine[3]]]
  transfers between devices with their start and end apart: 85 -> 93, of which waited for: 52 -> 34; matrix products, arithmetic and copies ran while one was open for 11% -> 4% of each run, Pallas kernels for 18% -> 46%
where the time goes in v2:
time: 554 us; the launch traced here: 547 us
  Pallas kernels  263 us (47%)
  waiting for transfers between devices  131 us (24%)
  starting transfers between devices  73 us (13%)
  local copies, waits for them, and re-layouts  46.8 us (8%)
  other arithmetic  17.1 us (3%)
  between operations  15.5 us (3%)
    pallas_call x8, Pallas kernels, mlp_grads(): pl.pallas_call(functools.partial(mlp_grads_kernel, layer, f, first, last,...  115 us
    ppermute x24, waiting for transfers between devices, scatter_rows(): lax.ppermute(part, 'tensor', pairs)  68.7 us
    unnamed x200, local copies, waits for them, and re-layouts  40.8 us
    pallas_call x7, Pallas kernels, prefetch(): pl.pallas_call(functools.partial(prefetch_kernel, layer, cuts), out_shape...  39.2 us
    ppermute x24, starting transfers between devices, gather_rows(): return [x] + [lax.ppermute(x, 'tensor', pairs) for pairs in partners(size)]  28.6 us
    ppermute x24, starting transfers between devices, scatter_rows(): lax.ppermute(part, 'tensor', pairs)  28.5 us
    ppermute x24, waiting for transfers between devices, gather_rows(): return [x] + [lax.ppermute(x, 'tensor', pairs) for pairs in partners(size)]  24.5 us
    ppermute x2, waiting for transfers between devices, local(): lax.ppermute(tied(x, parts[0]), 'tensor', x_pair)  24.2 us
  transfers between devices with their start and end apart: 93, of which 34 were waited for; matrix products, arithmetic and copies ran while one was open for 4% of the time, Pallas kernels for 46%

profile of v2, /device:TPU:0, one launch (start us, length us, event | category | flops | bytes accessed | tf_op | source)
XLA Modules:
  0.0 546.6 jit_solution(10309957080226011388)
XLA Ops:
  25.1 6.9 %collective-permute-done.2.g2 = bf16[64,2048]{1,0:T(8,128)(2,1)} collective-permute-done((bf16[64,2048]{1,0:T(8,128)(2,1)S(1)}, bf16[64,2048]{1,0:T(8,128)(2,1)}, u32[]{:S(2)}, u32[]{:S(2)}) %collective-permute-start.2) | collective-permute-done | bytes 262176 | tf_op jit(solution)/shard_map/ppermute | solution.py:59
  42.9 4.3 collective-permute-done.5.x2
  49.5 5.8 %attend_fwd.2 = (bf16[64,2048]{1,0:T(8,128)(2,1)S(1)}, bf16[64,2048]{1,0:T(8,128)(2,1)S(1)}, bf16[64,2048]{1,0:T(8,128)(2,1)S(1)}, bf16[64,2048]{1,0:T(8,128)(2,...) custom-call(bf16[64,2048]{1,0:T(8,128)(2,1)} %norm.1.after_ref.x0, ...), custom_call_target="tpu_custom_call" | custom-call | flops 100000000 | bytes 240000 | tf_op jit(solution)/shard_map/attend_fwd/pallas_call | solution.py:277
  59.8 10.8 %collective-permute-done.10.c_ref = bf16[64,2048]{1,0:T(8,128)(2,1)S(1)} collective-permute-done((bf16[64,2048]{1,0:T(8,128)(2,1)S(1)}, bf16[64,2048]{1,0:T(8,128)(2,1)S(1)}, u32[]{:S(2)}, u32[]{:S(2)}) %collective-permute-start.10) | collective-permute-done | bytes 262176 | tf_op jit(solution)/shard_map/ppermute | solution.py:64
  79.4 8.9 %prefetch.8 = (bf16[2048,2048]{1,0:T(8,128)(2,1)S(1)}, bf16[2048,2048]{1,0:T(8,128)(2,1)S(1)}, bf16[2048,2048]{1,0:T(8,128)(2,1)S(1)}, f32[8,128]{1,0:T(8,128)}) custom-call(bf16[64,2048]{1,0:T(8,128)(2,1)S(1)} %copy-done.8, bf16[2048,2048]{1,0:T(8,128)(2,1)} %bitcast.51, bf16[2048,2048]{1,0:T(8,128)(2,1)} %collective-permute-done.15.refs_1_.refs_5_.refs_7_, ...), custom_call_target="tpu_custom_call" | custom-call | bytes 1006632 | tf_op jit(solution)/shard_map/prefetch/pallas_call | solution.py:169
  89.8 8.9 %mlp_fwd.1 = (bf16[64,2048]{1,0:T(8,128)(2,1)S(1)}, bf16[64,2048]{1,0:T(8,128)(2,1)S(1)}, bf16[64,2048]{1,0:T(8,128)(2,1)S(1)}, bf16[64,2048]{1,0:T(8,128)(2,1)S...) custom-call(bf16[64,2048]{1,0:T(8,128)(2,1)} %get-tuple-element.168.after_ref.x0, ...), custom_call_target="tpu_custom_call" | custom-call | flops 128849016 | bytes 600000 | tf_op jit(solution)/shard_map/mlp_fwd/pallas_call | solution.py:400
  103.6 5.1 collective-permute-done.18.b_ref
  128.5 5.8 %attend_fwd.3 = (bf16[64,2048]{1,0:T(8,128)(2,1)S(1)}, bf16[64,2048]{1,0:T(8,128)(2,1)S(1)}, bf16[64,2048]{1,0:T(8,128)(2,1)S(1)}, bf16[64,2048]{1,0:T(8,128)(2,...) custom-call(bf16[64,2048]{1,0:T(8,128)(2,1)} %get-tuple-element.180., ...), custom_call_target="tpu_custom_call" | custom-call | flops 100000000 | bytes 240000 | tf_op jit(solution)/shard_map/attend_fwd/pallas_call | solution.py:277
  141.6 6.0 %collective-permute-done.24.b_ref = bf16[64,2048]{1,0:T(8,128)(2,1)} collective-permute-done((bf16[64,2048]{1,0:T(8,128)(2,1)}, bf16[64,2048]{1,0:T(8,128)(2,1)}, u32[]{:S(2)}, u32[]{:S(2)}) %collective-permute-start.24) | collective-permute-done | bytes 262176 | tf_op jit(solution)/shard_map/ppermute | solution.py:64
  147.7 5.6 %collective-permute-done.25.c_ref = bf16[64,2048]{1,0:T(8,128)(2,1)} collective-permute-done((bf16[64,2048]{1,0:T(8,128)(2,1)}, bf16[64,2048]{1,0:T(8,128)(2,1)}, u32[]{:S(2)}, u32[]{:S(2)}) %collective-permute-start.25) | collective-permute-done | bytes 262176 | tf_op jit(solution)/shard_map/ppermute | solution.py:64
  160.1 8.9 %prefetch.10 = (bf16[2048,2048]{1,0:T(8,128)(2,1)S(1)}, bf16[2048,2048]{1,0:T(8,128)(2,1)S(1)}, bf16[2048,2048]{1,0:T(8,128)(2,1)S(1)}, f32[8,128]{1,0:T(8,128)}) custom-call(bf16[64,2048]{1,0:T(8,128)(2,1)S(1)} %copy-done.9, bf16[2048,2048]{1,0:T(8,128)(2,1)} %bitcast.52, bf16[2048,2048]{1,0:T(8,128)(2,1)} %collective-permute-done.15.refs_1_.refs_5_.refs_7_, ...), custom_call_target="tpu_custom_call" | custom-call | bytes 1006632 | tf_op jit(solution)/shard_map/prefetch/pallas_call | solution.py:169
  170.2 17.5 %mlp_both.1 = (bf16[64,2048]{1,0:T(8,128)(2,1)S(1)}, bf16[64,2048]{1,0:T(8,128)(2,1)S(1)}, bf16[64,2048]{1,0:T(8,128)(2,1)S(1)}, bf16[64,2048]{1,0:T(8,128)(2,1)...) custom-call(bf16[64,2048]{1,0:T(8,128)(2,1)} %get-tuple-element.189., ...), custom_call_target="tpu_custom_call" | custom-call | flops 257698032 | bytes 600000 | tf_op jit(solution)/shard_map/mlp_both/pallas_call | solution.py:505
  197.5 5.1 collective-permute-done.30.b_ref
  202.5 4.2 collective-permute-done.31.c_ref
  221.7 10.1 %attend_bwd.2 = (bf16[64,2048]{1,0:T(8,128)(2,1)S(1)}, bf16[64,2048]{1,0:T(8,128)(2,1)}, bf16[64,2048]{1,0:T(8,128)(2,1)}, bf16[64,2048]{1,0:T(8,128)(2,1)}, bf1...) custom-call(bf16[64,2048]{1,0:T(8,128)(2,1)} %get-tuple-element.203.after_ref.d0, bf16[64,2048]{1,0:T(8,128)(2,1)} %copy-done.86, ...), custom_call_target="tpu_custom_call" | custom-call | flops 140000000 | bytes 280000 | tf_op jit(solution)/shard_map/attend_bwd/pallas_call | solution.py:358
  242.5 7.2 %collective-permute-done.41.c_ref = bf16[64,2048]{1,0:T(8,128)(2,1)} collective-permute-done((bf16[64,2048]{1,0:T(8,128)(2,1)}, bf16[64,2048]{1,0:T(8,128)(2,1)}, u32[]{:S(2)}, u32[]{:S(2)}) %collective-permute-start.41) | collective-permute-done | bytes 262176 | tf_op jit(solution)/shard_map/ppermute | solution.py:64
  257.0 8.8 %prefetch.12 = (bf16[2048,2048]{1,0:T(8,128)(2,1)S(1)}, bf16[2048,2048]{1,0:T(8,128)(2,1)S(1)}, bf16[2048,2048]{1,0:T(8,128)(2,1)S(1)}, f32[8,128]{1,0:T(8,128)}) custom-call(bf16[64,2048]{1,0:T(8,128)(2,1)S(1)} %copy-done.6, bf16[2048,2048]{1,0:T(8,128)(2,1)} %bitcast.53, bf16[2048,2048]{1,0:T(8,128)(2,1)} %collective-permute-done.15.refs_1_.refs_5_.refs_7_, ...), custom_call_target="tpu_custom_call" | custom-call | bytes 1006632 | tf_op jit(solution)/shard_map/prefetch/pallas_call | solution.py:169
  267.7 9.8 %mlp_bwd.1 = (bf16[64,2048]{1,0:T(8,128)(2,1)S(1)}, bf16[64,2048]{1,0:T(8,128)(2,1)S(1)}, bf16[64,2048]{1,0:T(8,128)(2,1)S(1)}, bf16[64,2048]{1,0:T(8,128)(2,1)S(1)}, bf16[256,2048]{1,0:T(8,128)(2,1)}) custom-call(bf16[64,2048]{1,0:T(8,128)(2,1)} %get-tuple-element.219.after_ref.g0.res_ref, bf16[64,2048]{1,0:T(8,128)(2,1)} %copy-done.60, ...), custom_call_target="tpu_custom_call" | custom-call | flops 128849016 | bytes 600000 | tf_op jit(solution)/shard_map/mlp_bwd/pallas_call | solution.py:445
  283.7 5.9 %collective-permute-done.46.b_ref = bf16[64,2048]{1,0:T(8,128)(2,1)S(1)} collective-permute-done((bf16[64,2048]{1,0:T(8,128)(2,1)}, bf16[64,2048]{1,0:T(8,128)(2,1)S(1)}, u32[]{:S(2)}, u32[]{:S(2)}) %collective-permute-start.46) | collective-permute-done | bytes 262176 | tf_op jit(solution)/shard_map/ppermute | solution.py:64
  289.6 5.4 collective-permute-done.47.c_ref
  306.9 13.8 %mlp_grads.8.refs_10_ = bf16[512,1536]{1,0:T(8,128)(2,1)S(1)} custom-call(bf16[4,256,2048]{2,1,0:T(8,128)(2,1)} %bitcast.92, bf16[4,256,2048]{2,1,0:T(8,128)(2,1)} %collective-permute-done.49.refs_1_, bf16[4,256,2048]{2,1,0:T(8,128)(2,1)} %bitcast.87, bf16[4,256,2048]{2,1,0:T(8,128)(2,1)} %collective-permute-done.50.refs_3_, bf16[2048,2048]{1,0:T(8,128)(2,1)} %bitcast.54, ...), custom_call_target="tpu_custom_call" | custom-call | flops 161061280 | bytes 400000 | tf_op jit(solution)/shard_map/mlp_grads/pallas_call | solution.py:607
  321.6 10.0 %attend_bwd.3 = (bf16[64,2048]{1,0:T(8,128)(2,1)S(1)}, bf16[64,2048]{1,0:T(8,128)(2,1)}, bf16[64,2048]{1,0:T(8,128)(2,1)S(1)}, bf16[64,2048]{1,0:T(8,128)(2,1)S(...) custom-call(bf16[64,2048]{1,0:T(8,128)(2,1)} %get-tuple-element.234.after_ref.d0, ...), custom_call_target="tpu_custom_call" | custom-call | flops 140000000 | bytes 280000 | tf_op jit(solution)/shard_map/attend_bwd/pallas_call | solution.py:358
  342.5 15.3 %mlp_grads.9.refs_11_ = bf16[512,1536]{1,0:T(8,128)(2,1)} custom-call(bf16[4,256,2048]{2,1,0:T(8,128)(2,1)} %bitcast.93, bf16[4,256,2048]{2,1,0:T(8,128)(2,1)} %collective-permute-done.49.refs_1_, bf16[4,256,2048]{2,1,0:T(8,128)(2,1)} %bitcast.88, bf16[4,256,2048]{2,1,0:T(8,128)(2,1)} %collective-permute-done.50.refs_3_, bf16[2048,2048]{1,0:T(8,128)(2,1)} %bitcast.55, ...), custom_call_target="tpu_custom_call" | custom-call | flops 161061280 | bytes 400000 | tf_op jit(solution)/shard_map/mlp_grads/pallas_call | solution.py:607
  365.7 24.2 %collective-permute-done.62.refs_2_ = bf16[2,128,2048]{2,1,0:T(8,128)(2,1)S(1)} collective-permute-done((bf16[2,128,2048]{2,1,0:T(8,128)(2,1)S(1)}, bf16[2,128,2048]{2,1,0:T(8,128)(2,1)S(1)}, u32[]{:S(2)}, u32[]{:S(2)}) %collective-permute-start.62) | collective-permute-done | bytes 1048608 | tf_op jit(solution)/shard_map/ppermute | solution.py:871
  390.8 15.0 %mlp_grads.10.refs_12_ = bf16[512,1536]{1,0:T(8,128)(2,1)} custom-call(bf16[4,256,2048]{2,1,0:T(8,128)(2,1)} %bitcast.94, bf16[4,256,2048]{2,1,0:T(8,128)(2,1)} %collective-permute-done.49.refs_1_, bf16[4,256,2048]{2,1,0:T(8,128)(2,1)} %bitcast.89, bf16[4,256,2048]{2,1,0:T(8,128)(2,1)} %collective-permute-done.50.refs_3_, bf16[2048,2048]{1,0:T(8,128)(2,1)} %bitcast.56, ...), custom_call_target="tpu_custom_call" | custom-call | flops 161061280 | bytes 400000 | tf_op jit(solution)/shard_map/mlp_grads/pallas_call | solution.py:607
  405.8 14.9 %mlp_grads.11.refs_13_ = bf16[512,1536]{1,0:T(8,128)(2,1)} custom-call(bf16[4,256,2048]{2,1,0:T(8,128)(2,1)} %bitcast.95, bf16[4,256,2048]{2,1,0:T(8,128)(2,1)} %collective-permute-done.49.refs_1_, bf16[4,256,2048]{2,1,0:T(8,128)(2,1)} %bitcast.90, bf16[4,256,2048]{2,1,0:T(8,128)(2,1)} %collective-permute-done.50.refs_3_, bf16[2048,2048]{1,0:T(8,128)(2,1)} %bitcast.57, ...), custom_call_target="tpu_custom_call" | custom-call | flops 161061280 | bytes 400000 | tf_op jit(solution)/shard_map/mlp_grads/pallas_call | solution.py:607
  424.5 13.6 %mlp_grads.12.refs_0_ = bf16[512,1536]{1,0:T(8,128)(2,1)S(1)} custom-call(bf16[4,128,2048]{2,1,0:T(8,128)(2,1)} %bitcast.102, bf16[4,128,2048]{2,1,0:T(8,128)(2,1)} %copy-done.44, bf16[2,128,2048]{2,1,0:T(8,128)(2,1)} %copy-done.47, bf16[2,128,2048]{2,1,0:T(8,128)(2,1)} %copy-done.48, bf16[4,256,2048]{2,1,0:T(8,128)(2,1)} %bitcast.97, ...), custom_call_target="tpu_custom_call" | custom-call | flops 161061280 | bytes 400000 | tf_op jit(solution)/shard_map/mlp_grads/pallas_call | solution.py:607
  448.2 13.7 %mlp_grads.13.refs_2_ = bf16[512,1536]{1,0:T(8,128)(2,1)S(1)} custom-call(bf16[4,128,2048]{2,1,0:T(8,128)(2,1)} %bitcast.103, bf16[4,128,2048]{2,1,0:T(8,128)(2,1)} %copy-done.44, bf16[2,128,2048]{2,1,0:T(8,128)(2,1)} %copy-done.47, bf16[2,128,2048]{2,1,0:T(8,128)(2,1)} %copy-done.48, bf16[4,256,2048]{2,1,0:T(8,128)(2,1)} %bitcast.98, ...), custom_call_target="tpu_custom_call" | custom-call | flops 161061280 | bytes 400000 | tf_op jit(solution)/shard_map/mlp_grads/pallas_call | solution.py:607
  471.7 6.4 %collective-permute-done.66.c_ref = bf16[64,2048]{1,0:T(8,128)(2,1)S(1)} collective-permute-done((bf16[64,2048]{1,0:T(8,128)(2,1)S(1)}, bf16[64,2048]{1,0:T(8,128)(2,1)S(1)}, u32[]{:S(2)}, u32[]{:S(2)}) %collective-permute-start.66) | collective-permute-done | bytes 262176 | tf_op jit(solution)/shard_map/ppermute | solution.py:64
  480.8 13.7 %mlp_grads.14.refs_1_ = bf16[512,1536]{1,0:T(8,128)(2,1)S(1)} custom-call(bf16[4,128,2048]{2,1,0:T(8,128)(2,1)} %bitcast.104, bf16[4,128,2048]{2,1,0:T(8,128)(2,1)} %copy-done.44, bf16[2,128,2048]{2,1,0:T(8,128)(2,1)} %copy-done.46, bf16[2,128,2048]{2,1,0:T(8,128)(2,1)} %collective-permute-done.76.refs_3_, bf16[4,256,2048]{2,1,0:T(8,128)(2,1)} %bitcast.99, ...), custom_call_target="tpu_custom_call" | custom-call | flops 161061280 | bytes 400000 | tf_op jit(solution)/shard_map/mlp_grads/pallas_call | solution.py:607
  495.7 15.1 %mlp_grads.15.refs_3_ = bf16[512,1536]{1,0:T(8,128)(2,1)} custom-call(bf16[4,128,2048]{2,1,0:T(8,128)(2,1)} %bitcast.105, bf16[4,128,2048]{2,1,0:T(8,128)(2,1)} %copy-done.44, bf16[2,128,2048]{2,1,0:T(8,128)(2,1)} %copy-done.46, bf16[2,128,2048]{2,1,0:T(8,128)(2,1)} %collective-permute-done.76.refs_3_, bf16[4,256,2048]{2,1,0:T(8,128)(2,1)} %bitcast.100, ...), custom_call_target="tpu_custom_call" | custom-call | flops 161061280 | bytes 400000 | tf_op jit(solution)/shard_map/mlp_grads/pallas_call | solution.py:607
  527.5 11.9 %assemble.1 = (f32[512,512]{1,0:T(8,128)}, f32[512,128]{1,0:T(8,128)}, f32[512,128]{1,0:T(8,128)}, f32[512,512]{1,0:T(8,128)}, f32[512,2048]{1,0:T(8,128)}, /*index=5*/f32[512,2048]{1,0:T(8,128)}, f32[2048,512]{1,0:T(8,128)}) custom-call(bf16[512,1536]{1,0:T(8,128)(2,1)} %copy-done.3, bf16[512,1536]{1,0:T(8,128)(2,1)} %copy-done.5, ...), custom_call_target="tpu_custom_call" | custom-call | bytes 600000 | tf_op jit(solution)/shard_map/assemble/pallas_call | solution.py:698
  (434 shorter events, 212.7 us)
Async XLA Ops:
  7.2 130.6 %all-gather.9.cloned.1.call-start = ((), (), s32[]{:S(2)}) async-start(), calls=%async_computation.4 | async-start | bytes 5242880 | tf_op jit(solution)/shard_map/all_gather | solution.py:777
  12.5 19.5 %collective-permute-start.7 = (bf16[2048,768]{1,0:T(8,128)(2,1)}, bf16[2048,768]{1,0:T(8,128)(2,1)}, u32[]{:S(2)}, u32[]{:S(2)}) collective-permute-start(bf16[2048,768]{1,0:T(8,128)(2,1)} %pad_maximum_fusion.refs_0_), channel_id=1, source_target_pairs={{0,16},{16,0},{1,17},{17,1},{2,18},{18,2},{3,19},{19,3},{4,20},{20... | collective-permute-start | bytes 9437192 | tf_op jit(solution)/shard_map/ppermute | solution.py:69
  32.1 23.9 %collective-permute-start.15 = (bf16[2048,2048]{1,0:T(8,128)(2,1)}, bf16[2048,2048]{1,0:T(8,128)(2,1)}, u32[]{:S(2)}, u32[]{:S(2)}) collective-permute-start(bf16[2048,2048]{1,0:T(8,128)(2,1)} %bitcast.50), channel_id=1, source_target_pairs={{0,16},{16,0},{1,17},{17,1},{2,18},{18,2},{3,19},{19,3},{4,20},{20... | collective-permute-start | bytes 25165832 | tf_op jit(solution)/shard_map/ppermute | solution.py:69
  39.7 38.7 %collective-permute-start.16 = (bf16[2048,2048]{1,0:T(8,128)(2,1)}, bf16[2048,2048]{1,0:T(8,128)(2,1)}, u32[]{:S(2)}, u32[]{:S(2)}) collective-permute-start(bf16[2048,2048]{1,0:T(8,128)(2,1)} %bitcast.62), channel_id=1, source_target_pairs={{0,16},{16,0},{1,17},{17,1},{2,18},{18,2},{3,19},{19,3},{4,20},{20... | collective-permute-start | bytes 25165832 | tf_op jit(solution)/shard_map/ppermute | solution.py:69
  55.9 22.5 %collective-permute-start.17 = (bf16[2048,2048]{1,0:T(8,128)(2,1)}, bf16[2048,2048]{1,0:T(8,128)(2,1)}, u32[]{:S(2)}, u32[]{:S(2)}) collective-permute-start(bf16[2048,2048]{1,0:T(8,128)(2,1)} %bitcast.74), channel_id=1, source_target_pairs={{0,16},{16,0},{1,17},{17,1},{2,18},{18,2},{3,19},{19,3},{4,20},{20... | collective-permute-start | bytes 25165832 | tf_op jit(solution)/shard_map/ppermute | solution.py:69
  56.0 137.4 %all-gather.11.cloned.1.call-start = ((), (), s32[]{:S(2)}) async-start(), calls=%async_computation.5 | async-start | bytes 2621440 | tf_op jit(solution)/shard_map/all_gather | solution.py:777
  137.8 141.8 %all-gather.13.cloned.1.call-start = ((), (), s32[]{:S(2)}) async-start(), calls=%async_computation.6 | async-start | bytes 5242880 | tf_op jit(solution)/shard_map/all_gather | solution.py:777
  193.4 167.9 %all-gather.15.cloned.1.call-start = ((), (), s32[]{:S(2)}) async-start(), calls=%async_computation.7 | async-start | bytes 5242880 | tf_op jit(solution)/shard_map/all_gather | solution.py:777
  213.1 23.3 %collective-permute-start.36 = (bf16[256,2048]{1,0:T(8,128)(2,1)}, bf16[256,2048]{1,0:T(8,128)(2,1)S(1)}, u32[]{:S(2)}, u32[]{:S(2)}) collective-permute-start(bf16[256,2048]{1,0:T(8,128)(2,1)} %get-tuple-element.210.x_own), channel_id=1, source_target_pairs={{0,16},{16,0},{1,17},{17,1},{2,18},{18,2},{3,19},{19,3},{4,20},{20... | collective-permute-start | bytes 3145736 | tf_op jit(solution)/shard_map/ppermute | solution.py:69
  279.6 159.6 %reduce-scatter.3.cloned.1.call-start = ((), (), s32[]{:S(2)}) async-start(), calls=%async_computation.2 | async-start | bytes 3276800 | tf_op jit(solution)/shard_map/reduce_scatter | solution.py:748
  279.7 23.1 %collective-permute-start.49 = (bf16[4,256,2048]{2,1,0:T(8,128)(2,1)}, bf16[4,256,2048]{2,1,0:T(8,128)(2,1)}, u32[]{:S(2)}, u32[]{:S(2)}) collective-permute-start(bf16[4,256,2048]{2,1,0:T(8,128)(2,1)} %bitcast.91), channel_id=1, source_target_pairs={{0,16},{16,0},{1,17},{17,1},{2,18},{18,2},{3,19},{19,3},{4,20},{20... | collective-permute-start | bytes 12582920 | tf_op jit(solution)/shard_map/ppermute | solution.py:69
  279.8 27.2 %collective-permute-start.50 = (bf16[4,256,2048]{2,1,0:T(8,128)(2,1)}, bf16[4,256,2048]{2,1,0:T(8,128)(2,1)}, u32[]{:S(2)}, u32[]{:S(2)}) collective-permute-start(bf16[4,256,2048]{2,1,0:T(8,128)(2,1)} %bitcast.86), channel_id=1, source_target_pairs={{0,16},{16,0},{1,17},{17,1},{2,18},{18,2},{3,19},{19,3},{4,20},{20... | collective-permute-start | bytes 12582920 | tf_op jit(solution)/shard_map/ppermute | solution.py:69
  299.2 21.4 %collective-permute-start.51 = (bf16[64,2048]{1,0:T(8,128)(2,1)}, bf16[64,2048]{1,0:T(8,128)(2,1)S(1)}, u32[]{:S(2)}, u32[]{:S(2)}) collective-permute-start(bf16[64,2048]{1,0:T(8,128)(2,1)} %get-tuple-element.234.after_ref.d0), channel_id=1, source_target_pairs={{0,1},{1,0},{2,3},{3,2},{4,5},{5,4},{6,7},{7,6},{8,9},{9,8},{10,11... | collective-permute-start | bytes 786440 | tf_op jit(solution)/shard_map/ppermute | solution.py:59
  300.3 20.4 %collective-permute-start.52 = (bf16[64,2048]{1,0:T(8,128)(2,1)}, bf16[64,2048]{1,0:T(8,128)(2,1)S(1)}, u32[]{:S(2)}, u32[]{:S(2)}) collective-permute-start(bf16[64,2048]{1,0:T(8,128)(2,1)} %get-tuple-element.234.after_ref.d0), channel_id=1, source_target_pairs={{0,2},{1,3},{2,0},{3,1},{4,6},{5,7},{6,4},{7,5},{8,10},{9,11},{10,... | collective-permute-start | bytes 786440 | tf_op jit(solution)/shard_map/ppermute | solution.py:59
  301.2 19.6 %collective-permute-start.53 = (bf16[64,2048]{1,0:T(8,128)(2,1)}, bf16[64,2048]{1,0:T(8,128)(2,1)S(1)}, u32[]{:S(2)}, u32[]{:S(2)}) collective-permute-start(bf16[64,2048]{1,0:T(8,128)(2,1)} %get-tuple-element.234.after_ref.d0), channel_id=1, source_target_pairs={{0,3},{1,2},{2,1},{3,0},{4,7},{5,6},{6,5},{7,4},{8,11},{9,10},{10,... | collective-permute-start | bytes 786440 | tf_op jit(solution)/shard_map/ppermute | solution.py:59
  302.7 33.8 %collective-permute-start.54 = (bf16[256,2048]{1,0:T(8,128)(2,1)}, bf16[256,2048]{1,0:T(8,128)(2,1)S(1)}, u32[]{:S(2)}, u32[]{:S(2)}) collective-permute-start(bf16[256,2048]{1,0:T(8,128)(2,1)} %get-tuple-element.241.x_own), channel_id=1, source_target_pairs={{0,16},{16,0},{1,17},{17,1},{2,18},{18,2},{3,19},{19,3},{4,20},{20... | collective-permute-start | bytes 3145736 | tf_op jit(solution)/shard_map/ppermute | solution.py:69
  333.2 24.6 %collective-permute-start.58 = (bf16[64,2048]{1,0:T(8,128)(2,1)}, bf16[64,2048]{1,0:T(8,128)(2,1)S(1)}, u32[]{:S(2)}, u32[]{:S(2)}) collective-permute-start(bf16[64,2048]{1,0:T(8,128)(2,1)} %get-tuple-element.248), channel_id=1, source_target_pairs={{0,1},{1,0},{2,3},{3,2},{4,5},{5,4},{6,7},{7,6},{8,9},{9,8},{10,11... | collective-permute-start | bytes 786440 | tf_op jit(solution)/shard_map/ppermute | solution.py:64
  335.3 22.5 %collective-permute-start.59 = (bf16[64,2048]{1,0:T(8,128)(2,1)S(1)}, bf16[64,2048]{1,0:T(8,128)(2,1)}, u32[]{:S(2)}, u32[]{:S(2)}) collective-permute-start(bf16[64,2048]{1,0:T(8,128)(2,1)S(1)} %get-tuple-element.249), channel_id=1, source_target_pairs={{0,2},{1,3},{2,0},{3,1},{4,6},{5,7},{6,4},{7,5},{8,10},{9,11},{10,... | collective-permute-start | bytes 786440 | tf_op jit(solution)/shard_map/ppermute | solution.py:64
  336.5 21.3 %collective-permute-start.60 = (bf16[64,2048]{1,0:T(8,128)(2,1)S(1)}, bf16[64,2048]{1,0:T(8,128)(2,1)}, u32[]{:S(2)}, u32[]{:S(2)}) collective-permute-start(bf16[64,2048]{1,0:T(8,128)(2,1)S(1)} %get-tuple-element.250), channel_id=1, source_target_pairs={{0,3},{1,2},{2,1},{3,0},{4,7},{5,6},{6,5},{7,4},{8,11},{9,10},{10,... | collective-permute-start | bytes 786440 | tf_op jit(solution)/shard_map/ppermute | solution.py:64
  361.3 161.4 %reduce-scatter.5.cloned.1.call-start = ((), (), s32[]{:S(2)}) async-start(), calls=%async_computation.3 | async-start | bytes 3276800 | tf_op jit(solution)/shard_map/reduce_scatter | solution.py:748
  361.4 59.5 %collective-permute-start.64 = (bf16[4,256,2048]{2,1,0:T(8,128)(2,1)}, bf16[4,256,2048]{2,1,0:T(8,128)(2,1)S(1)}, u32[]{:S(2)}, u32[]{:S(2)}) collective-permute-start(bf16[4,256,2048]{2,1,0:T(8,128)(2,1)} %bitcast.96), channel_id=1, source_target_pairs={{0,16},{16,0},{1,17},{17,1},{2,18},{18,2},{3,19},{19,3},{4,20},{20... | collective-permute-start | bytes 12582920 | tf_op jit(solution)/shard_map/ppermute | solution.py:69
  361.5 59.3 %collective-permute-start.61 = (bf16[4,128,2048]{2,1,0:T(8,128)(2,1)}, bf16[4,128,2048]{2,1,0:T(8,128)(2,1)S(1)}, u32[]{:S(2)}, u32[]{:S(2)}) collective-permute-start(bf16[4,128,2048]{2,1,0:T(8,128)(2,1)} %bitcast.101), channel_id=1, source_target_pairs={{0,16},{16,0},{1,17},{17,1},{2,18},{18,2},{3,19},{19,3},{4,20},{20... | collective-permute-start | bytes 6291464 | tf_op jit(solution)/shard_map/ppermute | solution.py:69
  364.7 25.1 %collective-permute-start.62 = (bf16[2,128,2048]{2,1,0:T(8,128)(2,1)S(1)}, bf16[2,128,2048]{2,1,0:T(8,128)(2,1)S(1)}, u32[]{:S(2)}, u32[]{:S(2)}) collective-permute-start(bf16[2,128,2048]{2,1,0:T(8,128)(2,1)S(1)} %bitcast.112), channel_id=1, source_target_pairs={{0,1},{1,0},{2,3},{3,2},{4,5},{5,4},{6,7},{7,6},{8,9},{9,8},{10,11... | collective-permute-start | bytes 3145736 | tf_op jit(solution)/shard_map/ppermute | solution.py:871
  389.9 30.9 %collective-permute-start.63 = (bf16[2,128,2048]{2,1,0:T(8,128)(2,1)S(1)}, bf16[2,128,2048]{2,1,0:T(8,128)(2,1)S(1)}, u32[]{:S(2)}, u32[]{:S(2)}) collective-permute-start(bf16[2,128,2048]{2,1,0:T(8,128)(2,1)S(1)} %collective-permute-done.62.refs_2_), channel_id=1, source_target_pairs={{0,16},{16,0},{1,17},{17,1},{2,18},{18,2},{3,19},{19,3},{4,20},{20... | collective-permute-start | bytes 3145736 | tf_op jit(solution)/shard_map/ppermute | solution.py:69
  389.9 49.7 %collective-permute-start.75 = (bf16[2,128,2048]{2,1,0:T(8,128)(2,1)}, bf16[2,128,2048]{2,1,0:T(8,128)(2,1)S(1)}, u32[]{:S(2)}, u32[]{:S(2)}) collective-permute-start(bf16[2,128,2048]{2,1,0:T(8,128)(2,1)} %bitcast.28), channel_id=1, source_target_pairs={{0,1},{1,0},{2,3},{3,2},{4,5},{5,4},{6,7},{7,6},{8,9},{9,8},{10,11... | collective-permute-start | bytes 3145736 | tf_op jit(solution)/shard_map/ppermute | solution.py:871
  439.5 28.6 %collective-permute-start.76 = (bf16[2,128,2048]{2,1,0:T(8,128)(2,1)S(1)}, bf16[2,128,2048]{2,1,0:T(8,128)(2,1)}, u32[]{:S(2)}, u32[]{:S(2)}) collective-permute-start(bf16[2,128,2048]{2,1,0:T(8,128)(2,1)S(1)} %collective-permute-done.75.refs_2_), channel_id=1, source_target_pairs={{0,16},{16,0},{1,17},{17,1},{2,18},{18,2},{3,19},{19,3},{4,20},{20... | collective-permute-start | bytes 3145736 | tf_op jit(solution)/shard_map/ppermute | solution.py:69
  443.0 24.6 %collective-permute-start.69 = (f32[64,2048]{1,0:T(8,128)}, f32[64,2048]{1,0:T(8,128)}, u32[]{:S(2)}, u32[]{:S(2)}) collective-permute-start(f32[64,2048]{1,0:T(8,128)} %broadcast_select_fusion), channel_id=1, source_target_pairs={{0,16},{16,0},{1,17},{17,1},{2,18},{18,2},{3,19},{19,3},{4,20},{20... | collective-permute-start | bytes 1572872 | tf_op jit(solution)/shard_map/ppermute | solution.py:69
  467.6 46.8 %collective-permute-start.82 = (bf16[512,1536]{1,0:T(8,128)(2,1)S(1)}, bf16[512,1536]{1,0:T(8,128)(2,1)}, u32[]{:S(2)}, u32[]{:S(2)}) collective-permute-start(bf16[512,1536]{1,0:T(8,128)(2,1)S(1)} %mlp_grads.8.refs_10_), channel_id=1, source_target_pairs={{0,16},{16,0},{1,17},{17,1},{2,18},{18,2},{3,19},{19,3},{4,20},{20... | collective-permute-start | bytes 4718600 | tf_op jit(solution)/shard_map/ppermute | solution.py:69
  467.6 47.3 %collective-permute-start.85 = (bf16[512,1536]{1,0:T(8,128)(2,1)}, bf16[512,1536]{1,0:T(8,128)(2,1)}, u32[]{:S(2)}, u32[]{:S(2)}) collective-permute-start(bf16[512,1536]{1,0:T(8,128)(2,1)} %mlp_grads.11.refs_13_), channel_id=1, source_target_pairs={{0,16},{16,0},{1,17},{17,1},{2,18},{18,2},{3,19},{19,3},{4,20},{20... | collective-permute-start | bytes 4718600 | tf_op jit(solution)/shard_map/ppermute | solution.py:69
  468.1 46.8 %collective-permute-start.84 = (bf16[512,1536]{1,0:T(8,128)(2,1)}, bf16[512,1536]{1,0:T(8,128)(2,1)}, u32[]{:S(2)}, u32[]{:S(2)}) collective-permute-start(bf16[512,1536]{1,0:T(8,128)(2,1)} %mlp_grads.10.refs_12_), channel_id=1, source_target_pairs={{0,16},{16,0},{1,17},{17,1},{2,18},{18,2},{3,19},{19,3},{4,20},{20... | collective-permute-start | bytes 4718600 | tf_op jit(solution)/shard_map/ppermute | solution.py:69
  469.3 46.0 %collective-permute-start.83 = (bf16[512,1536]{1,0:T(8,128)(2,1)}, bf16[512,1536]{1,0:T(8,128)(2,1)}, u32[]{:S(2)}, u32[]{:S(2)}) collective-permute-start(bf16[512,1536]{1,0:T(8,128)(2,1)} %mlp_grads.9.refs_11_), channel_id=1, source_target_pairs={{0,16},{16,0},{1,17},{17,1},{2,18},{18,2},{3,19},{19,3},{4,20},{20... | collective-permute-start | bytes 4718600 | tf_op jit(solution)/shard_map/ppermute | solution.py:69
  478.1 32.6 %collective-permute-start.65 = (bf16[64,2048]{1,0:T(8,128)(2,1)S(1)}, bf16[64,2048]{1,0:T(8,128)(2,1)S(1)}, u32[]{:S(2)}, u32[]{:S(2)}) collective-permute-start(bf16[64,2048]{1,0:T(8,128)(2,1)S(1)} %copy-done.30), channel_id=1, source_target_pairs={{0,1},{1,0},{2,3},{3,2},{4,5},{5,4},{6,7},{7,6},{8,9},{9,8},{10,11... | collective-permute-start | bytes 786440 | tf_op jit(solution)/shard_map/ppermute | solution.py:64
  (161 other events, 1257.0 us)
Sparse Core Ops, SparseCore 0:
  56.1 81.5 all-gather.8
  139.8 44.4 all-gather.10
  193.5 78.1 all-gather.12
  279.8 80.8 all-gather.14
  363.4 50.6 reduce-scatter.2
  439.4 51.9 reduce-scatter.4

commit v3 on v2

--- a/solution.py
+++ b/solution.py
@@ -841,15 +841,24 @@
     parts[0] = tied(parts[0], half_x0)
     all_x1 = over_groups(tied(x_all, half_x0, parts[0]))
     d_mid, d_mid_low, mlp_part1 = norm_back(mid1, scatter_rows(parts, size), mlp_gains[1], g_low)
+    rest_x0 = []
+
+    def with_chunk(blocks, results):
+        chunk = lax.ppermute(tied(half_x0[len(rest_x0)], *blocks), "tensor", partners(size)[0])
+        results, chunk = lax.optimization_barrier((list(results), chunk))
+        rest_x0.append(chunk)
+        return results
+
     *weights_in, token = prefetch(1, attn_w, attn_cuts, d_mid_low)
-    *parts, dm, dqkv = attend_bwd(gather_rows(d_mid_low, size), (q1, k1, v1), weights_in, tables)
+    blocks = gather_rows(d_mid_low, size)
+    *parts, dm, dqkv = with_chunk(blocks, attend_bwd(blocks, (q1, k1, v1), weights_in, tables))
     attn_terms1 = attend_grads(x_attn1, dqkv, dm, att1)
     came = scatter_rows(parts, size)
     came[0] = tied(came[0], attn_terms1)
     d_stream1, d_low, attn_part1 = norm_back(act0, came, attn_gains[1], d_mid)
 
     *weights_in, token = prefetch(0, mlp_w, mlp_cuts, d_low)
-    *parts, g_all = mlp_bwd(gather_rows(d_low, size), gate0, up0, weights_in)
+    *parts, g_all = with_chunk([token], mlp_bwd(gather_rows(d_low, size), gate0, up0, weights_in))
     parts[0] = tied(parts[0], all_x1)
     all_g0 = over_groups(tied(g_all, all_x1, parts[0]))
     x1, g1 = from_both_cores((all_x1, ALL)), from_both_cores((all_g1, ALL))
@@ -865,50 +874,82 @@
     *weights_in, token = prefetch(0, attn_w, attn_cuts, d_mid_low)
     blocks = gather_rows(d_mid_low, size)
     blocks[0] = tied(blocks[0], piece1(d_mid_low, token))
-    *parts, dm, dqkv = attend_bwd(blocks, (q0, k0, v0), weights_in, tables)
+    *parts, dm, dqkv = with_chunk(blocks, attend_bwd(blocks, (q0, k0, v0), weights_in, tables))
     attn_terms0 = attend_grads(x_attn0, dqkv, dm, att0)
-    x_pair, at = partners(size)[0], groups // 2
-    rest_x0 = [lax.ppermute(tied(x, parts[0]), "tensor", x_pair) for x in (half_x0[:at], half_x0[at:])]
     came = scatter_rows(parts, size)
     came[0] = tied(came[0], piece1(parts[0], attn_terms0))
     d_stream0, _, attn_part0 = norm_back(tok, came, attn_gains[0], d_mid)
 
     attn_share1 = summed_over_groups(tied(attn_terms1, all_g0, d_stream0))
+
+    def beside(results, *transfers):
+        results, transfers = lax.optimization_barrier((results, list(transfers)))
+        return results, transfers
+
+    def halves(axis, count, dim, bit, total):
+        low, high = lax.slice_in_dim(total, 0, bit, axis=dim), lax.slice_in_dim(total, bit, 2 * bit, axis=dim)
+        upper = (lax.axis_index(axis) & bit) != 0
+        came = lax.ppermute(jnp.where(upper, low, high), axis, [(a, a ^ bit) for a in range(count)])
+        return jnp.where(upper, high, low), came
+
     keep, came = for_layer(
         [jnp.concatenate(p, axis=0) for p in ((attn_part0, mlp_part0), (attn_part1, mlp_part1))]
     )
+    others1, others0 = [swapped(tile) for tile in tiles1], []
+    while len(rest_x0) < groups:
+        rest_x0.append(lax.ppermute(tied(half_x0[len(rest_x0)], d_stream0), "tensor", partners(size)[0]))
+    tiles1[2], (came, rest_x0[-1], *others1) = beside(piece1(d_stream0), came, rest_x0[-1], *others1)
     shares = (keep + came).reshape(2, groups, size, depth // (groups * size))
-    while len(tiles1) < len(pieces):
-        piece1(tiles1[-1], d_stream0)
-    x0 = from_both_cores((half_x0, (0, 2)))
-    x0_rest = [from_both_cores((rest, (1, 3))) for rest in rest_x0]
-    g0 = from_both_cores((all_g0, ALL))
-    tiles0, others1 = [], [swapped(tile) for tile in tiles1]
+    steps = [("tensor", size, 2, 1 << n) for n in reversed(range(size.bit_length() - 1))]
+    steps += [("dp", groups, 1, 1 << n) for n in reversed(range(groups.bit_length() - 1))]
+
+    def step_beside(results, *transfers):
+        nonlocal shares
+        keep, came = halves(*steps.pop(0), shares)
+        results, (came, *transfers) = beside(results, came, *transfers)
+        shares = keep + came
+        return results, transfers
+
+    at = groups // 2
+    x0, g0 = from_both_cores((half_x0, (0, 2))), from_both_cores((all_g0, ALL))
+    x0_rest = [
+        from_both_cores((jnp.stack(part), (1, 3))) for part in (rest_x0[:at], rest_x0[at:])
+    ]
+    tiles1[3:], (moved,) = step_beside([piece1(tiles1[2])], swapped(tiles1[2]))
+    others1.append(moved)
     order0 = [(f, part) for part in range(2) for f in range(len(pieces) // 2)]
 
-    def piece0(*after):
+    def piece0(after):
         f, part = order0[len(tiles0)]
-        tiles0.append(mlp_grads(0, f, part, [(tied(a, *after), o) for a, o in x0 + x0_rest[part]], g0, mlp_w))
+        tiles0.append(mlp_grads(0, f, part, [(tied(a, after), o) for a, o in x0 + x0_rest[part]], g0, mlp_w))
         return tiles0[-1]
 
-    while len(tiles0) < len(pieces):
-        piece0(tiles1[-1], *tiles0[-1:])
+    tiles0 = []
+    tiles0[0:], (moved,) = step_beside([piece0(tiles1[3])], swapped(tiles1[3]))
+    others1.append(moved)
     attn_share0 = summed_over_groups(tied(attn_terms0, attn_share1, tiles0[0]))
-    done = iter([tiles1[2], tiles1[3], *tiles0])
-    for axis, count, dim in (("tensor", size, 2), ("dp", groups, 1)):
-        bit = count // 2
-        while bit:
-            shares = halved(tied(shares, next(done, tiles0[-1])), axis, count, bit, dim)
-            bit //= 2
+    tiles0[1:], (moved,) = step_beside([piece0(tiles0[0])], swapped(tiles0[0]))
+    others0.append(moved)
+    act_terms = scatter_rows([tied(p, tiles0[0]) for p in parts1], size)
+    tiles0[2:], (moved, *act_terms[1:]) = step_beside(
+        [piece0(tiles0[1])], swapped(tiles0[1]), *act_terms[1:]
+    )
+    others0.append(moved)
+    while steps:
+        step_beside([])
+    act1, _ = add_norm(mid1, act_terms, attn_gains[1], True)
     shares = shares.reshape(2, -1)
-    act1, _ = add_norm(
-        mid1, scatter_rows([tied(p, tiles0[1]) for p in parts1], size), attn_gains[1], True
+    tiles0[3:], (moved, swapped_share1) = beside(
+        [piece0(tied(tiles0[2], act1, shares))], swapped(tiles0[2]), swapped(attn_share1)
     )
+    others0.append(moved)
+    attn_share0 = tied(attn_share0, tiles0[3])
+    others0.append(swapped(tiles0[3]))
+    others0 = [others0[order0.index(piece)] for piece in pieces]
     tiles0 = [tiles0[order0.index(piece)] for piece in pieces]
-    others0 = [swapped(tile) for tile in tiles0]
     layers = [
         (tiles0, attn_share0, others0, swapped(attn_share0)),
-        (tiles1, attn_share1, others1, swapped(attn_share1)),
+        (tiles1, attn_share1, others1, swapped_share1),
     ]
     weight_grads = assemble(layers, mine[0].shape[1], mine[1].shape[1], mine[4].shape[1])
     acts, input_grads = (act0, act1), (d_stream0, d_stream1)

time: 554 us -> 513 us (0.926)
  waiting for transfers between devices: 131 us -> 100 us
  local copies, waits for them, and re-layouts: 46.8 us -> 38.4 us
    ppermute x6 -> x8, waiting for transfers between devices: 31 us -> 0.02 us  [the longest x4 0.01 us: halves(): lax.ppermute(jnp.where(upper, low, high), axis, [(a, a ^ bit) for a in ra...]
    ppermute x24, waiting for transfers between devices: 68.7 us -> 58.7 us  [scatter_rows(): lax.ppermute(part, 'tensor', pairs)]
    unnamed x200 -> x226, local copies, waits for them, and re-layouts: 40.8 us -> 32.5 us
    ppermute x24, waiting for transfers between devices: 24.5 us -> 30.6 us  [gather_rows(): return [x] + [lax.ppermute(x, 'tensor', pairs) for pairs in partners(size)]]
  transfers between devices with their start and end apart: 93 -> 95, of which waited for: 34 -> 26; matrix products, arithmetic and copies ran while one was open for 4% -> 4% of each run, Pallas kernels for 46% -> 50%
where the time goes in v3:
time: 513 us; the launch traced here: 507 us
  Pallas kernels  263 us (51%)
  waiting for transfers between devices  100 us (19%)
  starting transfers between devices  74.1 us (14%)
  local copies, waits for them, and re-layouts  38.4 us (7%)
  between operations  15.8 us (3%)
  other arithmetic  15.7 us (3%)
    pallas_call x8, Pallas kernels, mlp_grads(): pl.pallas_call(functools.partial(mlp_grads_kernel, layer, f, first, last,...  115 us
    ppermute x24, waiting for transfers between devices, scatter_rows(): lax.ppermute(part, 'tensor', pairs)  58.7 us
    pallas_call x7, Pallas kernels, prefetch(): pl.pallas_call(functools.partial(prefetch_kernel, layer, cuts), out_shape...  39.2 us
    unnamed x226, local copies, waits for them, and re-layouts  32.5 us
    ppermute x24, waiting for transfers between devices, gather_rows(): return [x] + [lax.ppermute(x, 'tensor', pairs) for pairs in partners(size)]  30.6 us
    ppermute x24, starting transfers between devices, scatter_rows(): lax.ppermute(part, 'tensor', pairs)  29.5 us
    ppermute x24, starting transfers between devices, gather_rows(): return [x] + [lax.ppermute(x, 'tensor', pairs) for pairs in partners(size)]  28.6 us
    pallas_call x2, Pallas kernels, attend_bwd(): pl.pallas_call(attend_bwd_kernel, out_shape=(block,) * 4 + (far((whole, d...  19.3 us
  transfers between devices with their start and end apart: 95, of which 26 were waited for; matrix products, arithmetic and copies ran while one was open for 4% of the time, Pallas kernels for 50%

profile of v3, /device:TPU:0, one launch (start us, length us, event | category | flops | bytes accessed | tf_op | source)
XLA Modules:
  0.0 507.2 jit_solution(17601579268382006460)
XLA Ops:
  24.2 6.8 %collective-permute-done.2.g2 = bf16[64,2048]{1,0:T(8,128)(2,1)S(1)} collective-permute-done((bf16[64,2048]{1,0:T(8,128)(2,1)S(1)}, bf16[64,2048]{1,0:T(8,128)(2,1)S(1)}, u32[]{:S(2)}, u32[]{:S(2)}) %collective-permute-start.2) | collective-permute-done | bytes 262176 | tf_op jit(solution)/shard_map/ppermute | solution.py:59
  41.8 4.4 collective-permute-done.5.x2
  48.5 5.8 %attend_fwd.2 = (bf16[64,2048]{1,0:T(8,128)(2,1)S(1)}, bf16[64,2048]{1,0:T(8,128)(2,1)S(1)}, bf16[64,2048]{1,0:T(8,128)(2,1)S(1)}, bf16[64,2048]{1,0:T(8,128)(2,...) custom-call(bf16[64,2048]{1,0:T(8,128)(2,1)} %norm.1.after_ref.x0, ...), custom_call_target="tpu_custom_call" | custom-call | flops 100000000 | bytes 240000 | tf_op jit(solution)/shard_map/attend_fwd/pallas_call | solution.py:277
  61.7 10.8 %collective-permute-done.10.c_ref = bf16[64,2048]{1,0:T(8,128)(2,1)S(1)} collective-permute-done((bf16[64,2048]{1,0:T(8,128)(2,1)S(1)}, bf16[64,2048]{1,0:T(8,128)(2,1)S(1)}, u32[]{:S(2)}, u32[]{:S(2)}) %collective-permute-start.10) | collective-permute-done | bytes 262176 | tf_op jit(solution)/shard_map/ppermute | solution.py:64
  81.3 8.9 %prefetch.8 = (bf16[2048,2048]{1,0:T(8,128)(2,1)S(1)}, bf16[2048,2048]{1,0:T(8,128)(2,1)S(1)}, bf16[2048,2048]{1,0:T(8,128)(2,1)S(1)}, f32[8,128]{1,0:T(8,128)}) custom-call(bf16[64,2048]{1,0:T(8,128)(2,1)S(1)} %copy-done.8, bf16[2048,2048]{1,0:T(8,128)(2,1)} %bitcast.53, bf16[2048,2048]{1,0:T(8,128)(2,1)} %collective-permute-done.15.refs_1_.refs_5_.refs_7_, ...), custom_call_target="tpu_custom_call" | custom-call | bytes 1006632 | tf_op jit(solution)/shard_map/prefetch/pallas_call | solution.py:169
  91.8 9.0 %mlp_fwd.1 = (bf16[64,2048]{1,0:T(8,128)(2,1)S(1)}, bf16[64,2048]{1,0:T(8,128)(2,1)S(1)}, bf16[64,2048]{1,0:T(8,128)(2,1)S(1)}, bf16[64,2048]{1,0:T(8,128)(2,1)S...) custom-call(bf16[64,2048]{1,0:T(8,128)(2,1)} %get-tuple-element.210.after_ref.x0, ...), custom_call_target="tpu_custom_call" | custom-call | flops 128849016 | bytes 600000 | tf_op jit(solution)/shard_map/mlp_fwd/pallas_call | solution.py:400
  105.6 5.1 %collective-permute-done.18.b_ref = bf16[64,2048]{1,0:T(8,128)(2,1)S(1)} collective-permute-done((bf16[64,2048]{1,0:T(8,128)(2,1)S(1)}, bf16[64,2048]{1,0:T(8,128)(2,1)S(1)}, u32[]{:S(2)}, u32[]{:S(2)}) %collective-permute-start.18) | collective-permute-done | bytes 262176 | tf_op jit(solution)/shard_map/ppermute | solution.py:64
  110.7 4.2 collective-permute-done.19.c_ref
  130.5 5.8 %attend_fwd.3 = (bf16[64,2048]{1,0:T(8,128)(2,1)S(1)}, bf16[64,2048]{1,0:T(8,128)(2,1)S(1)}, bf16[64,2048]{1,0:T(8,128)(2,1)S(1)}, bf16[64,2048]{1,0:T(8,128)(2,...) custom-call(bf16[64,2048]{1,0:T(8,128)(2,1)} %get-tuple-element.222., ...), custom_call_target="tpu_custom_call" | custom-call | flops 100000000 | bytes 240000 | tf_op jit(solution)/shard_map/attend_fwd/pallas_call | solution.py:277
  143.6 5.8 %collective-permute-done.24.b_ref = bf16[64,2048]{1,0:T(8,128)(2,1)S(1)} collective-permute-done((bf16[64,2048]{1,0:T(8,128)(2,1)S(1)}, bf16[64,2048]{1,0:T(8,128)(2,1)S(1)}, u32[]{:S(2)}, u32[]{:S(2)}) %collective-permute-start.24) | collective-permute-done | bytes 262176 | tf_op jit(solution)/shard_map/ppermute | solution.py:64
  149.3 5.1 %collective-permute-done.25.c_ref = bf16[64,2048]{1,0:T(8,128)(2,1)S(1)} collective-permute-done((bf16[64,2048]{1,0:T(8,128)(2,1)S(1)}, bf16[64,2048]{1,0:T(8,128)(2,1)S(1)}, u32[]{:S(2)}, u32[]{:S(2)}) %collective-permute-start.25) | collective-permute-done | bytes 262176 | tf_op jit(solution)/shard_map/ppermute | solution.py:64
  162.7 8.9 %prefetch.10 = (bf16[2048,2048]{1,0:T(8,128)(2,1)S(1)}, bf16[2048,2048]{1,0:T(8,128)(2,1)S(1)}, bf16[2048,2048]{1,0:T(8,128)(2,1)S(1)}, f32[8,128]{1,0:T(8,128)}) custom-call(bf16[64,2048]{1,0:T(8,128)(2,1)S(1)} %copy-done.9, bf16[2048,2048]{1,0:T(8,128)(2,1)} %bitcast.54, bf16[2048,2048]{1,0:T(8,128)(2,1)} %collective-permute-done.15.refs_1_.refs_5_.refs_7_, ...), custom_call_target="tpu_custom_call" | custom-call | bytes 1006632 | tf_op jit(solution)/shard_map/prefetch/pallas_call | solution.py:169
  172.5 17.5 %mlp_both.1 = (bf16[64,2048]{1,0:T(8,128)(2,1)S(1)}, bf16[64,2048]{1,0:T(8,128)(2,1)S(1)}, bf16[64,2048]{1,0:T(8,128)(2,1)S(1)}, bf16[64,2048]{1,0:T(8,128)(2,1)...) custom-call(bf16[64,2048]{1,0:T(8,128)(2,1)} %get-tuple-element.231., ...), custom_call_target="tpu_custom_call" | custom-call | flops 257698032 | bytes 600000 | tf_op jit(solution)/shard_map/mlp_both/pallas_call | solution.py:505
  199.7 6.1 %collective-permute-done.30.b_ref = bf16[64,2048]{1,0:T(8,128)(2,1)} collective-permute-done((bf16[64,2048]{1,0:T(8,128)(2,1)}, bf16[64,2048]{1,0:T(8,128)(2,1)}, u32[]{:S(2)}, u32[]{:S(2)}) %collective-permute-start.30) | collective-permute-done | bytes 262176 | tf_op jit(solution)/shard_map/ppermute | solution.py:64
  219.5 5.6 %collective-permute-done.34.d2 = bf16[64,2048]{1,0:T(8,128)(2,1)S(1)} collective-permute-done((bf16[64,2048]{1,0:T(8,128)(2,1)}, bf16[64,2048]{1,0:T(8,128)(2,1)S(1)}, u32[]{:S(2)}, u32[]{:S(2)}) %collective-permute-start.34) | collective-permute-done | bytes 262176 | tf_op jit(solution)/shard_map/ppermute | solution.py:59
  228.8 10.2 %attend_bwd.2 = (bf16[64,2048]{1,0:T(8,128)(2,1)S(1)}, bf16[64,2048]{1,0:T(8,128)(2,1)}, bf16[64,2048]{1,0:T(8,128)(2,1)}, bf16[64,2048]{1,0:T(8,128)(2,1)}, bf1...) custom-call(bf16[64,2048]{1,0:T(8,128)(2,1)} %get-tuple-element.245.after_ref.d0, bf16[64,2048]{1,0:T(8,128)(2,1)} %copy-done.98, ...), custom_call_target="tpu_custom_call" | custom-call | flops 140000000 | bytes 280000 | tf_op jit(solution)/shard_map/attend_bwd/pallas_call | solution.py:358
  251.5 6.4 %collective-permute-done.42.c_ref = bf16[64,2048]{1,0:T(8,128)(2,1)} collective-permute-done((bf16[64,2048]{1,0:T(8,128)(2,1)}, bf16[64,2048]{1,0:T(8,128)(2,1)}, u32[]{:S(2)}, u32[]{:S(2)}) %collective-permute-start.42) | collective-permute-done | bytes 262176 | tf_op jit(solution)/shard_map/ppermute | solution.py:64
  265.2 8.8 %prefetch.12 = (bf16[2048,2048]{1,0:T(8,128)(2,1)S(1)}, bf16[2048,2048]{1,0:T(8,128)(2,1)S(1)}, bf16[2048,2048]{1,0:T(8,128)(2,1)S(1)}, f32[8,128]{1,0:T(8,128)}) custom-call(bf16[64,2048]{1,0:T(8,128)(2,1)S(1)} %copy-done.6, bf16[2048,2048]{1,0:T(8,128)(2,1)} %bitcast.55, bf16[2048,2048]{1,0:T(8,128)(2,1)} %collective-permute-done.15.refs_1_.refs_5_.refs_7_, ...), custom_call_target="tpu_custom_call" | custom-call | bytes 1006632 | tf_op jit(solution)/shard_map/prefetch/pallas_call | solution.py:169
  274.0 4.4 collective-permute-done.46.g3
  279.1 9.8 %mlp_bwd.1 = (bf16[64,2048]{1,0:T(8,128)(2,1)S(1)}, bf16[64,2048]{1,0:T(8,128)(2,1)S(1)}, bf16[64,2048]{1,0:T(8,128)(2,1)S(1)}, bf16[64,2048]{1,0:T(8,128)(2,1)S(1)}, bf16[256,2048]{1,0:T(8,128)(2,1)}) custom-call(bf16[64,2048]{1,0:T(8,128)(2,1)} %get-tuple-element.268.after_ref.g0.res_ref, bf16[64,2048]{1,0:T(8,128)(2,1)} %copy-done.71, ...), custom_call_target="tpu_custom_call" | custom-call | flops 128849016 | bytes 600000 | tf_op jit(solution)/shard_map/mlp_bwd/pallas_call | solution.py:445
  293.7 5.7 %collective-permute-done.48.b_ref = bf16[64,2048]{1,0:T(8,128)(2,1)S(1)} collective-permute-done((bf16[64,2048]{1,0:T(8,128)(2,1)S(1)}, bf16[64,2048]{1,0:T(8,128)(2,1)S(1)}, u32[]{:S(2)}, u32[]{:S(2)}) %collective-permute-start.48) | collective-permute-done | bytes 262176 | tf_op jit(solution)/shard_map/ppermute | solution.py:64
  299.4 4.8 collective-permute-done.49.c_ref
  316.2 13.9 %mlp_grads.8.refs_10_ = bf16[512,1536]{1,0:T(8,128)(2,1)S(1)} custom-call(bf16[4,256,2048]{2,1,0:T(8,128)(2,1)} %bitcast.94, bf16[4,256,2048]{2,1,0:T(8,128)(2,1)} %collective-permute-done.51.refs_1_, bf16[4,256,2048]{2,1,0:T(8,128)(2,1)} %bitcast.89, bf16[4,256,2048]{2,1,0:T(8,128)(2,1)} %collective-permute-done.52.refs_3_, bf16[2048,2048]{1,0:T(8,128)(2,1)} %bitcast.56, ...), custom_call_target="tpu_custom_call" | custom-call | flops 161061280 | bytes 400000 | tf_op jit(solution)/shard_map/mlp_grads/pallas_call | solution.py:607
  332.0 9.1 %attend_bwd.3 = (bf16[64,2048]{1,0:T(8,128)(2,1)S(1)}, bf16[64,2048]{1,0:T(8,128)(2,1)S(1)}, bf16[64,2048]{1,0:T(8,128)(2,1)S(1)}, bf16[64,2048]{1,0:T(8,128)(2,...) custom-call(bf16[64,2048]{1,0:T(8,128)(2,1)} %get-tuple-element.288.after_ref.d0, ...), custom_call_target="tpu_custom_call" | custom-call | flops 140000000 | bytes 280000 | tf_op jit(solution)/shard_map/attend_bwd/pallas_call | solution.py:358
  352.0 14.9 %mlp_grads.9.refs_11_ = bf16[512,1536]{1,0:T(8,128)(2,1)} custom-call(bf16[4,256,2048]{2,1,0:T(8,128)(2,1)} %bitcast.95, bf16[4,256,2048]{2,1,0:T(8,128)(2,1)} %collective-permute-done.51.refs_1_, bf16[4,256,2048]{2,1,0:T(8,128)(2,1)} %bitcast.90, bf16[4,256,2048]{2,1,0:T(8,128)(2,1)} %collective-permute-done.52.refs_3_, bf16[2048,2048]{1,0:T(8,128)(2,1)} %bitcast.57, ...), custom_call_target="tpu_custom_call" | custom-call | flops 161061280 | bytes 400000 | tf_op jit(solution)/shard_map/mlp_grads/pallas_call | solution.py:607
  372.4 15.7 %mlp_grads.10.refs_12_ = bf16[512,1536]{1,0:T(8,128)(2,1)} custom-call(bf16[4,256,2048]{2,1,0:T(8,128)(2,1)} %bitcast.96, bf16[4,256,2048]{2,1,0:T(8,128)(2,1)} %collective-permute-done.51.refs_1_, bf16[4,256,2048]{2,1,0:T(8,128)(2,1)} %bitcast.91, bf16[4,256,2048]{2,1,0:T(8,128)(2,1)} %collective-permute-done.52.refs_3_, bf16[2048,2048]{1,0:T(8,128)(2,1)} %bitcast.58, ...), custom_call_target="tpu_custom_call" | custom-call | flops 161061280 | bytes 400000 | tf_op jit(solution)/shard_map/mlp_grads/pallas_call | solution.py:607
  389.5 13.8 %mlp_grads.11.refs_13_ = bf16[512,1536]{1,0:T(8,128)(2,1)S(1)} custom-call(bf16[4,256,2048]{2,1,0:T(8,128)(2,1)} %bitcast.97, bf16[4,256,2048]{2,1,0:T(8,128)(2,1)} %collective-permute-done.51.refs_1_, bf16[4,256,2048]{2,1,0:T(8,128)(2,1)} %bitcast.92, bf16[4,256,2048]{2,1,0:T(8,128)(2,1)} %collective-permute-done.52.refs_3_, bf16[2048,2048]{1,0:T(8,128)(2,1)} %bitcast.59, ...), custom_call_target="tpu_custom_call" | custom-call | flops 161061280 | bytes 400000 | tf_op jit(solution)/shard_map/mlp_grads/pallas_call | solution.py:607
  408.4 14.9 %mlp_grads.12.refs_0_ = bf16[512,1536]{1,0:T(8,128)(2,1)} custom-call(bf16[4,128,2048]{2,1,0:T(8,128)(2,1)} %bitcast.104, bf16[4,128,2048]{2,1,0:T(8,128)(2,1)} %collective-permute-done.70.refs_1_, bf16[2,128,2048]{2,1,0:T(8,128)(2,1)} %copy-done.52, bf16[2,128,2048]{2,1,0:T(8,128)(2,1)} %collective-permute-done.71.refs_3_, bf16[4,256,2048]{2,1,0:T(8,128)(2,1)} %bitcast.99, ...), custom_call_target="tpu_custom_call" | custom-call | flops 161061280 | bytes 400000 | tf_op jit(solution)/shard_map/mlp_grads/pallas_call | solution.py:607
  424.8 13.7 %mlp_grads.13.refs_2_ = bf16[512,1536]{1,0:T(8,128)(2,1)S(1)} custom-call(bf16[4,128,2048]{2,1,0:T(8,128)(2,1)} %bitcast.105, bf16[4,128,2048]{2,1,0:T(8,128)(2,1)} %collective-permute-done.70.refs_1_, bf16[2,128,2048]{2,1,0:T(8,128)(2,1)} %copy-done.52, bf16[2,128,2048]{2,1,0:T(8,128)(2,1)} %collective-permute-done.71.refs_3_, ...), custom_call_target="tpu_custom_call" | custom-call | flops 161061280 | bytes 400000 | tf_op jit(solution)/shard_map/mlp_grads/pallas_call | solution.py:607
  444.8 14.8 %mlp_grads.14.refs_1_ = bf16[512,1536]{1,0:T(8,128)(2,1)} custom-call(bf16[4,128,2048]{2,1,0:T(8,128)(2,1)} %bitcast.106, bf16[4,128,2048]{2,1,0:T(8,128)(2,1)} %collective-permute-done.70.refs_1_, bf16[2,128,2048]{2,1,0:T(8,128)(2,1)} %copy-done.51, bf16[2,128,2048]{2,1,0:T(8,128)(2,1)} %collective-permute-done.77.refs_3_, bf16[4,256,2048]{2,1,0:T(8,128)(2,1)} %bitcast.101, ...), custom_call_target="tpu_custom_call" | custom-call | flops 161061280 | bytes 400000 | tf_op jit(solution)/shard_map/mlp_grads/pallas_call | solution.py:607
  468.1 13.9 %mlp_grads.15.refs_3_ = bf16[512,1536]{1,0:T(8,128)(2,1)S(1)} custom-call(bf16[4,128,2048]{2,1,0:T(8,128)(2,1)} %bitcast.107, bf16[4,128,2048]{2,1,0:T(8,128)(2,1)} %collective-permute-done.70.refs_1_, bf16[2,128,2048]{2,1,0:T(8,128)(2,1)} %copy-done.51, bf16[2,128,2048]{2,1,0:T(8,128)(2,1)} %collective-permute-done.77.refs_3_, ...), custom_call_target="tpu_custom_call" | custom-call | flops 161061280 | bytes 400000 | tf_op jit(solution)/shard_map/mlp_grads/pallas_call | solution.py:607
  488.1 11.9 %assemble.1 = (f32[512,512]{1,0:T(8,128)}, f32[512,128]{1,0:T(8,128)}, f32[512,128]{1,0:T(8,128)}, f32[512,512]{1,0:T(8,128)}, f32[512,2048]{1,0:T(8,128)}, /*index=5*/f32[512,2048]{1,0:T(8,128)}, f32[2048,512]{1,0:T(8,128)}) custom-call(bf16[512,1536]{1,0:T(8,128)(2,1)} %mlp_grads.12.refs_0_, bf16[512,1536]{1,0:T(8,128)(2,1)} %mlp_grads.14.refs_1_, ...), custom_call_target="tpu_custom_call" | custom-call | bytes 600000 | tf_op jit(solution)/shard_map/assemble/pallas_call | solution.py:698
  (466 shorter events, 195.2 us)
Async XLA Ops:
  7.2 132.6 %all-gather.9.cloned.1.call-start = ((), (), s32[]{:S(2)}) async-start(), calls=%async_computation.4 | async-start | bytes 5242880 | tf_op jit(solution)/shard_map/all_gather | solution.py:777
  12.5 18.5 %collective-permute-start.7 = (bf16[2048,768]{1,0:T(8,128)(2,1)}, bf16[2048,768]{1,0:T(8,128)(2,1)}, u32[]{:S(2)}, u32[]{:S(2)}) collective-permute-start(bf16[2048,768]{1,0:T(8,128)(2,1)} %pad_maximum_fusion.refs_0_), channel_id=1, source_target_pairs={{0,16},{16,0},{1,17},{17,1},{2,18},{18,2},{3,19},{19,3},{4,20},{20... | collective-permute-start | bytes 9437192 | tf_op jit(solution)/shard_map/ppermute | solution.py:69
  12.6 18.4 %collective-permute-start.8 = (bf16[512,2048]{1,0:T(8,128)(2,1)S(1)}, bf16[512,2048]{1,0:T(8,128)(2,1)}, u32[]{:S(2)}, u32[]{:S(2)}) collective-permute-start(bf16[512,2048]{1,0:T(8,128)(2,1)S(1)} %bitcast.112), channel_id=1, source_target_pairs={{0,16},{16,0},{1,17},{17,1},{2,18},{18,2},{3,19},{19,3},{4,20},{20... | collective-permute-start | bytes 6291464 | tf_op jit(solution)/shard_map/ppermute | solution.py:69
  31.1 26.5 %collective-permute-start.15 = (bf16[2048,2048]{1,0:T(8,128)(2,1)}, bf16[2048,2048]{1,0:T(8,128)(2,1)}, u32[]{:S(2)}, u32[]{:S(2)}) collective-permute-start(bf16[2048,2048]{1,0:T(8,128)(2,1)} %bitcast.52), channel_id=1, source_target_pairs={{0,16},{16,0},{1,17},{17,1},{2,18},{18,2},{3,19},{19,3},{4,20},{20... | collective-permute-start | bytes 25165832 | tf_op jit(solution)/shard_map/ppermute | solution.py:69
  38.6 41.8 %collective-permute-start.16 = (bf16[2048,2048]{1,0:T(8,128)(2,1)}, bf16[2048,2048]{1,0:T(8,128)(2,1)}, u32[]{:S(2)}, u32[]{:S(2)}) collective-permute-start(bf16[2048,2048]{1,0:T(8,128)(2,1)} %bitcast.64), channel_id=1, source_target_pairs={{0,16},{16,0},{1,17},{17,1},{2,18},{18,2},{3,19},{19,3},{4,20},{20... | collective-permute-start | bytes 25165832 | tf_op jit(solution)/shard_map/ppermute | solution.py:69
  57.6 22.8 %collective-permute-start.17 = (bf16[2048,2048]{1,0:T(8,128)(2,1)}, bf16[2048,2048]{1,0:T(8,128)(2,1)}, u32[]{:S(2)}, u32[]{:S(2)}) collective-permute-start(bf16[2048,2048]{1,0:T(8,128)(2,1)} %bitcast.76), channel_id=1, source_target_pairs={{0,16},{16,0},{1,17},{17,1},{2,18},{18,2},{3,19},{19,3},{4,20},{20... | collective-permute-start | bytes 25165832 | tf_op jit(solution)/shard_map/ppermute | solution.py:69
  57.6 138.0 %all-gather.11.cloned.1.call-start = ((), (), s32[]{:S(2)}) async-start(), calls=%async_computation.5 | async-start | bytes 2621440 | tf_op jit(solution)/shard_map/all_gather | solution.py:777
  139.8 149.8 %all-gather.13.cloned.1.call-start = ((), (), s32[]{:S(2)}) async-start(), calls=%async_computation.6 | async-start | bytes 5242880 | tf_op jit(solution)/shard_map/all_gather | solution.py:777
  195.7 174.5 %all-gather.15.cloned.1.call-start = ((), (), s32[]{:S(2)}) async-start(), calls=%async_computation.7 | async-start | bytes 5242880 | tf_op jit(solution)/shard_map/all_gather | solution.py:777
  225.4 19.6 %collective-permute-start.37 = (bf16[256,2048]{1,0:T(8,128)(2,1)S(1)}, bf16[256,2048]{1,0:T(8,128)(2,1)S(1)}, u32[]{:S(2)}, u32[]{:S(2)}) collective-permute-start(bf16[256,2048]{1,0:T(8,128)(2,1)S(1)} %copy-done.11), channel_id=1, source_target_pairs={{0,16},{16,0},{1,17},{17,1},{2,18},{18,2},{3,19},{19,3},{4,20},{20... | collective-permute-start | bytes 3145736 | tf_op jit(solution)/shard_map/ppermute | solution.py:69
  246.5 43.1 %collective-permute-start.47 = (bf16[128,2048]{1,0:T(8,128)(2,1)}, bf16[128,2048]{1,0:T(8,128)(2,1)}, u32[]{:S(2)}, u32[]{:S(2)}) collective-permute-start(bf16[128,2048]{1,0:T(8,128)(2,1)} %get-tuple-element.391), channel_id=1, source_target_pairs={{0,1},{1,0},{2,3},{3,2},{4,5},{5,4},{6,7},{7,6},{8,9},{9,8},{10,11... | collective-permute-start | bytes 1572872 | tf_op jit(solution)/shard_map/ppermute | solution.py:847
  289.6 134.0 %reduce-scatter.3.cloned.1.call-start = ((), (), s32[]{:S(2)}) async-start(), calls=%async_computation.2 | async-start | bytes 3276800 | tf_op jit(solution)/shard_map/reduce_scatter | solution.py:748
  289.7 26.5 %collective-permute-start.51 = (bf16[4,256,2048]{2,1,0:T(8,128)(2,1)}, bf16[4,256,2048]{2,1,0:T(8,128)(2,1)}, u32[]{:S(2)}, u32[]{:S(2)}) collective-permute-start(bf16[4,256,2048]{2,1,0:T(8,128)(2,1)} %bitcast.93), channel_id=1, source_target_pairs={{0,16},{16,0},{1,17},{17,1},{2,18},{18,2},{3,19},{19,3},{4,20},{20... | collective-permute-start | bytes 12582920 | tf_op jit(solution)/shard_map/ppermute | solution.py:69
  289.8 26.4 %collective-permute-start.52 = (bf16[4,256,2048]{2,1,0:T(8,128)(2,1)}, bf16[4,256,2048]{2,1,0:T(8,128)(2,1)}, u32[]{:S(2)}, u32[]{:S(2)}) collective-permute-start(bf16[4,256,2048]{2,1,0:T(8,128)(2,1)} %bitcast.88), channel_id=1, source_target_pairs={{0,16},{16,0},{1,17},{17,1},{2,18},{18,2},{3,19},{19,3},{4,20},{20... | collective-permute-start | bytes 12582920 | tf_op jit(solution)/shard_map/ppermute | solution.py:69
  308.4 21.6 %collective-permute-start.53 = (bf16[64,2048]{1,0:T(8,128)(2,1)}, bf16[64,2048]{1,0:T(8,128)(2,1)S(1)}, u32[]{:S(2)}, u32[]{:S(2)}) collective-permute-start(bf16[64,2048]{1,0:T(8,128)(2,1)} %get-tuple-element.288.after_ref.d0), channel_id=1, source_target_pairs={{0,1},{1,0},{2,3},{3,2},{4,5},{5,4},{6,7},{7,6},{8,9},{9,8},{10,11... | collective-permute-start | bytes 786440 | tf_op jit(solution)/shard_map/ppermute | solution.py:59
  310.1 20.0 %collective-permute-start.54 = (bf16[64,2048]{1,0:T(8,128)(2,1)}, bf16[64,2048]{1,0:T(8,128)(2,1)S(1)}, u32[]{:S(2)}, u32[]{:S(2)}) collective-permute-start(bf16[64,2048]{1,0:T(8,128)(2,1)} %get-tuple-element.288.after_ref.d0), channel_id=1, source_target_pairs={{0,2},{1,3},{2,0},{3,1},{4,6},{5,7},{6,4},{7,5},{8,10},{9,11},{10,... | collective-permute-start | bytes 786440 | tf_op jit(solution)/shard_map/ppermute | solution.py:59
  310.4 19.7 %collective-permute-start.55 = (bf16[64,2048]{1,0:T(8,128)(2,1)}, bf16[64,2048]{1,0:T(8,128)(2,1)S(1)}, u32[]{:S(2)}, u32[]{:S(2)}) collective-permute-start(bf16[64,2048]{1,0:T(8,128)(2,1)} %get-tuple-element.288.after_ref.d0), channel_id=1, source_target_pairs={{0,3},{1,2},{2,1},{3,0},{4,7},{5,6},{6,5},{7,4},{8,11},{9,10},{10,... | collective-permute-start | bytes 786440 | tf_op jit(solution)/shard_map/ppermute | solution.py:59
  342.8 24.6 %collective-permute-start.61 = (bf16[64,2048]{1,0:T(8,128)(2,1)S(1)}, bf16[64,2048]{1,0:T(8,128)(2,1)}, u32[]{:S(2)}, u32[]{:S(2)}) collective-permute-start(bf16[64,2048]{1,0:T(8,128)(2,1)S(1)} %get-tuple-element.309), channel_id=1, source_target_pairs={{0,1},{1,0},{2,3},{3,2},{4,5},{5,4},{6,7},{7,6},{8,9},{9,8},{10,11... | collective-permute-start | bytes 786440 | tf_op jit(solution)/shard_map/ppermute | solution.py:64
  344.8 22.6 %collective-permute-start.62 = (bf16[64,2048]{1,0:T(8,128)(2,1)S(1)}, bf16[64,2048]{1,0:T(8,128)(2,1)}, u32[]{:S(2)}, u32[]{:S(2)}) collective-permute-start(bf16[64,2048]{1,0:T(8,128)(2,1)S(1)} %get-tuple-element.310), channel_id=1, source_target_pairs={{0,2},{1,3},{2,0},{3,1},{4,6},{5,7},{6,4},{7,5},{8,10},{9,11},{10,... | collective-permute-start | bytes 786440 | tf_op jit(solution)/shard_map/ppermute | solution.py:64
  345.8 21.6 %collective-permute-start.63 = (bf16[64,2048]{1,0:T(8,128)(2,1)S(1)}, bf16[64,2048]{1,0:T(8,128)(2,1)}, u32[]{:S(2)}, u32[]{:S(2)}) collective-permute-start(bf16[64,2048]{1,0:T(8,128)(2,1)S(1)} %get-tuple-element.311), channel_id=1, source_target_pairs={{0,3},{1,2},{2,1},{3,0},{4,7},{5,6},{6,5},{7,4},{8,11},{9,10},{10,... | collective-permute-start | bytes 786440 | tf_op jit(solution)/shard_map/ppermute | solution.py:64
  347.3 40.8 %collective-permute-start.66 = (bf16[512,1536]{1,0:T(8,128)(2,1)S(1)}, bf16[512,1536]{1,0:T(8,128)(2,1)}, u32[]{:S(2)}, u32[]{:S(2)}) collective-permute-start(bf16[512,1536]{1,0:T(8,128)(2,1)S(1)} %mlp_grads.8.refs_10_), channel_id=1, source_target_pairs={{0,16},{16,0},{1,17},{17,1},{2,18},{18,2},{3,19},{19,3},{4,20},{20... | collective-permute-start | bytes 4718600 | tf_op jit(solution)/shard_map/ppermute | solution.py:69
  366.9 21.2 %collective-permute-start.67 = (bf16[512,1536]{1,0:T(8,128)(2,1)}, bf16[512,1536]{1,0:T(8,128)(2,1)}, u32[]{:S(2)}, u32[]{:S(2)}) collective-permute-start(bf16[512,1536]{1,0:T(8,128)(2,1)} %mlp_grads.9.refs_11_), channel_id=1, source_target_pairs={{0,16},{16,0},{1,17},{17,1},{2,18},{18,2},{3,19},{19,3},{4,20},{20... | collective-permute-start | bytes 4718600 | tf_op jit(solution)/shard_map/ppermute | solution.py:69
  370.2 113.1 %reduce-scatter.5.cloned.1.call-start = ((), (), s32[]{:S(2)}) async-start(), calls=%async_computation.3 | async-start | bytes 3276800 | tf_op jit(solution)/shard_map/reduce_scatter | solution.py:748
  370.3 38.1 %collective-permute-start.72 = (bf16[4,256,2048]{2,1,0:T(8,128)(2,1)}, bf16[4,256,2048]{2,1,0:T(8,128)(2,1)}, u32[]{:S(2)}, u32[]{:S(2)}) collective-permute-start(bf16[4,256,2048]{2,1,0:T(8,128)(2,1)} %bitcast.98), channel_id=1, source_target_pairs={{0,16},{16,0},{1,17},{17,1},{2,18},{18,2},{3,19},{19,3},{4,20},{20... | collective-permute-start | bytes 12582920 | tf_op jit(solution)/shard_map/ppermute | solution.py:69
  370.5 17.7 %collective-permute-start.65 = (bf16[128,2048]{1,0:T(8,128)(2,1)S(1)}, bf16[128,2048]{1,0:T(8,128)(2,1)}, u32[]{:S(2)}, u32[]{:S(2)}) collective-permute-start(bf16[128,2048]{1,0:T(8,128)(2,1)S(1)} %copy-done.66), channel_id=1, source_target_pairs={{0,1},{1,0},{2,3},{3,2},{4,5},{5,4},{6,7},{7,6},{8,9},{9,8},{10,11... | collective-permute-start | bytes 1572872 | tf_op jit(solution)/shard_map/ppermute | solution.py:900
  388.3 20.1 %collective-permute-start.70 = (bf16[4,128,2048]{2,1,0:T(8,128)(2,1)}, bf16[4,128,2048]{2,1,0:T(8,128)(2,1)}, u32[]{:S(2)}, u32[]{:S(2)}) collective-permute-start(bf16[4,128,2048]{2,1,0:T(8,128)(2,1)} %bitcast.103), channel_id=1, source_target_pairs={{0,16},{16,0},{1,17},{17,1},{2,18},{18,2},{3,19},{19,3},{4,20},{20... | collective-permute-start | bytes 6291464 | tf_op jit(solution)/shard_map/ppermute | solution.py:69
  403.3 20.0 %collective-permute-start.74 = (bf16[512,1536]{1,0:T(8,128)(2,1)S(1)}, bf16[512,1536]{1,0:T(8,128)(2,1)}, u32[]{:S(2)}, u32[]{:S(2)}) collective-permute-start(bf16[512,1536]{1,0:T(8,128)(2,1)S(1)} %mlp_grads.11.refs_13_), channel_id=1, source_target_pairs={{0,16},{16,0},{1,17},{17,1},{2,18},{18,2},{3,19},{19,3},{4,20},{20... | collective-permute-start | bytes 4718600 | tf_op jit(solution)/shard_map/ppermute | solution.py:69
  405.1 18.2 %collective-permute-start.73 = (f32[2,4,1,128]{3,2,1,0:T(1,128)S(1)}, f32[2,4,1,128]{3,2,1,0:T(1,128)S(1)}, u32[]{:S(2)}, u32[]{:S(2)}) collective-permute-start(f32[2,4,1,128]{3,2,1,0:T(1,128)S(1)} %broadcast_select_fusion.8), channel_id=1, source_target_pairs={{0,1},{1,0},{2,3},{3,2},{4,5},{5,4},{6,7},{7,6},{8,9},{9,8},{10,11... | collective-permute-start | bytes 12296 | tf_op jit(solution)/shard_map/ppermute | solution.py:892
  438.5 21.2 %collective-permute-start.79 = (bf16[512,1536]{1,0:T(8,128)(2,1)S(1)}, bf16[512,1536]{1,0:T(8,128)(2,1)}, u32[]{:S(2)}, u32[]{:S(2)}) collective-permute-start(bf16[512,1536]{1,0:T(8,128)(2,1)S(1)} %mlp_grads.13.refs_2_), channel_id=1, source_target_pairs={{0,16},{16,0},{1,17},{17,1},{2,18},{18,2},{3,19},{19,3},{4,20},{20... | collective-permute-start | bytes 4718600 | tf_op jit(solution)/shard_map/ppermute | solution.py:69
  440.4 19.2 %collective-permute-start.82 = (bf16[64,2048]{1,0:T(8,128)(2,1)S(1)}, bf16[64,2048]{1,0:T(8,128)(2,1)S(1)}, u32[]{:S(2)}, u32[]{:S(2)}) collective-permute-start(bf16[64,2048]{1,0:T(8,128)(2,1)S(1)} %copy-done.46), channel_id=1, source_target_pairs={{0,3},{1,2},{2,1},{3,0},{4,7},{5,6},{6,5},{7,4},{8,11},{9,10},{10,... | collective-permute-start | bytes 786440 | tf_op jit(solution)/shard_map/ppermute | solution.py:64
  459.6 22.5 %collective-permute-start.85 = (bf16[512,1536]{1,0:T(8,128)(2,1)}, bf16[512,1536]{1,0:T(8,128)(2,1)}, u32[]{:S(2)}, u32[]{:S(2)}) collective-permute-start(bf16[512,1536]{1,0:T(8,128)(2,1)} %mlp_grads.14.refs_1_), channel_id=1, source_target_pairs={{0,16},{16,0},{1,17},{17,1},{2,18},{18,2},{3,19},{19,3},{4,20},{20... | collective-permute-start | bytes 4718600 | tf_op jit(solution)/shard_map/ppermute | solution.py:69
  460.6 21.5 %collective-permute-start.86 = (bf16[512,640]{1,0:T(8,128)(2,1)}, bf16[512,640]{1,0:T(8,128)(2,1)S(1)}, u32[]{:S(2)}, u32[]{:S(2)}) collective-permute-start(bf16[512,640]{1,0:T(8,128)(2,1)} %reduce-scatter.3.cloned.1.call-done.refs_14_), channel_id=1, source_target_pairs={{0,16},{16,0},{1,17},{17,1},{2,18},{18,2},{3,19},{19,3},{4,20},{20... | collective-permute-start | bytes 1966088 | tf_op jit(solution)/shard_map/ppermute | solution.py:69
  (176 other events, 1352.9 us)
Sparse Core Ops, SparseCore 0:
  57.7 81.5 all-gather.8
  141.4 44.7 all-gather.10
  195.8 78.4 all-gather.12
  289.8 78.8 all-gather.14
  371.3 50.6 reduce-scatter.2
  424.8 51.7 reduce-scatter.4

commit v4 on v3

--- a/solution.py
+++ b/solution.py
@@ -372,10 +372,10 @@
 
 
 def mlp_fwd_kernel(
-    x0, x1, x2, x3, wg, wu, wd, p0, p1, p2, p3, gate_out, up_out, x_kept, x_all, total, sems
+    x0, x1, x2, x3, wg, wu, wd, p0, p1, p2, p3, gate_out, up_out, x_kept, x_rest, x_all, total, sems
 ):
     rows = x0.shape[0]
-    held = Rows((x0, x1, x2, x3), x_all, sems, (x_kept, (0, 2)))
+    held = Rows((x0, x1, x2, x3), x_all, sems, (x_kept, (0, 2)), (x_rest, (1, 3)))
     held.ready()
 
     def step(f, first):
@@ -400,7 +400,7 @@
     return pl.pallas_call(
         mlp_fwd_kernel,
         in_specs=[HBM] * 4 + [VMEM] * 3,
-        out_specs=[VMEM] * 6 + [HBM],
+        out_specs=[VMEM] * 6 + [HBM] * 2,
         scratch_shapes=[
             pltpu.VMEM((whole, depth), BF),
             pltpu.VMEM((whole, depth), F32),
@@ -408,7 +408,7 @@
         ],
         out_shape=[shaped((rows, depth), BF)] * 4
         + [shaped((whole, units), BF)] * 2
-        + [far((whole // 2, depth))],
+        + [far((whole // 2, depth))] * 2,
         compiler_params=pltpu.CompilerParams(vmem_limit_bytes=12 * MIB),
         cost_estimate=cost(6 * whole * units * depth, 30e6),
         name="mlp_fwd",
@@ -525,11 +525,12 @@
 PIECE = 512
 
 
-def mlp_grads_kernel(layer, f, first, last, x_orders, g_orders, *refs):
+def mlp_grads_kernel(layer, f, first, last, has_prior, x_orders, g_orders, *refs):
     n_x, n_g = len(x_orders), len(g_orders)
     x_refs, g_refs, refs = refs[:n_x], refs[n_x : n_x + n_g], refs[n_x + n_g :]
-    *weights, out = refs[:7]
-    wg, wu, wd, x_all, g_all, total, w_sems, sems = refs[7:]
+    weights, refs = refs[:6], refs[6:]
+    prior, refs = (refs[0], refs[1:]) if has_prior else (None, refs)
+    out, wg, wu, wd, x_all, g_all, total, w_sems, sems = refs
     share = out.shape[0]
     units = weights[0].shape[1]
     mine = lax.axis_index("section") == layer
@@ -540,9 +541,9 @@
     def chunk(p, slot):
         moves = []
         for to, arrays, orders in ((x_all, x_refs, x_orders), (g_all, g_refs, g_orders)):
-            for a, (half, order) in zip(arrays, orders):
+            for a, (half, order, *relative) in zip(arrays, orders):
                 rows = a.shape[1] // len(order)
-                at = p if a.shape[0] > last - first else p - first
+                at = lax.rem(p - lax.axis_index("dp") + a.shape[0], a.shape[0]) if relative else p
                 for n, place in enumerate(order):
                     target = to.at[slot, pl.ds((half * 4 + place) * rows, rows), :]
                     source = a.at[at, pl.ds(n * rows, rows), :]
@@ -568,7 +569,7 @@
 
     for copy in chunk(first, 0):
         copy.start()
-    total[...] = jnp.zeros_like(total)
+    total[...] = prior[...].astype(F32) if has_prior else jnp.zeros_like(total)
     for copy in copies(*weights[0::2]):
         copy.wait()
 
@@ -599,16 +600,16 @@
     out[...] = total[...].astype(BF)
 
 
-def mlp_grads(layer, f, part, xs, gs, pairs):
+def mlp_grads(layer, f, span, xs, gs, pairs, prior=()):
     groups, _, depth = xs[0][0].shape
-    first, last = part * (groups // 2), (part + 1) * (groups // 2)
+    first, last = span
     rows = sum(a.shape[1] for a, _ in xs)
     share = depth // groups
     return pl.pallas_call(
         functools.partial(
-            mlp_grads_kernel, layer, f, first, last, [o for _, o in xs], [o for _, o in gs]
+            mlp_grads_kernel, layer, f, first, last, bool(prior), [o for _, o in xs], [o for _, o in gs]
         ),
-        in_specs=[HBM] * (len(xs) + len(gs) + 6),
+        in_specs=[HBM] * (len(xs) + len(gs) + 6) + [VMEM] * len(prior),
         out_specs=VMEM,
         out_shape=shaped((share, 3 * PIECE), BF),
         scratch_shapes=[
@@ -622,26 +623,24 @@
             pltpu.SemaphoreType.DMA((2, 16)),
         ],
         compiler_params=pltpu.CompilerParams(vmem_limit_bytes=50 * MIB),
-        cost_estimate=cost(3 * rows * groups * PIECE * (depth + share), 20e6),
+        cost_estimate=cost(6 * rows * (last - first) * PIECE * (depth + share), 20e6),
         name="mlp_grads",
-    )(*in_hbm(*[a for a, _ in xs], *[a for a, _ in gs], *[w for pair in pairs for w in pair]))
+    )(*in_hbm(*[a for a, _ in xs], *[a for a, _ in gs], *[w for pair in pairs for w in pair]), *prior)
 
 
 def assemble_kernel(n, *refs):
-    sources, outs, scratch = refs[: 4 * (n + 1)], refs[4 * (n + 1) : 4 * (n + 1) + 7], refs[4 * (n + 1) + 7 :]
+    shares, refs = refs[:2], refs[2:]
+    sources, outs, scratch = refs[: 4 * n], refs[4 * n : 4 * n + 7], refs[4 * n + 7 :]
     q_out, k_out, v_out, o_out, gate_out, up_out, down_out = outs
     held, attn, in_rows, wide, tall, flat, sems, out_sems = scratch
     sec = lax.axis_index("section")
 
     def fetches(layer):
-        mine = sources[layer * 2 * (n + 1) : (layer + 1) * 2 * (n + 1)]
-        moves = []
-        for side in range(2):
-            for f in range(n + 1):
-                source = mine[side * (n + 1) + f]
-                target = held.at[side, f] if f < n else attn.at[side]
-                moves.append(pltpu.make_async_copy(source, target, sems.at[len(moves)]))
-        return moves
+        mine = sources[layer * 2 * n : (layer + 1) * 2 * n]
+        width = attn.shape[2]
+        pairs = [(shares[side].at[:, pl.ds(layer * width, width)], attn.at[side]) for side in range(2)]
+        pairs += [(mine[side * n + f], held.at[side, f]) for side in range(2) for f in range(n)]
+        return [pltpu.make_async_copy(a, to, sems.at[k]) for k, (a, to) in enumerate(pairs)]
 
     for layer in range(2):
 
@@ -673,10 +672,10 @@
     leave(in_rows.at[:, pl.ds(q + k, k)], v_out)
     for kind, (target, out) in enumerate(((wide.at[0], gate_out), (wide.at[1], up_out), (tall, down_out))):
         for side, half in enumerate(halves):
-            for f in range(n // 2):
+            for f in range(n):
                 at = pl.ds(pl.multiple_of(half * half_units + f * PIECE, PIECE), PIECE)
                 cut = slice(kind * PIECE, (kind + 1) * PIECE)
-                tile = held[side, 2 * f, :, cut].astype(F32) + held[side, 2 * f + 1, :, cut].astype(F32)
+                tile = held[side, f, :, cut].astype(F32)
                 if kind < 2:
                     target[:, at] = tile
                 else:
@@ -686,13 +685,13 @@
         move.wait()
 
 
-def assemble(layers, width, narrow, units):
+def assemble(shares, layers, width, narrow, units):
     n = len(layers[0][0])
-    share, attn_width = layers[0][1].shape
+    share, attn_width = shares[0].shape[0], shares[0].shape[1] // 2
     depth_out = 2 * attn_width - width - 2 * narrow
-    sources = []
-    for tiles, part, other_tiles, other_part in layers:
-        sources += [*tiles, part, *other_tiles, other_part]
+    sources = [*shares]
+    for tiles, other_tiles in layers:
+        sources += [*tiles, *other_tiles]
     shapes = [(share, width), (share, narrow), (share, narrow), (depth_out, share)]
     shapes += [(share, units), (share, units), (units, share)]
     return pl.pallas_call(
@@ -716,8 +715,8 @@
     )(*in_hbm(*sources))
 
 
-def attend_grads_kernel(x_own, x_other, d_own, d_other, m_own, m_other, a_own, a_other, out):
-    sec = lax.axis_index("section")
+def attend_grads_kernel(x_own, x_other, d_own, d_other, m_own, m_other, a_own, a_other, *refs):
+    out, sec = refs[-1], lax.axis_index("section")
     at = 0
     for left_own, left_other, own, other in (
         (x_own, x_other, d_own, d_other),
@@ -727,21 +726,22 @@
         half = pl.ds(pl.multiple_of(sec * width, width), width)
         out[:, at : at + width] = (tn(left_own[...], own[:, half]) + tn(left_other[...], other[:, half])).astype(BF)
         at += width
-
-
-def attend_grads(x, d_qkv, d_mid, att):
+    if len(refs) > 1:
+        out[:, at:] = refs[0][...]
+
+
+def attend_grads(x, d_qkv, d_mid, att, *before):
     depth, width = x.shape[1], (d_qkv.shape[1] + att.shape[1]) // 2
     terms = [x, swapped(x), d_qkv, swapped(d_qkv), d_mid, swapped(d_mid), att, swapped(att)]
-    both = pl.pallas_call(
+    return pl.pallas_call(
         attend_grads_kernel,
-        in_specs=[VMEM] * 8,
+        in_specs=[VMEM] * (8 + len(before)),
         out_specs=VMEM,
-        out_shape=shaped((depth, width), BF),
+        out_shape=shaped((depth, width + sum(b.shape[1] for b in before)), BF),
         compiler_params=pltpu.CompilerParams(vmem_limit_bytes=14 * MIB),
         cost_estimate=cost(4 * x.size * width, 6e6),
         name="attend_grads",
-    )(*terms)
-    return both
+    )(*terms, *before)
 
 
 def summed_over_groups(x):
@@ -802,14 +802,6 @@
 
     g_low = jnp.where((own_places < length)[:, None], cot, jnp.zeros_like(cot))
 
-    def for_layer(pair):
-        keep, send = jnp.where(first, pair[0], pair[1]), jnp.where(first, pair[1], pair[0])
-        return keep, swapped(send)
-
-    def both(pair):
-        keep, came = for_layer(pair)
-        return [jnp.where(first, keep, came), jnp.where(first, came, keep)]
-
     attn_mine = [jnp.concatenate(mine[:3], axis=1), mine[3]]
     attn_w = [(w, swapped(tied(w, other_gains))) for w in attn_mine]
     attn_cuts = [(0, w.shape[0]) for w in attn_mine]
@@ -827,7 +819,7 @@
     mlp_cuts = [(0, w.shape[0]) for w in mine[4:]]
     mid0, normed = add_norm(tok, scatter_rows(parts, size), mlp_gains[0], False)
     *weights_in, token = prefetch(0, mlp_w, mlp_cuts, normed)
-    *parts, gate0, up0, x_half = mlp_fwd(gather_rows(normed, size), weights_in)
+    *parts, gate0, up0, x_half, x_rest = mlp_fwd(gather_rows(normed, size), weights_in)
     act0, normed = add_norm(mid0, scatter_rows(parts, size), attn_gains[1], True)
 
     *weights_in, token = prefetch(1, attn_w, attn_cuts, normed)
@@ -841,10 +833,12 @@
     parts[0] = tied(parts[0], half_x0)
     all_x1 = over_groups(tied(x_all, half_x0, parts[0]))
     d_mid, d_mid_low, mlp_part1 = norm_back(mid1, scatter_rows(parts, size), mlp_gains[1], g_low)
-    rest_x0 = []
+    rest_x0 = [x_rest]
 
     def with_chunk(blocks, results):
-        chunk = lax.ppermute(tied(half_x0[len(rest_x0)], *blocks), "tensor", partners(size)[0])
+        group = lax.rem(lax.axis_index("dp") + len(rest_x0), groups)
+        sent = lax.dynamic_index_in_dim(half_x0, group, 0, False)
+        chunk = lax.ppermute(tied(sent, *blocks), "tensor", partners(size)[0])
         results, chunk = lax.optimization_barrier((list(results), chunk))
         rest_x0.append(chunk)
         return results
@@ -858,29 +852,24 @@
     d_stream1, d_low, attn_part1 = norm_back(act0, came, attn_gains[1], d_mid)
 
     *weights_in, token = prefetch(0, mlp_w, mlp_cuts, d_low)
-    *parts, g_all = with_chunk([token], mlp_bwd(gather_rows(d_low, size), gate0, up0, weights_in))
+    *parts, g_rows = with_chunk([token], mlp_bwd(gather_rows(d_low, size), gate0, up0, weights_in))
     parts[0] = tied(parts[0], all_x1)
-    all_g0 = over_groups(tied(g_all, all_x1, parts[0]))
+    all_g0 = over_groups(tied(g_rows, all_x1, parts[0]))
     x1, g1 = from_both_cores((all_x1, ALL)), from_both_cores((all_g1, ALL))
-    pieces = [(f, part) for f in range(mine[4].shape[1] // (2 * PIECE)) for part in range(2)]
-    tiles1 = []
-
-    def piece1(*after):
-        f, part = pieces[len(tiles1)]
-        tiles1.append(mlp_grads(1, f, part, [(tied(a, *after), o) for a, o in x1], g1, mlp_w))
-        return tiles1[-1]
-
+    middle = groups // 2
     d_mid, d_mid_low, mlp_part0 = norm_back(mid0, scatter_rows(parts, size), mlp_gains[0], d_low)
     *weights_in, token = prefetch(0, attn_w, attn_cuts, d_mid_low)
     blocks = gather_rows(d_mid_low, size)
-    blocks[0] = tied(blocks[0], piece1(d_mid_low, token))
+    late_x1 = [(tied(a, d_mid_low, token), o) for a, o in x1]
+    tile = mlp_grads(1, 0, (0, middle), late_x1, g1, mlp_w)
+    blocks[0] = tied(blocks[0], tile)
     *parts, dm, dqkv = with_chunk(blocks, attend_bwd(blocks, (q0, k0, v0), weights_in, tables))
-    attn_terms0 = attend_grads(x_attn0, dqkv, dm, att0)
+    attn_terms = attend_grads(x_attn0, dqkv, dm, att0, attn_terms1)
+    late_x1 = [(tied(a, parts[0], attn_terms), o) for a, o in x1]
+    tile = mlp_grads(1, 0, (middle, groups), late_x1, g1, mlp_w, (tile,))
     came = scatter_rows(parts, size)
-    came[0] = tied(came[0], piece1(parts[0], attn_terms0))
+    came[0] = tied(came[0], tile)
     d_stream0, _, attn_part0 = norm_back(tok, came, attn_gains[0], d_mid)
-
-    attn_share1 = summed_over_groups(tied(attn_terms1, all_g0, d_stream0))
 
     def beside(results, *transfers):
         results, transfers = lax.optimization_barrier((results, list(transfers)))
@@ -892,16 +881,7 @@
         came = lax.ppermute(jnp.where(upper, low, high), axis, [(a, a ^ bit) for a in range(count)])
         return jnp.where(upper, high, low), came
 
-    keep, came = for_layer(
-        [jnp.concatenate(p, axis=0) for p in ((attn_part0, mlp_part0), (attn_part1, mlp_part1))]
-    )
-    others1, others0 = [swapped(tile) for tile in tiles1], []
-    while len(rest_x0) < groups:
-        rest_x0.append(lax.ppermute(tied(half_x0[len(rest_x0)], d_stream0), "tensor", partners(size)[0]))
-    tiles1[2], (came, rest_x0[-1], *others1) = beside(piece1(d_stream0), came, rest_x0[-1], *others1)
-    shares = (keep + came).reshape(2, groups, size, depth // (groups * size))
     steps = [("tensor", size, 2, 1 << n) for n in reversed(range(size.bit_length() - 1))]
-    steps += [("dp", groups, 1, 1 << n) for n in reversed(range(groups.bit_length() - 1))]
 
     def step_beside(results, *transfers):
         nonlocal shares
@@ -910,53 +890,72 @@
         shares = keep + came
         return results, transfers
 
-    at = groups // 2
-    x0, g0 = from_both_cores((half_x0, (0, 2))), from_both_cores((all_g0, ALL))
-    x0_rest = [
-        from_both_cores((jnp.stack(part), (1, 3))) for part in (rest_x0[:at], rest_x0[at:])
-    ]
-    tiles1[3:], (moved,) = step_beside([piece1(tiles1[2])], swapped(tiles1[2]))
+    while len(rest_x0) < groups:
+        with_chunk([d_stream0], [])
+    rest_own = jnp.stack(rest_x0)
+    attn_share = summed_over_groups(tied(attn_terms, all_g0, d_stream0))
+    shares = jnp.concatenate([attn_part0, mlp_part0, attn_part1, mlp_part1], axis=0)
+    shares = shares.reshape(2, 2 * groups, size, depth // (groups * size))
+    stream_keep, stream_send = jnp.where(first, d_stream0, d_stream1), jnp.where(first, d_stream1, d_stream0)
+    late_x1 = [(tied(a, d_stream0), o) for a, o in x1]
+    tiles1 = [tile]
+    tile, (rest_other, g0_other, moved, stream_came) = step_beside(
+        mlp_grads(1, 1, (0, groups), late_x1, g1, mlp_w),
+        swapped(rest_own),
+        swapped(tied(all_g0, d_stream0)),
+        swapped(tile),
+        swapped(stream_send),
+    )
+    tiles1.append(tile)
+    others1 = [moved]
+    x0 = from_both_cores((half_x0, (0, 2))) + [(rest_own, (0, (1, 3), True)), (rest_other, (1, (1, 3), True))]
+    g0 = [(all_g0, (0, ALL)), (g0_other, (1, ALL))]
+    act_terms = scatter_rows([tied(p, tile) for p in parts1], size)
+    tile, (moved, *act_terms[1:]) = step_beside(
+        mlp_grads(0, 0, (0, groups), [(tied(a, tile), o) for a, o in x0], g0, mlp_w),
+        swapped(tiles1[1]),
+        *act_terms[1:],
+    )
+    tiles0 = [tile]
     others1.append(moved)
-    order0 = [(f, part) for part in range(2) for f in range(len(pieces) // 2)]
-
-    def piece0(after):
-        f, part = order0[len(tiles0)]
-        tiles0.append(mlp_grads(0, f, part, [(tied(a, after), o) for a, o in x0 + x0_rest[part]], g0, mlp_w))
-        return tiles0[-1]
-
-    tiles0 = []
-    tiles0[0:], (moved,) = step_beside([piece0(tiles1[3])], swapped(tiles1[3]))
-    others1.append(moved)
-    attn_share0 = summed_over_groups(tied(attn_terms0, attn_share1, tiles0[0]))
-    tiles0[1:], (moved,) = step_beside([piece0(tiles0[0])], swapped(tiles0[0]))
-    others0.append(moved)
-    act_terms = scatter_rows([tied(p, tiles0[0]) for p in parts1], size)
-    tiles0[2:], (moved, *act_terms[1:]) = step_beside(
-        [piece0(tiles0[1])], swapped(tiles0[1]), *act_terms[1:]
-    )
-    others0.append(moved)
+    act1, _ = add_norm(mid1, act_terms, attn_gains[1], True)
+    act_keep, act_send = jnp.where(first, act0, act1), jnp.where(first, act1, act0)
     while steps:
         step_beside([])
-    act1, _ = add_norm(mid1, act_terms, attn_gains[1], True)
-    shares = shares.reshape(2, -1)
-    tiles0[3:], (moved, swapped_share1) = beside(
-        [piece0(tied(tiles0[2], act1, shares))], swapped(tiles0[2]), swapped(attn_share1)
-    )
-    others0.append(moved)
-    attn_share0 = tied(attn_share0, tiles0[3])
-    others0.append(swapped(tiles0[3]))
-    others0 = [others0[order0.index(piece)] for piece in pieces]
-    tiles0 = [tiles0[order0.index(piece)] for piece in pieces]
-    layers = [
-        (tiles0, attn_share0, others0, swapped(attn_share0)),
-        (tiles1, attn_share1, others1, swapped_share1),
-    ]
-    weight_grads = assemble(layers, mine[0].shape[1], mine[1].shape[1], mine[4].shape[1])
-    acts, input_grads = (act0, act1), (d_stream0, d_stream1)
+    by_group, i = shares.reshape(4, groups, -1), lax.axis_index("dp")
+    group_terms = []
+    for k in range(1, groups):
+        sent = lax.dynamic_index_in_dim(by_group, lax.rem(i + k, groups), 1, False)
+        group_terms.append(lax.ppermute(sent, "dp", [(j, (j + k) % groups) for j in range(groups)]))
+    tile, (moved, act_came, *group_terms) = beside(
+        mlp_grads(0, 1, (0, groups), [(tied(a, tile, act_keep), o) for a, o in x0], g0, mlp_w),
+        swapped(tiles0[0]),
+        swapped(act_send),
+        *group_terms,
+    )
+    shares = lax.dynamic_index_in_dim(by_group, i, 1, False) + sum(group_terms)
+    shares = shares.reshape(2, 2, -1)
+    shares_keep, shares_send = jnp.where(first, shares[0], shares[1]), jnp.where(first, shares[1], shares[0])
+    tiles0.append(tile)
+    others0 = [moved, swapped(tile)]
+    attn_share = tied(attn_share, tile)
+    attn_other = swapped(attn_share)
+    weight_grads = assemble(
+        (attn_share, attn_other),
+        ((tiles0, others0), (tiles1, others1)),
+        mine[0].shape[1],
+        mine[1].shape[1],
+        mine[4].shape[1],
+    )
+    weight_grads, (shares,) = beside(weight_grads, swapped(shares_send))
+    shares = shares_keep + shares
+
+    def both(keep, came):
+        return jnp.stack([jnp.where(first, keep, came), jnp.where(first, came, keep)])[None]
 
     return (
-        jnp.stack(both(acts))[None],
-        jnp.stack(both(input_grads))[None],
+        both(act_keep, act_came),
+        both(stream_keep, stream_came),
         shares[0:1],
         shares[1:2],
         *[grad[None] for grad in weight_grads],

time: 513 us -> 494 us (0.963)
  Pallas kernels: 263 us -> 241 us
    pallas_call x8 -> x5, Pallas kernels: 115 us -> 99.3 us  [mlp_grads(): pl.pallas_call(functools.partial(mlp_grads_kernel, layer, f, first, last,...]
    ppermute x4 -> x6, starting transfers between devices: 3.4 us -> 10.8 us  [the longest x3 5.55 us: local(): lax.ppermute(sent, 'dp', [(j, (j + k) % groups) for j in range(groups)])]
    ppermute x33 -> x27, waiting for transfers between devices: 10.6 us -> 6.87 us  [swapped(): return lax.ppermute(x, 'section', [(0, 1), (1, 0)])]
    unnamed x226 -> x218, local copies, waits for them, and re-layouts: 32.5 us -> 34 us
  transfers between devices with their start and end apart: 95 -> 88, of which waited for: 26 -> 29; matrix products, arithmetic and copies ran while one was open for 4% -> 4% of each run, Pallas kernels for 50% -> 50%
where the time goes in v4:
time: 494 us; the launch traced here: 488 us
  Pallas kernels  241 us (49%)
  waiting for transfers between devices  99.4 us (20%)
  starting transfers between devices  74.9 us (15%)
  local copies, waits for them, and re-layouts  39.8 us (8%)
  other arithmetic  16.5 us (3%)
  between operations  15.6 us (3%)
    pallas_call x5, Pallas kernels, mlp_grads(): pl.pallas_call(functools.partial(mlp_grads_kernel, layer, f, first, last,...  99.3 us
    ppermute x24, waiting for transfers between devices, scatter_rows(): lax.ppermute(part, 'tensor', pairs)  59.9 us
    pallas_call x7, Pallas kernels, prefetch(): pl.pallas_call(functools.partial(prefetch_kernel, layer, cuts), out_shape...  39.3 us
    unnamed x218, local copies, waits for them, and re-layouts  34 us
    ppermute x24, starting transfers between devices, gather_rows(): return [x] + [lax.ppermute(x, 'tensor', pairs) for pairs in partners(size)]  28.6 us
    ppermute x24, waiting for transfers between devices, gather_rows(): return [x] + [lax.ppermute(x, 'tensor', pairs) for pairs in partners(size)]  28 us
    ppermute x24, starting transfers between devices, scatter_rows(): lax.ppermute(part, 'tensor', pairs)  25.7 us
    pallas_call x2, Pallas kernels, attend_bwd(): pl.pallas_call(attend_bwd_kernel, out_shape=(block,) * 4 + (far((whole, d...  19.2 us
  transfers between devices with their start and end apart: 88, of which 29 were waited for; matrix products, arithmetic and copies ran while one was open for 4% of the time, Pallas kernels for 50%

profile of v4, /device:TPU:0, one launch (start us, length us, event | category | flops | bytes accessed | tf_op | source)
XLA Modules:
  0.0 487.5 jit_solution(18011446422482363795)
XLA Ops:
  8.6 4.0 pad_maximum_fusion.refs_0_
  25.1 6.9 %collective-permute-done.2.g2 = bf16[64,2048]{1,0:T(8,128)(2,1)} collective-permute-done((bf16[64,2048]{1,0:T(8,128)(2,1)S(1)}, bf16[64,2048]{1,0:T(8,128)(2,1)}, u32[]{:S(2)}, u32[]{:S(2)}) %collective-permute-start.2) | collective-permute-done | bytes 262176 | tf_op jit(solution)/shard_map/ppermute | solution.py:59
  42.9 4.3 collective-permute-done.5.x2
  49.5 5.8 %attend_fwd.2 = (bf16[64,2048]{1,0:T(8,128)(2,1)S(1)}, bf16[64,2048]{1,0:T(8,128)(2,1)S(1)}, bf16[64,2048]{1,0:T(8,128)(2,1)S(1)}, bf16[64,2048]{1,0:T(8,128)(2,...) custom-call(bf16[64,2048]{1,0:T(8,128)(2,1)} %norm.1.after_ref.x0, ...), custom_call_target="tpu_custom_call" | custom-call | flops 100000000 | bytes 240000 | tf_op jit(solution)/shard_map/attend_fwd/pallas_call | solution.py:277
  61.7 10.8 %collective-permute-done.10.c_ref = bf16[64,2048]{1,0:T(8,128)(2,1)S(1)} collective-permute-done((bf16[64,2048]{1,0:T(8,128)(2,1)S(1)}, bf16[64,2048]{1,0:T(8,128)(2,1)S(1)}, u32[]{:S(2)}, u32[]{:S(2)}) %collective-permute-start.10) | collective-permute-done | bytes 262176 | tf_op jit(solution)/shard_map/ppermute | solution.py:64
  81.3 8.9 %prefetch.8 = (bf16[2048,2048]{1,0:T(8,128)(2,1)S(1)}, bf16[2048,2048]{1,0:T(8,128)(2,1)S(1)}, bf16[2048,2048]{1,0:T(8,128)(2,1)S(1)}, f32[8,128]{1,0:T(8,128)}) custom-call(bf16[64,2048]{1,0:T(8,128)(2,1)S(1)} %copy-done.9, bf16[2048,2048]{1,0:T(8,128)(2,1)} %bitcast.68, bf16[2048,2048]{1,0:T(8,128)(2,1)} %collective-permute-done.15.refs_1_.refs_5_.refs_7_, ...), custom_call_target="tpu_custom_call" | custom-call | bytes 1006632 | tf_op jit(solution)/shard_map/prefetch/pallas_call | solution.py:169
  91.8 8.9 %mlp_fwd.1 = (bf16[64,2048]{1,0:T(8,128)(2,1)S(1)}, bf16[64,2048]{1,0:T(8,128)(2,1)S(1)}, bf16[64,2048]{1,0:T(8,128)(2,1)S(1)}, bf16[64,2048]{1,0:T(8,128)(2,1)S...) custom-call(bf16[64,2048]{1,0:T(8,128)(2,1)} %get-tuple-element.202., ...), custom_call_target="tpu_custom_call" | custom-call | flops 128849016 | bytes 600000 | tf_op jit(solution)/shard_map/mlp_fwd/pallas_call | solution.py:400
  107.5 5.1 %collective-permute-done.18.b_ref = bf16[64,2048]{1,0:T(8,128)(2,1)S(1)} collective-permute-done((bf16[64,2048]{1,0:T(8,128)(2,1)S(1)}, bf16[64,2048]{1,0:T(8,128)(2,1)S(1)}, u32[]{:S(2)}, u32[]{:S(2)}) %collective-permute-start.18) | collective-permute-done | bytes 262176 | tf_op jit(solution)/shard_map/ppermute | solution.py:64
  112.6 4.1 collective-permute-done.19.c_ref
  127.7 3.8 collective-permute-done.22.x2
  132.3 5.8 %attend_fwd.3 = (bf16[64,2048]{1,0:T(8,128)(2,1)S(1)}, bf16[64,2048]{1,0:T(8,128)(2,1)S(1)}, bf16[64,2048]{1,0:T(8,128)(2,1)S(1)}, bf16[64,2048]{1,0:T(8,128)(2,...) custom-call(bf16[64,2048]{1,0:T(8,128)(2,1)} %get-tuple-element.214., ...), custom_call_target="tpu_custom_call" | custom-call | flops 100000000 | bytes 240000 | tf_op jit(solution)/shard_map/attend_fwd/pallas_call | solution.py:277
  143.5 5.7 %collective-permute-done.24.b_ref = bf16[64,2048]{1,0:T(8,128)(2,1)S(1)} collective-permute-done((bf16[64,2048]{1,0:T(8,128)(2,1)S(1)}, bf16[64,2048]{1,0:T(8,128)(2,1)S(1)}, u32[]{:S(2)}, u32[]{:S(2)}) %collective-permute-start.24) | collective-permute-done | bytes 262176 | tf_op jit(solution)/shard_map/ppermute | solution.py:64
  149.2 5.7 %collective-permute-done.25.c_ref = bf16[64,2048]{1,0:T(8,128)(2,1)S(1)} collective-permute-done((bf16[64,2048]{1,0:T(8,128)(2,1)S(1)}, bf16[64,2048]{1,0:T(8,128)(2,1)S(1)}, u32[]{:S(2)}, u32[]{:S(2)}) %collective-permute-start.25) | collective-permute-done | bytes 262176 | tf_op jit(solution)/shard_map/ppermute | solution.py:64
  162.5 8.9 %prefetch.10 = (bf16[2048,2048]{1,0:T(8,128)(2,1)S(1)}, bf16[2048,2048]{1,0:T(8,128)(2,1)S(1)}, bf16[2048,2048]{1,0:T(8,128)(2,1)S(1)}, f32[8,128]{1,0:T(8,128)}) custom-call(bf16[64,2048]{1,0:T(8,128)(2,1)S(1)} %copy-done.16, bf16[2048,2048]{1,0:T(8,128)(2,1)} %bitcast.69, bf16[2048,2048]{1,0:T(8,128)(2,1)} %collective-permute-done.15.refs_1_.refs_5_.refs_7_, ...), custom_call_target="tpu_custom_call" | custom-call | bytes 1006632 | tf_op jit(solution)/shard_map/prefetch/pallas_call | solution.py:169
  172.7 17.5 %mlp_both.1 = (bf16[64,2048]{1,0:T(8,128)(2,1)S(1)}, bf16[64,2048]{1,0:T(8,128)(2,1)S(1)}, bf16[64,2048]{1,0:T(8,128)(2,1)S(1)}, bf16[64,2048]{1,0:T(8,128)(2,1)...) custom-call(bf16[64,2048]{1,0:T(8,128)(2,1)} %get-tuple-element.223., ...), custom_call_target="tpu_custom_call" | custom-call | flops 257698032 | bytes 600000 | tf_op jit(solution)/shard_map/mlp_both/pallas_call | solution.py:505
  196.5 5.3 %collective-permute-done.30.b_ref = bf16[64,2048]{1,0:T(8,128)(2,1)} collective-permute-done((bf16[64,2048]{1,0:T(8,128)(2,1)}, bf16[64,2048]{1,0:T(8,128)(2,1)}, u32[]{:S(2)}, u32[]{:S(2)}) %collective-permute-start.30) | collective-permute-done | bytes 262176 | tf_op jit(solution)/shard_map/ppermute | solution.py:64
  201.8 4.0 collective-permute-done.31.c_ref
  215.9 4.1 collective-permute-done.34.d2
  222.1 3.2 prefetch.11
  225.4 9.2 %attend_bwd.2 = (bf16[64,2048]{1,0:T(8,128)(2,1)S(1)}, bf16[64,2048]{1,0:T(8,128)(2,1)S(1)}, bf16[64,2048]{1,0:T(8,128)(2,1)S(1)}, bf16[64,2048]{1,0:T(8,128)(2,...) custom-call(bf16[64,2048]{1,0:T(8,128)(2,1)} %get-tuple-element.237.after_ref.d0, ...), custom_call_target="tpu_custom_call" | custom-call | flops 140000000 | bytes 280000 | tf_op jit(solution)/shard_map/attend_bwd/pallas_call | solution.py:358
  246.0 6.6 %collective-permute-done.42.c_ref = bf16[64,2048]{1,0:T(8,128)(2,1)S(1)} collective-permute-done((bf16[64,2048]{1,0:T(8,128)(2,1)S(1)}, bf16[64,2048]{1,0:T(8,128)(2,1)S(1)}, u32[]{:S(2)}, u32[]{:S(2)}) %collective-permute-start.42) | collective-permute-done | bytes 262176 | tf_op jit(solution)/shard_map/ppermute | solution.py:64
  261.3 8.9 %prefetch.12 = (bf16[2048,2048]{1,0:T(8,128)(2,1)S(1)}, bf16[2048,2048]{1,0:T(8,128)(2,1)S(1)}, bf16[2048,2048]{1,0:T(8,128)(2,1)S(1)}, f32[8,128]{1,0:T(8,128)}) custom-call(bf16[64,2048]{1,0:T(8,128)(2,1)S(1)} %copy-done.7, bf16[2048,2048]{1,0:T(8,128)(2,1)} %bitcast.70, bf16[2048,2048]{1,0:T(8,128)(2,1)} %collective-permute-done.15.refs_1_.refs_5_.refs_7_, ...), custom_call_target="tpu_custom_call" | custom-call | bytes 1006632 | tf_op jit(solution)/shard_map/prefetch/pallas_call | solution.py:169
  273.1 9.8 %mlp_bwd.1 = (bf16[64,2048]{1,0:T(8,128)(2,1)S(1)}, bf16[64,2048]{1,0:T(8,128)(2,1)S(1)}, bf16[64,2048]{1,0:T(8,128)(2,1)S(1)}, bf16[64,2048]{1,0:T(8,128)(2,1)S(1)}, bf16[256,2048]{1,0:T(8,128)(2,1)}) custom-call(bf16[64,2048]{1,0:T(8,128)(2,1)} %get-tuple-element.260.after_ref.g0.res_ref, bf16[64,2048]{1,0:T(8,128)(2,1)} %copy-done.68, ...), custom_call_target="tpu_custom_call" | custom-call | flops 128849016 | bytes 600000 | tf_op jit(solution)/shard_map/mlp_bwd/pallas_call | solution.py:445
  289.1 6.0 %collective-permute-done.48.b_ref = bf16[64,2048]{1,0:T(8,128)(2,1)} collective-permute-done((bf16[64,2048]{1,0:T(8,128)(2,1)}, bf16[64,2048]{1,0:T(8,128)(2,1)}, u32[]{:S(2)}, u32[]{:S(2)}) %collective-permute-start.48) | collective-permute-done | bytes 262176 | tf_op jit(solution)/shard_map/ppermute | solution.py:64
  295.1 5.3 %collective-permute-done.50.d_ref = bf16[64,2048]{1,0:T(8,128)(2,1)} collective-permute-done((bf16[64,2048]{1,0:T(8,128)(2,1)}, bf16[64,2048]{1,0:T(8,128)(2,1)}, u32[]{:S(2)}, u32[]{:S(2)}) %collective-permute-start.50) | collective-permute-done | bytes 262176 | tf_op jit(solution)/shard_map/ppermute | solution.py:64
  310.9 14.0 %mlp_grads.5.refs_10_ = bf16[512,1536]{1,0:T(8,128)(2,1)S(1)} custom-call(bf16[4,256,2048]{2,1,0:T(8,128)(2,1)} %bitcast.99, bf16[4,256,2048]{2,1,0:T(8,128)(2,1)} %collective-permute-done.51.refs_1_, bf16[4,256,2048]{2,1,0:T(8,128)(2,1)} %bitcast.95, bf16[4,256,2048]{2,1,0:T(8,128)(2,1)} %collective-permute-done.52.refs_3_, bf16[2048,2048]{1,0:T(8,128)(2,1)} %bitcast.71, ...), custom_call_target="tpu_custom_call" | custom-call | flops 161061280 | bytes 400000 | tf_op jit(solution)/shard_map/mlp_grads/pallas_call | solution.py:608
  326.4 10.0 %attend_bwd.3 = (bf16[64,2048]{1,0:T(8,128)(2,1)S(1)}, bf16[64,2048]{1,0:T(8,128)(2,1)}, bf16[64,2048]{1,0:T(8,128)(2,1)}, bf16[64,2048]{1,0:T(8,128)(2,1)S(1)},...) custom-call(bf16[64,2048]{1,0:T(8,128)(2,1)} %get-tuple-element.280.after_ref.d0, bf16[64,2048]{1,0:T(8,128)(2,1)} %copy-done.93, ...), custom_call_target="tpu_custom_call" | custom-call | flops 140000000 | bytes 280000 | tf_op jit(solution)/shard_map/attend_bwd/pallas_call | solution.py:358
  349.4 14.0 %mlp_grads.6.refs_6_ = bf16[512,1536]{1,0:T(8,128)(2,1)S(1)} custom-call(bf16[4,256,2048]{2,1,0:T(8,128)(2,1)} %bitcast.100, bf16[4,256,2048]{2,1,0:T(8,128)(2,1)} %collective-permute-done.51.refs_1_, bf16[4,256,2048]{2,1,0:T(8,128)(2,1)} %bitcast.96, bf16[4,256,2048]{2,1,0:T(8,128)(2,1)} %collective-permute-done.52.refs_3_, bf16[2048,2048]{1,0:T(8,128)(2,1)} %bitcast.72, ...), custom_call_target="tpu_custom_call" | custom-call | flops 161061280 | bytes 400000 | tf_op jit(solution)/shard_map/mlp_grads/pallas_call | solution.py:608
  375.1 24.2 %mlp_grads.7.refs_7_ = bf16[512,1536]{1,0:T(8,128)(2,1)} custom-call(bf16[4,256,2048]{2,1,0:T(8,128)(2,1)} %bitcast.101, bf16[4,256,2048]{2,1,0:T(8,128)(2,1)} %collective-permute-done.51.refs_1_, bf16[4,256,2048]{2,1,0:T(8,128)(2,1)} %bitcast.97, bf16[4,256,2048]{2,1,0:T(8,128)(2,1)} %collective-permute-done.52.refs_3_, bf16[2048,2048]{1,0:T(8,128)(2,1)} %bitcast.73, ...), custom_call_target="tpu_custom_call" | custom-call | flops 322122560 | bytes 400000 | tf_op jit(solution)/shard_map/mlp_grads/pallas_call | solution.py:608
  405.6 23.1 %mlp_grads.8.refs_2_ = bf16[512,1536]{1,0:T(8,128)(2,1)S(1)} custom-call(bf16[4,128,2048]{2,1,0:T(8,128)(2,1)} %bitcast.112, bf16[4,128,2048]{2,1,0:T(8,128)(2,1)} %collective-permute-done.69.refs_1_, bf16[4,128,2048]{2,1,0:T(8,128)(2,1)} %pad_maximum_fusion.1.refs_2_, bf16[4,128,2048]{2,1,0:T(8,128)(2,1)} %collective-permute-done.65.refs_3_, ...), custom_call_target="tpu_custom_call" | custom-call | flops 322122560 | bytes 400000 | tf_op jit(solution)/shard_map/mlp_grads/pallas_call | solution.py:608
  439.8 24.1 %mlp_grads.9.refs_3_ = bf16[512,1536]{1,0:T(8,128)(2,1)} custom-call(bf16[4,128,2048]{2,1,0:T(8,128)(2,1)} %bitcast.113, bf16[4,128,2048]{2,1,0:T(8,128)(2,1)} %collective-permute-done.69.refs_1_, bf16[4,128,2048]{2,1,0:T(8,128)(2,1)} %pad_maximum_fusion.1.refs_2_, bf16[4,128,2048]{2,1,0:T(8,128)(2,1)} %collective-permute-done.65.refs_3_, ...), custom_call_target="tpu_custom_call" | custom-call | flops 322122560 | bytes 400000 | tf_op jit(solution)/shard_map/mlp_grads/pallas_call | solution.py:608
  470.5 9.4 %assemble.1 = (f32[512,512]{1,0:T(8,128)}, f32[512,128]{1,0:T(8,128)}, f32[512,128]{1,0:T(8,128)}, f32[512,512]{1,0:T(8,128)}, f32[512,2048]{1,0:T(8,128)}, /*index=5*/f32[512,2048]{1,0:T(8,128)}, f32[2048,512]{1,0:T(8,128)}) custom-call(bf16[512,1280]{1,0:T(8,128)(2,1)} %reduce-scatter.2.cloned.1.call-done.refs_0_, bf16[512,1280]{1,0:T(8,128)(2,1)} %copy-done.58, ...), custom_call_target="tpu_custom_call" | custom-call | bytes 600000 | tf_op jit(solution)/shard_map/assemble/pallas_call | solution.py:697
  (438 shorter events, 184.7 us)
Async XLA Ops:
  7.2 132.4 %all-gather.9.cloned.1.call-start = ((), (), s32[]{:S(2)}) async-start(), calls=%async_computation.2 | async-start | bytes 5242880 | tf_op jit(solution)/shard_map/all_gather | solution.py:777
  12.5 19.5 %collective-permute-start.7 = (bf16[2048,768]{1,0:T(8,128)(2,1)}, bf16[2048,768]{1,0:T(8,128)(2,1)}, u32[]{:S(2)}, u32[]{:S(2)}) collective-permute-start(bf16[2048,768]{1,0:T(8,128)(2,1)} %pad_maximum_fusion.refs_0_), channel_id=1, source_target_pairs={{0,16},{16,0},{1,17},{17,1},{2,18},{18,2},{3,19},{19,3},{4,20},{20... | collective-permute-start | bytes 9437192 | tf_op jit(solution)/shard_map/ppermute | solution.py:69
  32.1 25.8 %collective-permute-start.15 = (bf16[2048,2048]{1,0:T(8,128)(2,1)}, bf16[2048,2048]{1,0:T(8,128)(2,1)}, u32[]{:S(2)}, u32[]{:S(2)}) collective-permute-start(bf16[2048,2048]{1,0:T(8,128)(2,1)} %bitcast.67), channel_id=1, source_target_pairs={{0,16},{16,0},{1,17},{17,1},{2,18},{18,2},{3,19},{19,3},{4,20},{20... | collective-permute-start | bytes 25165832 | tf_op jit(solution)/shard_map/ppermute | solution.py:69
  39.7 40.6 %collective-permute-start.16 = (bf16[2048,2048]{1,0:T(8,128)(2,1)}, bf16[2048,2048]{1,0:T(8,128)(2,1)}, u32[]{:S(2)}, u32[]{:S(2)}) collective-permute-start(bf16[2048,2048]{1,0:T(8,128)(2,1)} %bitcast.76), channel_id=1, source_target_pairs={{0,16},{16,0},{1,17},{17,1},{2,18},{18,2},{3,19},{19,3},{4,20},{20... | collective-permute-start | bytes 25165832 | tf_op jit(solution)/shard_map/ppermute | solution.py:69
  57.9 22.5 %collective-permute-start.17 = (bf16[2048,2048]{1,0:T(8,128)(2,1)}, bf16[2048,2048]{1,0:T(8,128)(2,1)}, u32[]{:S(2)}, u32[]{:S(2)}) collective-permute-start(bf16[2048,2048]{1,0:T(8,128)(2,1)} %bitcast.85), channel_id=1, source_target_pairs={{0,16},{16,0},{1,17},{17,1},{2,18},{18,2},{3,19},{19,3},{4,20},{20... | collective-permute-start | bytes 25165832 | tf_op jit(solution)/shard_map/ppermute | solution.py:69
  57.9 134.5 %all-gather.11.cloned.1.call-start = ((), (), s32[]{:S(2)}) async-start(), calls=%async_computation.3 | async-start | bytes 2621440 | tf_op jit(solution)/shard_map/all_gather | solution.py:777
  139.6 145.3 %all-gather.13.cloned.1.call-start = ((), (), s32[]{:S(2)}) async-start(), calls=%async_computation.4 | async-start | bytes 5242880 | tf_op jit(solution)/shard_map/all_gather | solution.py:777
  192.5 174.6 %all-gather.15.cloned.1.call-start = ((), (), s32[]{:S(2)}) async-start(), calls=%async_computation.5 | async-start | bytes 5242880 | tf_op jit(solution)/shard_map/all_gather | solution.py:777
  239.9 45.1 %collective-permute-start.47 = (bf16[128,2048]{1,0:T(8,128)(2,1)}, bf16[128,2048]{1,0:T(8,128)(2,1)}, u32[]{:S(2)}, u32[]{:S(2)}) collective-permute-start(bf16[128,2048]{1,0:T(8,128)(2,1)} %get-tuple-element.374), channel_id=1, source_target_pairs={{0,1},{1,0},{2,3},{3,2},{4,5},{5,4},{6,7},{7,6},{8,9},{9,8},{10,11... | collective-permute-start | bytes 1572872 | tf_op jit(solution)/shard_map/ppermute | solution.py:841
  285.0 179.1 %reduce-scatter.2.cloned.1.call-start = ((), (), s32[]{:S(2)}) async-start(), calls=%async_computation.1 | async-start | bytes 6553600 | tf_op jit(solution)/shard_map/reduce_scatter | solution.py:748
  285.1 25.8 %collective-permute-start.51 = (bf16[4,256,2048]{2,1,0:T(8,128)(2,1)}, bf16[4,256,2048]{2,1,0:T(8,128)(2,1)}, u32[]{:S(2)}, u32[]{:S(2)}) collective-permute-start(bf16[4,256,2048]{2,1,0:T(8,128)(2,1)} %bitcast.98), channel_id=1, source_target_pairs={{0,16},{16,0},{1,17},{17,1},{2,18},{18,2},{3,19},{19,3},{4,20},{20... | collective-permute-start | bytes 12582920 | tf_op jit(solution)/shard_map/ppermute | solution.py:69
  285.1 25.8 %collective-permute-start.52 = (bf16[4,256,2048]{2,1,0:T(8,128)(2,1)}, bf16[4,256,2048]{2,1,0:T(8,128)(2,1)}, u32[]{:S(2)}, u32[]{:S(2)}) collective-permute-start(bf16[4,256,2048]{2,1,0:T(8,128)(2,1)} %bitcast.94), channel_id=1, source_target_pairs={{0,16},{16,0},{1,17},{17,1},{2,18},{18,2},{3,19},{19,3},{4,20},{20... | collective-permute-start | bytes 12582920 | tf_op jit(solution)/shard_map/ppermute | solution.py:69
  303.2 21.8 %collective-permute-start.53 = (bf16[64,2048]{1,0:T(8,128)(2,1)}, bf16[64,2048]{1,0:T(8,128)(2,1)S(1)}, u32[]{:S(2)}, u32[]{:S(2)}) collective-permute-start(bf16[64,2048]{1,0:T(8,128)(2,1)} %get-tuple-element.280.after_ref.d0), channel_id=1, source_target_pairs={{0,1},{1,0},{2,3},{3,2},{4,5},{5,4},{6,7},{7,6},{8,9},{9,8},{10,11... | collective-permute-start | bytes 786440 | tf_op jit(solution)/shard_map/ppermute | solution.py:59
  304.4 20.6 %collective-permute-start.54 = (bf16[64,2048]{1,0:T(8,128)(2,1)}, bf16[64,2048]{1,0:T(8,128)(2,1)S(1)}, u32[]{:S(2)}, u32[]{:S(2)}) collective-permute-start(bf16[64,2048]{1,0:T(8,128)(2,1)} %get-tuple-element.280.after_ref.d0), channel_id=1, source_target_pairs={{0,2},{1,3},{2,0},{3,1},{4,6},{5,7},{6,4},{7,5},{8,10},{9,11},{10,... | collective-permute-start | bytes 786440 | tf_op jit(solution)/shard_map/ppermute | solution.py:59
  338.1 25.3 %collective-permute-start.61 = (bf16[64,2048]{1,0:T(8,128)(2,1)}, bf16[64,2048]{1,0:T(8,128)(2,1)S(1)}, u32[]{:S(2)}, u32[]{:S(2)}) collective-permute-start(bf16[64,2048]{1,0:T(8,128)(2,1)} %get-tuple-element.301), channel_id=1, source_target_pairs={{0,1},{1,0},{2,3},{3,2},{4,5},{5,4},{6,7},{7,6},{8,9},{9,8},{10,11... | collective-permute-start | bytes 786440 | tf_op jit(solution)/shard_map/ppermute | solution.py:64
  340.4 23.1 %collective-permute-start.62 = (bf16[64,2048]{1,0:T(8,128)(2,1)}, bf16[64,2048]{1,0:T(8,128)(2,1)}, u32[]{:S(2)}, u32[]{:S(2)}) collective-permute-start(bf16[64,2048]{1,0:T(8,128)(2,1)} %get-tuple-element.302), channel_id=1, source_target_pairs={{0,2},{1,3},{2,0},{3,1},{4,6},{5,7},{6,4},{7,5},{8,10},{9,11},{10,... | collective-permute-start | bytes 786440 | tf_op jit(solution)/shard_map/ppermute | solution.py:64
  341.5 22.0 %collective-permute-start.63 = (bf16[64,2048]{1,0:T(8,128)(2,1)S(1)}, bf16[64,2048]{1,0:T(8,128)(2,1)}, u32[]{:S(2)}, u32[]{:S(2)}) collective-permute-start(bf16[64,2048]{1,0:T(8,128)(2,1)S(1)} %get-tuple-element.303), channel_id=1, source_target_pairs={{0,3},{1,2},{2,1},{3,0},{4,7},{5,6},{6,5},{7,4},{8,11},{9,10},{10,... | collective-permute-start | bytes 786440 | tf_op jit(solution)/shard_map/ppermute | solution.py:64
  367.2 32.9 %collective-permute-start.66 = (bf16[4,256,2048]{2,1,0:T(8,128)(2,1)}, bf16[4,256,2048]{2,1,0:T(8,128)(2,1)}, u32[]{:S(2)}, u32[]{:S(2)}) collective-permute-start(bf16[4,256,2048]{2,1,0:T(8,128)(2,1)} %bitcast.107), channel_id=1, source_target_pairs={{0,16},{16,0},{1,17},{17,1},{2,18},{18,2},{3,19},{19,3},{4,20},{20... | collective-permute-start | bytes 12582920 | tf_op jit(solution)/shard_map/ppermute | solution.py:69
  370.3 29.0 %collective-permute-start.65 = (bf16[4,128,2048]{2,1,0:T(8,128)(2,1)}, bf16[4,128,2048]{2,1,0:T(8,128)(2,1)}, u32[]{:S(2)}, u32[]{:S(2)}) collective-permute-start(bf16[4,128,2048]{2,1,0:T(8,128)(2,1)} %pad_maximum_fusion.1.refs_2_), channel_id=1, source_target_pairs={{0,16},{16,0},{1,17},{17,1},{2,18},{18,2},{3,19},{19,3},{4,20},{20... | collective-permute-start | bytes 6291464 | tf_op jit(solution)/shard_map/ppermute | solution.py:69
  370.7 28.6 %collective-permute-start.67 = (bf16[512,1536]{1,0:T(8,128)(2,1)S(1)}, bf16[512,1536]{1,0:T(8,128)(2,1)}, u32[]{:S(2)}, u32[]{:S(2)}) collective-permute-start(bf16[512,1536]{1,0:T(8,128)(2,1)S(1)} %mlp_grads.6.refs_6_), channel_id=1, source_target_pairs={{0,16},{16,0},{1,17},{17,1},{2,18},{18,2},{3,19},{19,3},{4,20},{20... | collective-permute-start | bytes 4718600 | tf_op jit(solution)/shard_map/ppermute | solution.py:69
  370.8 33.3 %collective-permute-start.69 = (bf16[4,128,2048]{2,1,0:T(8,128)(2,1)}, bf16[4,128,2048]{2,1,0:T(8,128)(2,1)}, u32[]{:S(2)}, u32[]{:S(2)}) collective-permute-start(bf16[4,128,2048]{2,1,0:T(8,128)(2,1)} %bitcast.111), channel_id=1, source_target_pairs={{0,16},{16,0},{1,17},{17,1},{2,18},{18,2},{3,19},{19,3},{4,20},{20... | collective-permute-start | bytes 6291464 | tf_op jit(solution)/shard_map/ppermute | solution.py:69
  375.1 24.2 %collective-permute-start.68 = (f32[64,2048]{1,0:T(8,128)S(1)}, f32[64,2048]{1,0:T(8,128)S(1)}, u32[]{:S(2)}, u32[]{:S(2)}) collective-permute-start(f32[64,2048]{1,0:T(8,128)S(1)} %broadcast_select_fusion.3), channel_id=1, source_target_pairs={{0,16},{16,0},{1,17},{17,1},{2,18},{18,2},{3,19},{19,3},{4,20},{20... | collective-permute-start | bytes 1572872 | tf_op jit(solution)/shard_map/ppermute | solution.py:69
  400.1 29.4 %collective-permute-start.71 = (bf16[512,1536]{1,0:T(8,128)(2,1)}, bf16[512,1536]{1,0:T(8,128)(2,1)}, u32[]{:S(2)}, u32[]{:S(2)}) collective-permute-start(bf16[512,1536]{1,0:T(8,128)(2,1)} %mlp_grads.7.refs_7_), channel_id=1, source_target_pairs={{0,16},{16,0},{1,17},{17,1},{2,18},{18,2},{3,19},{19,3},{4,20},{20... | collective-permute-start | bytes 4718600 | tf_op jit(solution)/shard_map/ppermute | solution.py:69
  400.5 28.2 %collective-permute-start.74 = (bf16[64,2048]{1,0:T(8,128)(2,1)S(1)}, bf16[64,2048]{1,0:T(8,128)(2,1)S(1)}, u32[]{:S(2)}, u32[]{:S(2)}) collective-permute-start(bf16[64,2048]{1,0:T(8,128)(2,1)S(1)} %copy-done.46), channel_id=1, source_target_pairs={{0,3},{1,2},{2,1},{3,0},{4,7},{5,6},{6,5},{7,4},{8,11},{9,10},{10,... | collective-permute-start | bytes 786440 | tf_op jit(solution)/shard_map/ppermute | solution.py:64
  402.4 26.3 %collective-permute-start.73 = (bf16[64,2048]{1,0:T(8,128)(2,1)S(1)}, bf16[64,2048]{1,0:T(8,128)(2,1)S(1)}, u32[]{:S(2)}, u32[]{:S(2)}) collective-permute-start(bf16[64,2048]{1,0:T(8,128)(2,1)S(1)} %copy-done.44), channel_id=1, source_target_pairs={{0,2},{1,3},{2,0},{3,1},{4,6},{5,7},{6,4},{7,5},{8,10},{9,11},{10,... | collective-permute-start | bytes 786440 | tf_op jit(solution)/shard_map/ppermute | solution.py:64
  403.4 25.3 %collective-permute-start.72 = (bf16[64,2048]{1,0:T(8,128)(2,1)S(1)}, bf16[64,2048]{1,0:T(8,128)(2,1)S(1)}, u32[]{:S(2)}, u32[]{:S(2)}) collective-permute-start(bf16[64,2048]{1,0:T(8,128)(2,1)S(1)} %copy-done.42), channel_id=1, source_target_pairs={{0,1},{1,0},{2,3},{3,2},{4,5},{5,4},{6,7},{7,6},{8,9},{9,8},{10,11... | collective-permute-start | bytes 786440 | tf_op jit(solution)/shard_map/ppermute | solution.py:64
  404.1 24.6 %collective-permute-start.70 = (f32[2,8,1,128]{3,2,1,0:T(1,128)S(1)}, f32[2,8,1,128]{3,2,1,0:T(1,128)S(1)}, u32[]{:S(2)}, u32[]{:S(2)}) collective-permute-start(f32[2,8,1,128]{3,2,1,0:T(1,128)S(1)} %broadcast_select_fusion.5), channel_id=1, source_target_pairs={{0,1},{1,0},{2,3},{3,2},{4,5},{5,4},{6,7},{7,6},{8,9},{9,8},{10,11... | collective-permute-start | bytes 24584 | tf_op jit(solution)/shard_map/ppermute | solution.py:881
  430.2 33.6 %collective-permute-start.75 = (bf16[512,1536]{1,0:T(8,128)(2,1)S(1)}, bf16[512,1536]{1,0:T(8,128)(2,1)}, u32[]{:S(2)}, u32[]{:S(2)}) collective-permute-start(bf16[512,1536]{1,0:T(8,128)(2,1)S(1)} %mlp_grads.8.refs_2_), channel_id=1, source_target_pairs={{0,16},{16,0},{1,17},{17,1},{2,18},{18,2},{3,19},{19,3},{4,20},{20... | collective-permute-start | bytes 4718600 | tf_op jit(solution)/shard_map/ppermute | solution.py:69
  433.6 30.3 %collective-permute-start.76 = (bf16[64,2048]{1,0:T(8,128)(2,1)S(1)}, bf16[64,2048]{1,0:T(8,128)(2,1)S(1)}, u32[]{:S(2)}, u32[]{:S(2)}) collective-permute-start(bf16[64,2048]{1,0:T(8,128)(2,1)S(1)} %get-tuple-element.380), channel_id=1, source_target_pairs={{0,16},{16,0},{1,17},{17,1},{2,18},{18,2},{3,19},{19,3},{4,20},{20... | collective-permute-start | bytes 786440 | tf_op jit(solution)/shard_map/ppermute | solution.py:69
  434.2 29.6 %collective-permute-start.77 = (f32[4,128]{1,0:T(4,128)S(1)}, f32[4,128]{1,0:T(4,128)S(1)}, u32[]{:S(2)}, u32[]{:S(2)}) collective-permute-start(f32[4,128]{1,0:T(4,128)S(1)} %bitcast.125), channel_id=1, source_target_pairs={{0,4},{4,8},{8,12},{12,0},{1,5},{5,9},{9,13},{13,1},{2,6},{6,10},{... | collective-permute-start | bytes 6152 | tf_op jit(solution)/shard_map/ppermute | solution.py:929
  437.3 26.5 %collective-permute-start.78 = (f32[4,128]{1,0:T(4,128)S(1)}, f32[4,128]{1,0:T(4,128)S(1)}, u32[]{:S(2)}, u32[]{:S(2)}) collective-permute-start(f32[4,128]{1,0:T(4,128)S(1)} %bitcast.124), channel_id=1, source_target_pairs={{0,8},{4,12},{8,0},{12,4},{1,9},{5,13},{9,1},{13,5},{2,10},{6,14},... | collective-permute-start | bytes 6152 | tf_op jit(solution)/shard_map/ppermute | solution.py:929
  438.1 25.8 %collective-permute-start.79 = (f32[4,128]{1,0:T(4,128)S(1)}, f32[4,128]{1,0:T(4,128)S(1)}, u32[]{:S(2)}, u32[]{:S(2)}) collective-permute-start(f32[4,128]{1,0:T(4,128)S(1)} %bitcast.123), channel_id=1, source_target_pairs={{0,12},{4,0},{8,4},{12,8},{1,13},{5,1},{9,5},{13,9},{2,14},{6,2},{... | collective-permute-start | bytes 6152 | tf_op jit(solution)/shard_map/ppermute | solution.py:929
  (165 other events, 1540.7 us)
Sparse Core Ops, SparseCore 0:
  58.0 81.5 all-gather.8
  141.8 44.4 all-gather.10
  192.6 78.2 all-gather.12
  285.1 80.0 all-gather.14
  367.4 93.3 reduce-scatter.1

commit v5 on v4

--- a/solution.py
+++ b/solution.py
@@ -16,7 +16,7 @@
 HBM = pl.BlockSpec(memory_space=pltpu.HBM)
 ANY = pl.BlockSpec(memory_space=pl.ANY)
 MIB = 1024 * 1024
-SHRINK = 50
+SHRINK = 20
 
 
 def nn(a, b):

time: 494 us -> 494 us (level)
  no operation moved by 1% of the time
where the time goes in v5:
time: 494 us; the launch traced here: 488 us
  Pallas kernels  241 us (49%)
  waiting for transfers between devices  99.4 us (20%)
  starting transfers between devices  74.9 us (15%)
  local copies, waits for them, and re-layouts  39.8 us (8%)
  other arithmetic  16.5 us (3%)
  between operations  15.6 us (3%)
    pallas_call x5, Pallas kernels, mlp_grads(): pl.pallas_call(functools.partial(mlp_grads_kernel, layer, f, first, last,...  99.3 us
    ppermute x24, waiting for transfers between devices, scatter_rows(): lax.ppermute(part, 'tensor', pairs)  59.9 us
    pallas_call x7, Pallas kernels, prefetch(): pl.pallas_call(functools.partial(prefetch_kernel, layer, cuts), out_shape...  39.3 us
    unnamed x218, local copies, waits for them, and re-layouts  34 us
    ppermute x24, starting transfers between devices, gather_rows(): return [x] + [lax.ppermute(x, 'tensor', pairs) for pairs in partners(size)]  28.6 us
    ppermute x24, waiting for transfers between devices, gather_rows(): return [x] + [lax.ppermute(x, 'tensor', pairs) for pairs in partners(size)]  28 us
    ppermute x24, starting transfers between devices, scatter_rows(): lax.ppermute(part, 'tensor', pairs)  25.7 us
    pallas_call x2, Pallas kernels, attend_bwd(): pl.pallas_call(attend_bwd_kernel, out_shape=(block,) * 4 + (far((whole, d...  19.2 us
  transfers between devices with their start and end apart: 88, of which 29 were waited for; matrix products, arithmetic and copies ran while one was open for 4% of the time, Pallas kernels for 50%

profile of v5, /device:TPU:0, one launch (start us, length us, event | category | flops | bytes accessed | tf_op | source)
XLA Modules:
  0.0 487.5 jit_solution(1812000185977774126)
XLA Ops:
  8.6 4.0 pad_maximum_fusion.refs_0_
  25.1 6.9 %collective-permute-done.2.g2 = bf16[64,2048]{1,0:T(8,128)(2,1)} collective-permute-done((bf16[64,2048]{1,0:T(8,128)(2,1)S(1)}, bf16[64,2048]{1,0:T(8,128)(2,1)}, u32[]{:S(2)}, u32[]{:S(2)}) %collective-permute-start.2) | collective-permute-done | bytes 262176 | tf_op jit(solution)/shard_map/ppermute | solution.py:59
  42.9 4.3 collective-permute-done.5.x2
  49.5 5.8 %attend_fwd.2 = (bf16[64,2048]{1,0:T(8,128)(2,1)S(1)}, bf16[64,2048]{1,0:T(8,128)(2,1)S(1)}, bf16[64,2048]{1,0:T(8,128)(2,1)S(1)}, bf16[64,2048]{1,0:T(8,128)(2,...) custom-call(bf16[64,2048]{1,0:T(8,128)(2,1)} %norm.1.after_ref.x0, ...), custom_call_target="tpu_custom_call" | custom-call | flops 250000000 | bytes 600000 | tf_op jit(solution)/shard_map/attend_fwd/pallas_call | solution.py:277
  61.7 10.8 %collective-permute-done.10.c_ref = bf16[64,2048]{1,0:T(8,128)(2,1)S(1)} collective-permute-done((bf16[64,2048]{1,0:T(8,128)(2,1)S(1)}, bf16[64,2048]{1,0:T(8,128)(2,1)S(1)}, u32[]{:S(2)}, u32[]{:S(2)}) %collective-permute-start.10) | collective-permute-done | bytes 262176 | tf_op jit(solution)/shard_map/ppermute | solution.py:64
  81.3 8.9 %prefetch.8 = (bf16[2048,2048]{1,0:T(8,128)(2,1)S(1)}, bf16[2048,2048]{1,0:T(8,128)(2,1)S(1)}, bf16[2048,2048]{1,0:T(8,128)(2,1)S(1)}, f32[8,128]{1,0:T(8,128)}) custom-call(bf16[64,2048]{1,0:T(8,128)(2,1)S(1)} %copy-done.9, bf16[2048,2048]{1,0:T(8,128)(2,1)} %bitcast.68, bf16[2048,2048]{1,0:T(8,128)(2,1)} %collective-permute-done.15.refs_1_.refs_5_.refs_7_, ...), custom_call_target="tpu_custom_call" | custom-call | bytes 2516582 | tf_op jit(solution)/shard_map/prefetch/pallas_call | solution.py:169
  91.8 8.9 %mlp_fwd.1 = (bf16[64,2048]{1,0:T(8,128)(2,1)S(1)}, bf16[64,2048]{1,0:T(8,128)(2,1)S(1)}, bf16[64,2048]{1,0:T(8,128)(2,1)S(1)}, bf16[64,2048]{1,0:T(8,128)(2,1)S...) custom-call(bf16[64,2048]{1,0:T(8,128)(2,1)} %get-tuple-element.202., ...), custom_call_target="tpu_custom_call" | custom-call | flops 322122560 | bytes 1500000 | tf_op jit(solution)/shard_map/mlp_fwd/pallas_call | solution.py:400
  107.5 5.1 %collective-permute-done.18.b_ref = bf16[64,2048]{1,0:T(8,128)(2,1)S(1)} collective-permute-done((bf16[64,2048]{1,0:T(8,128)(2,1)S(1)}, bf16[64,2048]{1,0:T(8,128)(2,1)S(1)}, u32[]{:S(2)}, u32[]{:S(2)}) %collective-permute-start.18) | collective-permute-done | bytes 262176 | tf_op jit(solution)/shard_map/ppermute | solution.py:64
  112.6 4.1 collective-permute-done.19.c_ref
  127.7 3.8 collective-permute-done.22.x2
  132.3 5.8 %attend_fwd.3 = (bf16[64,2048]{1,0:T(8,128)(2,1)S(1)}, bf16[64,2048]{1,0:T(8,128)(2,1)S(1)}, bf16[64,2048]{1,0:T(8,128)(2,1)S(1)}, bf16[64,2048]{1,0:T(8,128)(2,...) custom-call(bf16[64,2048]{1,0:T(8,128)(2,1)} %get-tuple-element.214., ...), custom_call_target="tpu_custom_call" | custom-call | flops 250000000 | bytes 600000 | tf_op jit(solution)/shard_map/attend_fwd/pallas_call | solution.py:277
  143.5 5.7 %collective-permute-done.24.b_ref = bf16[64,2048]{1,0:T(8,128)(2,1)S(1)} collective-permute-done((bf16[64,2048]{1,0:T(8,128)(2,1)S(1)}, bf16[64,2048]{1,0:T(8,128)(2,1)S(1)}, u32[]{:S(2)}, u32[]{:S(2)}) %collective-permute-start.24) | collective-permute-done | bytes 262176 | tf_op jit(solution)/shard_map/ppermute | solution.py:64
  149.2 5.7 %collective-permute-done.25.c_ref = bf16[64,2048]{1,0:T(8,128)(2,1)S(1)} collective-permute-done((bf16[64,2048]{1,0:T(8,128)(2,1)S(1)}, bf16[64,2048]{1,0:T(8,128)(2,1)S(1)}, u32[]{:S(2)}, u32[]{:S(2)}) %collective-permute-start.25) | collective-permute-done | bytes 262176 | tf_op jit(solution)/shard_map/ppermute | solution.py:64
  162.5 8.9 %prefetch.10 = (bf16[2048,2048]{1,0:T(8,128)(2,1)S(1)}, bf16[2048,2048]{1,0:T(8,128)(2,1)S(1)}, bf16[2048,2048]{1,0:T(8,128)(2,1)S(1)}, f32[8,128]{1,0:T(8,128)}) custom-call(bf16[64,2048]{1,0:T(8,128)(2,1)S(1)} %copy-done.16, bf16[2048,2048]{1,0:T(8,128)(2,1)} %bitcast.69, bf16[2048,2048]{1,0:T(8,128)(2,1)} %collective-permute-done.15.refs_1_.refs_5_.refs_7_, ...), custom_call_target="tpu_custom_call" | custom-call | bytes 2516582 | tf_op jit(solution)/shard_map/prefetch/pallas_call | solution.py:169
  172.7 17.5 %mlp_both.1 = (bf16[64,2048]{1,0:T(8,128)(2,1)S(1)}, bf16[64,2048]{1,0:T(8,128)(2,1)S(1)}, bf16[64,2048]{1,0:T(8,128)(2,1)S(1)}, bf16[64,2048]{1,0:T(8,128)(2,1)...) custom-call(bf16[64,2048]{1,0:T(8,128)(2,1)} %get-tuple-element.223., ...), custom_call_target="tpu_custom_call" | custom-call | flops 644245120 | bytes 1500000 | tf_op jit(solution)/shard_map/mlp_both/pallas_call | solution.py:505
  196.5 5.3 %collective-permute-done.30.b_ref = bf16[64,2048]{1,0:T(8,128)(2,1)} collective-permute-done((bf16[64,2048]{1,0:T(8,128)(2,1)}, bf16[64,2048]{1,0:T(8,128)(2,1)}, u32[]{:S(2)}, u32[]{:S(2)}) %collective-permute-start.30) | collective-permute-done | bytes 262176 | tf_op jit(solution)/shard_map/ppermute | solution.py:64
  201.8 4.0 collective-permute-done.31.c_ref
  215.9 4.1 collective-permute-done.34.d2
  222.1 3.2 prefetch.11
  225.4 9.2 %attend_bwd.2 = (bf16[64,2048]{1,0:T(8,128)(2,1)S(1)}, bf16[64,2048]{1,0:T(8,128)(2,1)S(1)}, bf16[64,2048]{1,0:T(8,128)(2,1)S(1)}, bf16[64,2048]{1,0:T(8,128)(2,...) custom-call(bf16[64,2048]{1,0:T(8,128)(2,1)} %get-tuple-element.237.after_ref.d0, ...), custom_call_target="tpu_custom_call" | custom-call | flops 350000000 | bytes 700000 | tf_op jit(solution)/shard_map/attend_bwd/pallas_call | solution.py:358
  246.0 6.6 %collective-permute-done.42.c_ref = bf16[64,2048]{1,0:T(8,128)(2,1)S(1)} collective-permute-done((bf16[64,2048]{1,0:T(8,128)(2,1)S(1)}, bf16[64,2048]{1,0:T(8,128)(2,1)S(1)}, u32[]{:S(2)}, u32[]{:S(2)}) %collective-permute-start.42) | collective-permute-done | bytes 262176 | tf_op jit(solution)/shard_map/ppermute | solution.py:64
  261.3 8.9 %prefetch.12 = (bf16[2048,2048]{1,0:T(8,128)(2,1)S(1)}, bf16[2048,2048]{1,0:T(8,128)(2,1)S(1)}, bf16[2048,2048]{1,0:T(8,128)(2,1)S(1)}, f32[8,128]{1,0:T(8,128)}) custom-call(bf16[64,2048]{1,0:T(8,128)(2,1)S(1)} %copy-done.7, bf16[2048,2048]{1,0:T(8,128)(2,1)} %bitcast.70, bf16[2048,2048]{1,0:T(8,128)(2,1)} %collective-permute-done.15.refs_1_.refs_5_.refs_7_, ...), custom_call_target="tpu_custom_call" | custom-call | bytes 2516582 | tf_op jit(solution)/shard_map/prefetch/pallas_call | solution.py:169
  273.1 9.8 %mlp_bwd.1 = (bf16[64,2048]{1,0:T(8,128)(2,1)S(1)}, bf16[64,2048]{1,0:T(8,128)(2,1)S(1)}, bf16[64,2048]{1,0:T(8,128)(2,1)S(1)}, bf16[64,2048]{1,0:T(8,128)(2,1)S(1)}, bf16[256,2048]{1,0:T(8,128)(2,1)}) custom-call(bf16[64,2048]{1,0:T(8,128)(2,1)} %get-tuple-element.260.after_ref.g0.res_ref, bf16[64,2048]{1,0:T(8,128)(2,1)} %copy-done.68, ...), custom_call_target="tpu_custom_call" | custom-call | flops 322122560 | bytes 1500000 | tf_op jit(solution)/shard_map/mlp_bwd/pallas_call | solution.py:445
  289.1 6.0 %collective-permute-done.48.b_ref = bf16[64,2048]{1,0:T(8,128)(2,1)} collective-permute-done((bf16[64,2048]{1,0:T(8,128)(2,1)}, bf16[64,2048]{1,0:T(8,128)(2,1)}, u32[]{:S(2)}, u32[]{:S(2)}) %collective-permute-start.48) | collective-permute-done | bytes 262176 | tf_op jit(solution)/shard_map/ppermute | solution.py:64
  295.1 5.3 %collective-permute-done.50.d_ref = bf16[64,2048]{1,0:T(8,128)(2,1)} collective-permute-done((bf16[64,2048]{1,0:T(8,128)(2,1)}, bf16[64,2048]{1,0:T(8,128)(2,1)}, u32[]{:S(2)}, u32[]{:S(2)}) %collective-permute-start.50) | collective-permute-done | bytes 262176 | tf_op jit(solution)/shard_map/ppermute | solution.py:64
  310.9 14.0 %mlp_grads.5.refs_10_ = bf16[512,1536]{1,0:T(8,128)(2,1)S(1)} custom-call(bf16[4,256,2048]{2,1,0:T(8,128)(2,1)} %bitcast.99, bf16[4,256,2048]{2,1,0:T(8,128)(2,1)} %collective-permute-done.51.refs_1_, bf16[4,256,2048]{2,1,0:T(8,128)(2,1)} %bitcast.95, bf16[4,256,2048]{2,1,0:T(8,128)(2,1)} %collective-permute-done.52.refs_3_, bf16[2048,2048]{1,0:T(8,128)(2,1)} %bitcast.71, ...), custom_call_target="tpu_custom_call" | custom-call | flops 402653184 | bytes 1000000 | tf_op jit(solution)/shard_map/mlp_grads/pallas_call | solution.py:608
  326.4 10.0 %attend_bwd.3 = (bf16[64,2048]{1,0:T(8,128)(2,1)S(1)}, bf16[64,2048]{1,0:T(8,128)(2,1)}, bf16[64,2048]{1,0:T(8,128)(2,1)}, bf16[64,2048]{1,0:T(8,128)(2,1)S(1)},...) custom-call(bf16[64,2048]{1,0:T(8,128)(2,1)} %get-tuple-element.280.after_ref.d0, bf16[64,2048]{1,0:T(8,128)(2,1)} %copy-done.93, ...), custom_call_target="tpu_custom_call" | custom-call | flops 350000000 | bytes 700000 | tf_op jit(solution)/shard_map/attend_bwd/pallas_call | solution.py:358
  349.4 14.0 %mlp_grads.6.refs_6_ = bf16[512,1536]{1,0:T(8,128)(2,1)S(1)} custom-call(bf16[4,256,2048]{2,1,0:T(8,128)(2,1)} %bitcast.100, bf16[4,256,2048]{2,1,0:T(8,128)(2,1)} %collective-permute-done.51.refs_1_, bf16[4,256,2048]{2,1,0:T(8,128)(2,1)} %bitcast.96, bf16[4,256,2048]{2,1,0:T(8,128)(2,1)} %collective-permute-done.52.refs_3_, bf16[2048,2048]{1,0:T(8,128)(2,1)} %bitcast.72, ...), custom_call_target="tpu_custom_call" | custom-call | flops 402653184 | bytes 1000000 | tf_op jit(solution)/shard_map/mlp_grads/pallas_call | solution.py:608
  375.1 24.2 %mlp_grads.7.refs_7_ = bf16[512,1536]{1,0:T(8,128)(2,1)} custom-call(bf16[4,256,2048]{2,1,0:T(8,128)(2,1)} %bitcast.101, bf16[4,256,2048]{2,1,0:T(8,128)(2,1)} %collective-permute-done.51.refs_1_, bf16[4,256,2048]{2,1,0:T(8,128)(2,1)} %bitcast.97, bf16[4,256,2048]{2,1,0:T(8,128)(2,1)} %collective-permute-done.52.refs_3_, bf16[2048,2048]{1,0:T(8,128)(2,1)} %bitcast.73, ...), custom_call_target="tpu_custom_call" | custom-call | flops 805306368 | bytes 1000000 | tf_op jit(solution)/shard_map/mlp_grads/pallas_call | solution.py:608
  405.6 23.1 %mlp_grads.8.refs_2_ = bf16[512,1536]{1,0:T(8,128)(2,1)S(1)} custom-call(bf16[4,128,2048]{2,1,0:T(8,128)(2,1)} %bitcast.112, bf16[4,128,2048]{2,1,0:T(8,128)(2,1)} %collective-permute-done.69.refs_1_, bf16[4,128,2048]{2,1,0:T(8,128)(2,1)} %pad_maximum_fusion.1.refs_2_, bf16[4,128,2048]{2,1,0:T(8,128)(2,1)} %collective-permute-done.65.refs_3_, ...), custom_call_target="tpu_custom_call" | custom-call | flops 805306368 | bytes 1000000 | tf_op jit(solution)/shard_map/mlp_grads/pallas_call | solution.py:608
  439.8 24.1 %mlp_grads.9.refs_3_ = bf16[512,1536]{1,0:T(8,128)(2,1)} custom-call(bf16[4,128,2048]{2,1,0:T(8,128)(2,1)} %bitcast.113, bf16[4,128,2048]{2,1,0:T(8,128)(2,1)} %collective-permute-done.69.refs_1_, bf16[4,128,2048]{2,1,0:T(8,128)(2,1)} %pad_maximum_fusion.1.refs_2_, bf16[4,128,2048]{2,1,0:T(8,128)(2,1)} %collective-permute-done.65.refs_3_, ...), custom_call_target="tpu_custom_call" | custom-call | flops 805306368 | bytes 1000000 | tf_op jit(solution)/shard_map/mlp_grads/pallas_call | solution.py:608
  470.5 9.4 %assemble.1 = (f32[512,512]{1,0:T(8,128)}, f32[512,128]{1,0:T(8,128)}, f32[512,128]{1,0:T(8,128)}, f32[512,512]{1,0:T(8,128)}, f32[512,2048]{1,0:T(8,128)}, /*index=5*/f32[512,2048]{1,0:T(8,128)}, f32[2048,512]{1,0:T(8,128)}) custom-call(bf16[512,1280]{1,0:T(8,128)(2,1)} %reduce-scatter.2.cloned.1.call-done.refs_0_, bf16[512,1280]{1,0:T(8,128)(2,1)} %copy-done.58, ...), custom_call_target="tpu_custom_call" | custom-call | bytes 1500000 | tf_op jit(solution)/shard_map/assemble/pallas_call | solution.py:697
  (438 shorter events, 184.7 us)
Async XLA Ops:
  7.2 132.4 %all-gather.9.cloned.1.call-start = ((), (), s32[]{:S(2)}) async-start(), calls=%async_computation.2 | async-start | bytes 5242880 | tf_op jit(solution)/shard_map/all_gather | solution.py:777
  12.5 19.5 %collective-permute-start.7 = (bf16[2048,768]{1,0:T(8,128)(2,1)}, bf16[2048,768]{1,0:T(8,128)(2,1)}, u32[]{:S(2)}, u32[]{:S(2)}) collective-permute-start(bf16[2048,768]{1,0:T(8,128)(2,1)} %pad_maximum_fusion.refs_0_), channel_id=1, source_target_pairs={{0,16},{16,0},{1,17},{17,1},{2,18},{18,2},{3,19},{19,3},{4,20},{20... | collective-permute-start | bytes 9437192 | tf_op jit(solution)/shard_map/ppermute | solution.py:69
  32.1 25.8 %collective-permute-start.15 = (bf16[2048,2048]{1,0:T(8,128)(2,1)}, bf16[2048,2048]{1,0:T(8,128)(2,1)}, u32[]{:S(2)}, u32[]{:S(2)}) collective-permute-start(bf16[2048,2048]{1,0:T(8,128)(2,1)} %bitcast.67), channel_id=1, source_target_pairs={{0,16},{16,0},{1,17},{17,1},{2,18},{18,2},{3,19},{19,3},{4,20},{20... | collective-permute-start | bytes 25165832 | tf_op jit(solution)/shard_map/ppermute | solution.py:69
  39.7 40.6 %collective-permute-start.16 = (bf16[2048,2048]{1,0:T(8,128)(2,1)}, bf16[2048,2048]{1,0:T(8,128)(2,1)}, u32[]{:S(2)}, u32[]{:S(2)}) collective-permute-start(bf16[2048,2048]{1,0:T(8,128)(2,1)} %bitcast.76), channel_id=1, source_target_pairs={{0,16},{16,0},{1,17},{17,1},{2,18},{18,2},{3,19},{19,3},{4,20},{20... | collective-permute-start | bytes 25165832 | tf_op jit(solution)/shard_map/ppermute | solution.py:69
  57.9 22.5 %collective-permute-start.17 = (bf16[2048,2048]{1,0:T(8,128)(2,1)}, bf16[2048,2048]{1,0:T(8,128)(2,1)}, u32[]{:S(2)}, u32[]{:S(2)}) collective-permute-start(bf16[2048,2048]{1,0:T(8,128)(2,1)} %bitcast.85), channel_id=1, source_target_pairs={{0,16},{16,0},{1,17},{17,1},{2,18},{18,2},{3,19},{19,3},{4,20},{20... | collective-permute-start | bytes 25165832 | tf_op jit(solution)/shard_map/ppermute | solution.py:69
  57.9 134.5 %all-gather.11.cloned.1.call-start = ((), (), s32[]{:S(2)}) async-start(), calls=%async_computation.3 | async-start | bytes 2621440 | tf_op jit(solution)/shard_map/all_gather | solution.py:777
  139.6 145.3 %all-gather.13.cloned.1.call-start = ((), (), s32[]{:S(2)}) async-start(), calls=%async_computation.4 | async-start | bytes 5242880 | tf_op jit(solution)/shard_map/all_gather | solution.py:777
  192.5 174.6 %all-gather.15.cloned.1.call-start = ((), (), s32[]{:S(2)}) async-start(), calls=%async_computation.5 | async-start | bytes 5242880 | tf_op jit(solution)/shard_map/all_gather | solution.py:777
  239.9 45.1 %collective-permute-start.47 = (bf16[128,2048]{1,0:T(8,128)(2,1)}, bf16[128,2048]{1,0:T(8,128)(2,1)}, u32[]{:S(2)}, u32[]{:S(2)}) collective-permute-start(bf16[128,2048]{1,0:T(8,128)(2,1)} %get-tuple-element.374), channel_id=1, source_target_pairs={{0,1},{1,0},{2,3},{3,2},{4,5},{5,4},{6,7},{7,6},{8,9},{9,8},{10,11... | collective-permute-start | bytes 1572872 | tf_op jit(solution)/shard_map/ppermute | solution.py:841
  285.0 179.1 %reduce-scatter.2.cloned.1.call-start = ((), (), s32[]{:S(2)}) async-start(), calls=%async_computation.1 | async-start | bytes 6553600 | tf_op jit(solution)/shard_map/reduce_scatter | solution.py:748
  285.1 25.8 %collective-permute-start.51 = (bf16[4,256,2048]{2,1,0:T(8,128)(2,1)}, bf16[4,256,2048]{2,1,0:T(8,128)(2,1)}, u32[]{:S(2)}, u32[]{:S(2)}) collective-permute-start(bf16[4,256,2048]{2,1,0:T(8,128)(2,1)} %bitcast.98), channel_id=1, source_target_pairs={{0,16},{16,0},{1,17},{17,1},{2,18},{18,2},{3,19},{19,3},{4,20},{20... | collective-permute-start | bytes 12582920 | tf_op jit(solution)/shard_map/ppermute | solution.py:69
  285.1 25.8 %collective-permute-start.52 = (bf16[4,256,2048]{2,1,0:T(8,128)(2,1)}, bf16[4,256,2048]{2,1,0:T(8,128)(2,1)}, u32[]{:S(2)}, u32[]{:S(2)}) collective-permute-start(bf16[4,256,2048]{2,1,0:T(8,128)(2,1)} %bitcast.94), channel_id=1, source_target_pairs={{0,16},{16,0},{1,17},{17,1},{2,18},{18,2},{3,19},{19,3},{4,20},{20... | collective-permute-start | bytes 12582920 | tf_op jit(solution)/shard_map/ppermute | solution.py:69
  303.2 21.8 %collective-permute-start.53 = (bf16[64,2048]{1,0:T(8,128)(2,1)}, bf16[64,2048]{1,0:T(8,128)(2,1)S(1)}, u32[]{:S(2)}, u32[]{:S(2)}) collective-permute-start(bf16[64,2048]{1,0:T(8,128)(2,1)} %get-tuple-element.280.after_ref.d0), channel_id=1, source_target_pairs={{0,1},{1,0},{2,3},{3,2},{4,5},{5,4},{6,7},{7,6},{8,9},{9,8},{10,11... | collective-permute-start | bytes 786440 | tf_op jit(solution)/shard_map/ppermute | solution.py:59
  304.4 20.6 %collective-permute-start.54 = (bf16[64,2048]{1,0:T(8,128)(2,1)}, bf16[64,2048]{1,0:T(8,128)(2,1)S(1)}, u32[]{:S(2)}, u32[]{:S(2)}) collective-permute-start(bf16[64,2048]{1,0:T(8,128)(2,1)} %get-tuple-element.280.after_ref.d0), channel_id=1, source_target_pairs={{0,2},{1,3},{2,0},{3,1},{4,6},{5,7},{6,4},{7,5},{8,10},{9,11},{10,... | collective-permute-start | bytes 786440 | tf_op jit(solution)/shard_map/ppermute | solution.py:59
  338.1 25.3 %collective-permute-start.61 = (bf16[64,2048]{1,0:T(8,128)(2,1)}, bf16[64,2048]{1,0:T(8,128)(2,1)S(1)}, u32[]{:S(2)}, u32[]{:S(2)}) collective-permute-start(bf16[64,2048]{1,0:T(8,128)(2,1)} %get-tuple-element.301), channel_id=1, source_target_pairs={{0,1},{1,0},{2,3},{3,2},{4,5},{5,4},{6,7},{7,6},{8,9},{9,8},{10,11... | collective-permute-start | bytes 786440 | tf_op jit(solution)/shard_map/ppermute | solution.py:64
  340.4 23.1 %collective-permute-start.62 = (bf16[64,2048]{1,0:T(8,128)(2,1)}, bf16[64,2048]{1,0:T(8,128)(2,1)}, u32[]{:S(2)}, u32[]{:S(2)}) collective-permute-start(bf16[64,2048]{1,0:T(8,128)(2,1)} %get-tuple-element.302), channel_id=1, source_target_pairs={{0,2},{1,3},{2,0},{3,1},{4,6},{5,7},{6,4},{7,5},{8,10},{9,11},{10,... | collective-permute-start | bytes 786440 | tf_op jit(solution)/shard_map/ppermute | solution.py:64
  341.5 22.0 %collective-permute-start.63 = (bf16[64,2048]{1,0:T(8,128)(2,1)S(1)}, bf16[64,2048]{1,0:T(8,128)(2,1)}, u32[]{:S(2)}, u32[]{:S(2)}) collective-permute-start(bf16[64,2048]{1,0:T(8,128)(2,1)S(1)} %get-tuple-element.303), channel_id=1, source_target_pairs={{0,3},{1,2},{2,1},{3,0},{4,7},{5,6},{6,5},{7,4},{8,11},{9,10},{10,... | collective-permute-start | bytes 786440 | tf_op jit(solution)/shard_map/ppermute | solution.py:64
  367.2 32.9 %collective-permute-start.66 = (bf16[4,256,2048]{2,1,0:T(8,128)(2,1)}, bf16[4,256,2048]{2,1,0:T(8,128)(2,1)}, u32[]{:S(2)}, u32[]{:S(2)}) collective-permute-start(bf16[4,256,2048]{2,1,0:T(8,128)(2,1)} %bitcast.107), channel_id=1, source_target_pairs={{0,16},{16,0},{1,17},{17,1},{2,18},{18,2},{3,19},{19,3},{4,20},{20... | collective-permute-start | bytes 12582920 | tf_op jit(solution)/shard_map/ppermute | solution.py:69
  370.3 29.0 %collective-permute-start.65 = (bf16[4,128,2048]{2,1,0:T(8,128)(2,1)}, bf16[4,128,2048]{2,1,0:T(8,128)(2,1)}, u32[]{:S(2)}, u32[]{:S(2)}) collective-permute-start(bf16[4,128,2048]{2,1,0:T(8,128)(2,1)} %pad_maximum_fusion.1.refs_2_), channel_id=1, source_target_pairs={{0,16},{16,0},{1,17},{17,1},{2,18},{18,2},{3,19},{19,3},{4,20},{20... | collective-permute-start | bytes 6291464 | tf_op jit(solution)/shard_map/ppermute | solution.py:69
  370.7 28.6 %collective-permute-start.67 = (bf16[512,1536]{1,0:T(8,128)(2,1)S(1)}, bf16[512,1536]{1,0:T(8,128)(2,1)}, u32[]{:S(2)}, u32[]{:S(2)}) collective-permute-start(bf16[512,1536]{1,0:T(8,128)(2,1)S(1)} %mlp_grads.6.refs_6_), channel_id=1, source_target_pairs={{0,16},{16,0},{1,17},{17,1},{2,18},{18,2},{3,19},{19,3},{4,20},{20... | collective-permute-start | bytes 4718600 | tf_op jit(solution)/shard_map/ppermute | solution.py:69
  370.8 33.3 %collective-permute-start.69 = (bf16[4,128,2048]{2,1,0:T(8,128)(2,1)}, bf16[4,128,2048]{2,1,0:T(8,128)(2,1)}, u32[]{:S(2)}, u32[]{:S(2)}) collective-permute-start(bf16[4,128,2048]{2,1,0:T(8,128)(2,1)} %bitcast.111), channel_id=1, source_target_pairs={{0,16},{16,0},{1,17},{17,1},{2,18},{18,2},{3,19},{19,3},{4,20},{20... | collective-permute-start | bytes 6291464 | tf_op jit(solution)/shard_map/ppermute | solution.py:69
  375.1 24.2 %collective-permute-start.68 = (f32[64,2048]{1,0:T(8,128)S(1)}, f32[64,2048]{1,0:T(8,128)S(1)}, u32[]{:S(2)}, u32[]{:S(2)}) collective-permute-start(f32[64,2048]{1,0:T(8,128)S(1)} %broadcast_select_fusion.3), channel_id=1, source_target_pairs={{0,16},{16,0},{1,17},{17,1},{2,18},{18,2},{3,19},{19,3},{4,20},{20... | collective-permute-start | bytes 1572872 | tf_op jit(solution)/shard_map/ppermute | solution.py:69
  400.1 29.4 %collective-permute-start.71 = (bf16[512,1536]{1,0:T(8,128)(2,1)}, bf16[512,1536]{1,0:T(8,128)(2,1)}, u32[]{:S(2)}, u32[]{:S(2)}) collective-permute-start(bf16[512,1536]{1,0:T(8,128)(2,1)} %mlp_grads.7.refs_7_), channel_id=1, source_target_pairs={{0,16},{16,0},{1,17},{17,1},{2,18},{18,2},{3,19},{19,3},{4,20},{20... | collective-permute-start | bytes 4718600 | tf_op jit(solution)/shard_map/ppermute | solution.py:69
  400.5 28.2 %collective-permute-start.74 = (bf16[64,2048]{1,0:T(8,128)(2,1)S(1)}, bf16[64,2048]{1,0:T(8,128)(2,1)S(1)}, u32[]{:S(2)}, u32[]{:S(2)}) collective-permute-start(bf16[64,2048]{1,0:T(8,128)(2,1)S(1)} %copy-done.46), channel_id=1, source_target_pairs={{0,3},{1,2},{2,1},{3,0},{4,7},{5,6},{6,5},{7,4},{8,11},{9,10},{10,... | collective-permute-start | bytes 786440 | tf_op jit(solution)/shard_map/ppermute | solution.py:64
  402.4 26.3 %collective-permute-start.73 = (bf16[64,2048]{1,0:T(8,128)(2,1)S(1)}, bf16[64,2048]{1,0:T(8,128)(2,1)S(1)}, u32[]{:S(2)}, u32[]{:S(2)}) collective-permute-start(bf16[64,2048]{1,0:T(8,128)(2,1)S(1)} %copy-done.44), channel_id=1, source_target_pairs={{0,2},{1,3},{2,0},{3,1},{4,6},{5,7},{6,4},{7,5},{8,10},{9,11},{10,... | collective-permute-start | bytes 786440 | tf_op jit(solution)/shard_map/ppermute | solution.py:64
  403.4 25.3 %collective-permute-start.72 = (bf16[64,2048]{1,0:T(8,128)(2,1)S(1)}, bf16[64,2048]{1,0:T(8,128)(2,1)S(1)}, u32[]{:S(2)}, u32[]{:S(2)}) collective-permute-start(bf16[64,2048]{1,0:T(8,128)(2,1)S(1)} %copy-done.42), channel_id=1, source_target_pairs={{0,1},{1,0},{2,3},{3,2},{4,5},{5,4},{6,7},{7,6},{8,9},{9,8},{10,11... | collective-permute-start | bytes 786440 | tf_op jit(solution)/shard_map/ppermute | solution.py:64
  404.1 24.6 %collective-permute-start.70 = (f32[2,8,1,128]{3,2,1,0:T(1,128)S(1)}, f32[2,8,1,128]{3,2,1,0:T(1,128)S(1)}, u32[]{:S(2)}, u32[]{:S(2)}) collective-permute-start(f32[2,8,1,128]{3,2,1,0:T(1,128)S(1)} %broadcast_select_fusion.5), channel_id=1, source_target_pairs={{0,1},{1,0},{2,3},{3,2},{4,5},{5,4},{6,7},{7,6},{8,9},{9,8},{10,11... | collective-permute-start | bytes 24584 | tf_op jit(solution)/shard_map/ppermute | solution.py:881
  430.2 33.6 %collective-permute-start.75 = (bf16[512,1536]{1,0:T(8,128)(2,1)S(1)}, bf16[512,1536]{1,0:T(8,128)(2,1)}, u32[]{:S(2)}, u32[]{:S(2)}) collective-permute-start(bf16[512,1536]{1,0:T(8,128)(2,1)S(1)} %mlp_grads.8.refs_2_), channel_id=1, source_target_pairs={{0,16},{16,0},{1,17},{17,1},{2,18},{18,2},{3,19},{19,3},{4,20},{20... | collective-permute-start | bytes 4718600 | tf_op jit(solution)/shard_map/ppermute | solution.py:69
  433.6 30.3 %collective-permute-start.76 = (bf16[64,2048]{1,0:T(8,128)(2,1)S(1)}, bf16[64,2048]{1,0:T(8,128)(2,1)S(1)}, u32[]{:S(2)}, u32[]{:S(2)}) collective-permute-start(bf16[64,2048]{1,0:T(8,128)(2,1)S(1)} %get-tuple-element.380), channel_id=1, source_target_pairs={{0,16},{16,0},{1,17},{17,1},{2,18},{18,2},{3,19},{19,3},{4,20},{20... | collective-permute-start | bytes 786440 | tf_op jit(solution)/shard_map/ppermute | solution.py:69
  434.2 29.6 %collective-permute-start.77 = (f32[4,128]{1,0:T(4,128)S(1)}, f32[4,128]{1,0:T(4,128)S(1)}, u32[]{:S(2)}, u32[]{:S(2)}) collective-permute-start(f32[4,128]{1,0:T(4,128)S(1)} %bitcast.125), channel_id=1, source_target_pairs={{0,4},{4,8},{8,12},{12,0},{1,5},{5,9},{9,13},{13,1},{2,6},{6,10},{... | collective-permute-start | bytes 6152 | tf_op jit(solution)/shard_map/ppermute | solution.py:929
  437.3 26.5 %collective-permute-start.78 = (f32[4,128]{1,0:T(4,128)S(1)}, f32[4,128]{1,0:T(4,128)S(1)}, u32[]{:S(2)}, u32[]{:S(2)}) collective-permute-start(f32[4,128]{1,0:T(4,128)S(1)} %bitcast.124), channel_id=1, source_target_pairs={{0,8},{4,12},{8,0},{12,4},{1,9},{5,13},{9,1},{13,5},{2,10},{6,14},... | collective-permute-start | bytes 6152 | tf_op jit(solution)/shard_map/ppermute | solution.py:929
  438.1 25.8 %collective-permute-start.79 = (f32[4,128]{1,0:T(4,128)S(1)}, f32[4,128]{1,0:T(4,128)S(1)}, u32[]{:S(2)}, u32[]{:S(2)}) collective-permute-start(f32[4,128]{1,0:T(4,128)S(1)} %bitcast.123), channel_id=1, source_target_pairs={{0,12},{4,0},{8,4},{12,8},{1,13},{5,1},{9,5},{13,9},{2,14},{6,2},{... | collective-permute-start | bytes 6152 | tf_op jit(solution)/shard_map/ppermute | solution.py:929
  (165 other events, 1540.7 us)
Sparse Core Ops, SparseCore 0:
  58.0 81.5 all-gather.8
  141.8 44.4 all-gather.10
  192.6 78.2 all-gather.12
  285.1 80.0 all-gather.14
  367.4 93.3 reduce-scatter.1
